TPU v7x, 32 devices: a whole 2x2x4 slice. The times are simulated.
32 devices in a mesh: seq: 8 (over z, x), head: 4 (over y, core).
Axes of the slice: x: 2, y: 2, z: 4, core: 2. Of those that a mesh axis runs over, the one named last changes fastest.
Arguments:
- prompt_q: bfloat16 [8192, 2048], P('seq', 'head'), may hold values from -6 to 6
- prompt_k: bfloat16 [8192, 2048], P('seq', 'head'), may hold values from -6 to 6
- prompt_v: bfloat16 [8192, 2048], P('seq', 'head'), may hold values from -6 to 6
- prompt_grad: bfloat16 [8192, 2048], P('seq', 'head'), may hold values from -6 to 6
- cand_q: bfloat16 [4096, 2048], P('seq', 'head'), may hold values from -6 to 6
- cand_k: bfloat16 [4096, 2048], P('seq', 'head'), may hold values from -6 to 6
- cand_v: bfloat16 [4096, 2048], P('seq', 'head'), may hold values from -6 to 6
- readout: float32 [2048], P('head'), may hold values from -0.24 to 0.24
- prompt_ends: int32 [8], replicated, may hold values from 1 to 8192, as said below
- cand_lengths: int32 [8, 2], P('seq'), may hold values from 1 to 384, 512 in all within a row
- cand_prompt: int32 [16], replicated, may hold values from 0 to 7
- cand_ranks: int32 [16], replicated, may hold values from 0 to 3
Outputs:
- prompt_dq: bfloat16 [8192, 2048], P('seq', 'head')
- prompt_dk: bfloat16 [8192, 2048], P('seq', 'head')
- prompt_dv: bfloat16 [8192, 2048], P('seq', 'head')
- cand_dq: bfloat16 [4096, 2048], P('seq', 'head')
- cand_dk: bfloat16 [4096, 2048], P('seq', 'head')
- cand_dv: bfloat16 [4096, 2048], P('seq', 'head')
- list_loss: float32 [], replicated
Inputs may be any that keep to these rules, and one draw needn't show every extreme that they name: `prompt_ends`: strictly increasing; the last equals 8192; at most 2 ends lie in each range (d * 1024, (d + 1) * 1024], and in some range exactly 2. `cand_lengths`: each row sums to 512, and no entry exceeds 384.
All inputs are finite; a program needn't handle non-finite values.
Results may differ from a plain program's by a relative error of at most 0.0062.
Values may be sent and summed in bfloat16 or wider, within the bound.
No kernel may reach another device: no remote copies, remote signals or barrier semaphores. Data moves between devices by JAX's collectives and lax.ppermute only.
A program may use at most 128 MiB of HBM per device.

v0:
```python
import math

import jax
import jax.numpy as jnp
from jax import lax
from jax.sharding import PartitionSpec as P

E = 128
ENDS = 2


grad_scale = 1048576.0


def prefix(part, axis, combine, identity, reverse):
    count = lax.axis_size(axis)
    place = lax.axis_index(axis)
    ahead = count - 1 - place if reverse else place
    gathered = jax.tree.map(lambda a: lax.all_gather(a, axis), part)
    state = jax.tree.map(lambda a, e: jnp.zeros_like(a) + jnp.asarray(e, a.dtype), part, identity)

    def one(lap, state):
        source = count - 1 - lap if reverse else lap
        return combine(
            state, jax.tree.map(lambda a: lax.dynamic_index_in_dim(a, source, 0, False), gathered)
        )

    return lax.fori_loop(0, ahead, one, state)


def pick_value(table, wanted):
    spots = jnp.arange(table.shape[0], dtype=jnp.int32)
    return jnp.sum(jnp.where(spots == wanted, table, 0))


def slab_layout(prompt_ends, slab_index, slab_width, slot_count):
    prompt_count = prompt_ends.shape[0]
    slab_start = slab_index * slab_width
    position = slab_start + jnp.arange(slab_width, dtype=jnp.int32)
    segment = jnp.sum((prompt_ends[None, :] <= position[:, None]).astype(jnp.int32), axis=1)
    begins = jnp.logical_or(slab_index == 0, jnp.any(prompt_ends == slab_start))
    first_seg = segment[0]
    last_seg = segment[slab_width - 1]
    first_end = jnp.sum((prompt_ends <= slab_start).astype(jnp.int32))
    slot_pid = first_end + jnp.arange(slot_count, dtype=jnp.int32)
    prompt_ids = jnp.arange(prompt_count, dtype=jnp.int32)
    slot_end = jnp.sum(
        jnp.where(prompt_ids[None, :] == slot_pid[:, None], prompt_ends[None, :], 0), axis=1
    )
    slot_valid = jnp.logical_and(slot_pid < prompt_count, slot_end <= slab_start + slab_width)
    slot_masks = jnp.logical_and(segment[None, :] == slot_pid[:, None], slot_valid[:, None])
    row_masks = jnp.concatenate([slot_masks, (segment == last_seg)[None, :]], axis=0)
    start_flag = jnp.logical_or(begins, first_seg != last_seg).astype(jnp.float32)
    end_flag = slot_valid[0].astype(jnp.float32)
    cont_right = (pick_value(prompt_ends, last_seg) != slab_start + slab_width).astype(jnp.float32)
    contin = 1.0 - begins.astype(jnp.float32)
    first_mask = segment == first_seg
    from_first = jnp.logical_and(slot_pid == first_seg, slot_valid).astype(jnp.float32)
    return (
        segment,
        row_masks,
        first_mask,
        contin,
        from_first,
        slot_pid,
        slot_valid,
        start_flag,
        end_flag,
        cont_right,
    )


def slot_rows(row_ids, prompt_ends, slab_width, slot_count):
    prompt_count = prompt_ends.shape[0]
    device_of = row_ids // slot_count
    slot_of = row_ids % slot_count
    first_end = jnp.sum(
        (prompt_ends[None, :] <= (device_of * slab_width)[:, None]).astype(jnp.int32), axis=1
    )
    row_pid = first_end + slot_of
    prompt_ids = jnp.arange(prompt_count, dtype=jnp.int32)
    row_end = jnp.sum(
        jnp.where(prompt_ids[None, :] == row_pid[:, None], prompt_ends[None, :], 0), axis=1
    )
    row_valid = jnp.logical_and(row_pid < prompt_count, row_end <= (device_of + 1) * slab_width)
    return (row_pid, row_valid)


def chain_combine(earlier, later):
    return (later[0] + (1.0 - later[1]) * earlier[0], jnp.maximum(earlier[1], later[1]))


def listwise(raw_scores, cand_prompt, cand_ranks, prompt_count):
    squashed = 3.0 * jnp.tanh(raw_scores)
    same_group = (cand_prompt[:, None] == cand_prompt[None, :]).astype(jnp.float32)
    exp_scores = jnp.exp(squashed)
    denoms = jnp.sum(same_group * exp_scores[None, :], axis=1)
    rank_weight = jnp.exp(-cand_ranks.astype(jnp.float32))
    targets = rank_weight / jnp.sum(same_group * rank_weight[None, :], axis=1)
    list_loss = -jnp.sum(targets * (squashed - jnp.log(denoms))) / prompt_count
    tanh_raw = jnp.tanh(raw_scores)
    raw_grad = (
        grad_scale
        / prompt_count
        * (exp_scores / denoms - targets)
        * 3.0
        * (1.0 - tanh_raw * tanh_raw)
    )
    return (list_loss, raw_grad)


def per_device(
    prompt_q,
    prompt_k,
    prompt_v,
    prompt_grad,
    cand_q,
    cand_k,
    cand_v,
    readout,
    prompt_ends,
    cand_lengths,
    cand_prompt,
    cand_ranks,
):
    slab_width = prompt_q.shape[0]
    cand_width = cand_q.shape[0]
    local_heads = prompt_q.shape[1] // E
    slab_count = lax.axis_size("seq")
    slab_index = lax.axis_index("seq")
    cand_count = cand_prompt.shape[0]
    per_slab = cand_lengths.shape[1]
    prompt_count = prompt_ends.shape[0]
    slot_count = ENDS
    scaling = 1.0 / math.sqrt(E * slab_width)
    queries = prompt_q.reshape(slab_width, local_heads, E)
    keys_in = prompt_k.reshape(slab_width, local_heads, E)
    values_in = prompt_v.reshape(slab_width, local_heads, E)
    grads_in = prompt_grad.reshape(slab_width, local_heads, E)
    cand_queries = cand_q.reshape(cand_width, local_heads, E)
    cand_keys = cand_k.reshape(cand_width, local_heads, E)
    cand_values = cand_v.reshape(cand_width, local_heads, E)
    readout_heads = readout.reshape(local_heads, E)
    (
        segment,
        row_masks,
        first_mask,
        contin,
        from_first,
        slot_pid,
        slot_valid,
        start_flag,
        end_flag,
        cont_right,
    ) = slab_layout(prompt_ends, slab_index, slab_width, slot_count)
    mask_rows = row_masks.astype(jnp.bfloat16)
    masked_keys = mask_rows[:, :, None, None] * keys_in[None]
    masked_values = mask_rows[:, :, None, None] * values_in[None]
    slab_sums = jnp.einsum(
        "mthd,the->mhde", masked_keys, values_in, preferred_element_type=jnp.float32
    )
    tail_state = slab_sums[slot_count]
    zero_state = jnp.zeros_like(tail_state)
    valid_float = slot_valid.astype(jnp.float32)
    lengths = cand_lengths[0]
    bounds = jnp.cumsum(lengths)
    tok_pos = jnp.arange(cand_width, dtype=jnp.int32)
    cand_id = jnp.sum((bounds[None, :] <= tok_pos[:, None]).astype(jnp.int32), axis=1)
    cand_masks = cand_id[None, :] == jnp.arange(per_slab, dtype=jnp.int32)[:, None]
    cand_float = cand_masks.astype(jnp.float32)
    cand_bf = cand_masks.astype(jnp.bfloat16)
    same_cand = jnp.logical_and(
        cand_id[:, None] == cand_id[None, :], tok_pos[None, :] <= tok_pos[:, None]
    )
    own_prompts = lax.dynamic_slice_in_dim(cand_prompt, slab_index * per_slab, per_slab)
    incoming, unused_flag = prefix(
        (tail_state, start_flag),
        "seq",
        chain_combine,
        (zero_state, jnp.zeros((), jnp.float32)),
        False,
    )
    incoming_first = contin * incoming
    end_slots = (
        slab_sums[:slot_count] + from_first[:, None, None, None] * incoming_first[None]
    ) * valid_float[:, None, None, None]
    shard_rows = lax.all_gather(end_slots.astype(jnp.bfloat16), "seq", axis=0, tiled=True)
    row_ids = jnp.arange(shard_rows.shape[0], dtype=jnp.int32)
    row_pid, row_valid = slot_rows(row_ids, prompt_ends, slab_width, slot_count)
    matches = jnp.logical_and(own_prompts[:, None] == row_pid[None, :], row_valid[None, :]).astype(
        jnp.bfloat16
    )
    cand_states = jnp.einsum(
        "jr,rhde->jhde", matches, shard_rows, preferred_element_type=jnp.float32
    ).astype(jnp.bfloat16)
    qk_scores = jnp.einsum(
        "thd,shd->hts", cand_queries, cand_keys, preferred_element_type=jnp.float32
    )
    attn_weights = jnp.where(same_cand[None], qk_scores, 0.0).astype(jnp.bfloat16)
    masked_queries = cand_bf[:, :, None, None] * cand_queries[None]
    outputs = scaling * (
        jnp.einsum("hts,she->the", attn_weights, cand_values, preferred_element_type=jnp.float32)
        + jnp.einsum(
            "jthd,jhde->the", masked_queries, cand_states, preferred_element_type=jnp.float32
        )
    )
    token_score = jnp.sum(jax.nn.silu(outputs) * readout_heads[None], axis=(1, 2))
    partial_raw = jnp.sum(cand_float * token_score[None, :], axis=1) / lengths.astype(jnp.float32)
    all_slots = jnp.arange(cand_count, dtype=jnp.int32)
    placed = jnp.where(all_slots // per_slab == slab_index, jnp.tile(partial_raw, slab_count), 0.0)
    raw_scores = lax.psum(placed, ("seq", "head"))
    list_loss, raw_grad = listwise(raw_scores, cand_prompt, cand_ranks, prompt_count)
    own_grad = lax.dynamic_slice_in_dim(raw_grad, slab_index * per_slab, per_slab) / lengths.astype(
        jnp.float32
    )
    token_coef = jnp.sum(cand_float * own_grad[:, None], axis=0)
    sigma = jax.nn.sigmoid(outputs)
    out_grad = (
        token_coef[:, None, None] * readout_heads[None] * sigma * (1.0 + outputs * (1.0 - sigma))
    ).astype(jnp.bfloat16)
    gv_scores = jnp.einsum(
        "the,she->hts", out_grad, cand_values, preferred_element_type=jnp.float32
    )
    grad_weights = jnp.where(same_cand[None], gv_scores, 0.0).astype(jnp.bfloat16)
    masked_grads = cand_bf[:, :, None, None] * out_grad[None]
    cand_dq = scaling * (
        jnp.einsum("hts,shd->thd", grad_weights, cand_keys, preferred_element_type=jnp.float32)
        + jnp.einsum(
            "jthe,jhde->thd", masked_grads, cand_states, preferred_element_type=jnp.float32
        )
    )
    cand_dk = scaling * jnp.einsum(
        "hts,thd->shd", grad_weights, cand_queries, preferred_element_type=jnp.float32
    )
    cand_dv = scaling * jnp.einsum(
        "hts,the->she", attn_weights, out_grad, preferred_element_type=jnp.float32
    )
    state_grads = (
        scaling
        * jnp.einsum("jthd,the->jhde", masked_queries, out_grad, preferred_element_type=jnp.float32)
    ).astype(jnp.bfloat16)
    matches = jnp.logical_and(
        slot_pid[:, None] == cand_prompt[None, :], slot_valid[:, None]
    ).astype(jnp.bfloat16)
    slot_grads = jnp.einsum(
        "kr,rhde->khde",
        matches,
        lax.all_gather(state_grads, "seq", axis=0, tiled=True),
        preferred_element_type=jnp.float32,
    )
    slot_grads = slot_grads * valid_float[:, None, None, None]
    first_bf = first_mask.astype(jnp.bfloat16)
    head_state = (
        scaling
        * jnp.einsum(
            "thd,the->hde",
            first_bf[:, None, None] * queries,
            grads_in,
            preferred_element_type=jnp.float32,
        )
        + end_flag * slot_grads[0]
    )
    from_right, unused_back = prefix(
        (head_state, end_flag), "seq", chain_combine, (zero_state, jnp.zeros((), jnp.float32)), True
    )
    right_states = jnp.concatenate([slot_grads, (cont_right * from_right)[None]], axis=0).astype(
        jnp.bfloat16
    )
    incoming_bf = incoming_first.astype(jnp.bfloat16)
    slab_pos = jnp.arange(slab_width, dtype=jnp.int32)
    same_prompt = jnp.logical_and(
        segment[:, None] == segment[None, :], slab_pos[None, :] <= slab_pos[:, None]
    )
    attn_prompt = jnp.where(
        same_prompt[None],
        jnp.einsum("thd,shd->hts", queries, keys_in, preferred_element_type=jnp.float32),
        0.0,
    ).astype(jnp.bfloat16)
    grad_prompt = jnp.where(
        same_prompt[None],
        jnp.einsum("the,she->hts", grads_in, values_in, preferred_element_type=jnp.float32),
        0.0,
    ).astype(jnp.bfloat16)
    first_float = first_mask.astype(jnp.float32)
    prompt_dq = scaling * (
        jnp.einsum("hts,shd->thd", grad_prompt, keys_in, preferred_element_type=jnp.float32)
        + first_float[:, None, None]
        * jnp.einsum("the,hde->thd", grads_in, incoming_bf, preferred_element_type=jnp.float32)
    )
    prompt_dk = scaling * jnp.einsum(
        "hts,thd->shd", grad_prompt, queries, preferred_element_type=jnp.float32
    ) + jnp.einsum(
        "mshe,mhde->shd", masked_values, right_states, preferred_element_type=jnp.float32
    )
    prompt_dv = scaling * jnp.einsum(
        "hts,the->she", attn_prompt, grads_in, preferred_element_type=jnp.float32
    ) + jnp.einsum("mshd,mhde->she", masked_keys, right_states, preferred_element_type=jnp.float32)
    flat_width = local_heads * E
    return (
        prompt_dq.astype(jnp.bfloat16).reshape(slab_width, flat_width),
        prompt_dk.astype(jnp.bfloat16).reshape(slab_width, flat_width),
        prompt_dv.astype(jnp.bfloat16).reshape(slab_width, flat_width),
        cand_dq.astype(jnp.bfloat16).reshape(cand_width, flat_width),
        cand_dk.astype(jnp.bfloat16).reshape(cand_width, flat_width),
        cand_dv.astype(jnp.bfloat16).reshape(cand_width, flat_width),
        list_loss,
    )


def solution(mesh):
    return jax.shard_map(
        per_device,
        mesh=mesh,
        in_specs=(
            P("seq", "head"),
            P("seq", "head"),
            P("seq", "head"),
            P("seq", "head"),
            P("seq", "head"),
            P("seq", "head"),
            P("seq", "head"),
            P("head"),
            P(),
            P("seq", None),
            P(),
            P(),
        ),
        out_specs=(
            P("seq", "head"),
            P("seq", "head"),
            P("seq", "head"),
            P("seq", "head"),
            P("seq", "head"),
            P("seq", "head"),
            P(),
        ),
        check_vma=False,
    )
```

profile of v0, /device:TPU:0, one launch (start us, length us, event | category | flops | bytes accessed | tf_op | source)
XLA Modules:
  0.0 322.7 jit_solution(10575364997644604391)
XLA Ops:
  7.3 0.9 convert_reduce_fusion
  8.7 2.0 fusion.94
  10.7 1.3 fusion.108
  12.2 0.7 iota_add_fusion.1
  13.1 1.3 and_convert_fusion
  14.5 1.1 reshape.343
  15.6 2.8 fusion.40
  18.5 0.9 copy-done.12
  19.4 0.7 slice.24
  21.5 0.6 compare_reduce_fusion
  23.4 0.7 fusion.103
  24.1 0.8 dynamic-update-slice
  24.9 23.2 %all-reduce.2 = (f32[8]{0:T(128)S(1)}, f32[8]{0:T(128)S(1)}) all-reduce(f32[8]{0:T(128)S(1)} %dynamic-update-slice, f32[8]{0:T(128)S(1)} %fusion.103), channel_id=1, replica_groups=mesh['seq'=8,'head'=4] {'seq'}, use_global_device_ids=true, to_apply=%add | all-reduce | flops 16 | bytes 128
  48.1 24.4 %all-gather.6.cloned.1.call-done = f32[8,4,128,128]{3,2,0,1:T(8,128)} async-done(((f32[1,4,128,128]{3,2,0,1:T(8,128)}), f32[8,4,128,128]{3,2,0,1:T(8,128)}) %all-gather.6.cloned.1.call-update) | async-done | bytes 2097168 | tf_op jit(solution)/shard_map/all_gather | solution.py:19
  72.6 1.0 copy-done.13
  73.6 0.8 fusion.63
  74.7 1.3 copy.175
  76.7 2.1 select_convert_fusion.3
  78.8 58.8 %all-gather.8.cloned.1.call-done = bf16[16,4,128,128]{3,2,0,1:T(8,128)(2,1)} async-done(((bf16[2,4,128,128]{3,2,0,1:T(8,128)(2,1)}), bf16[16,4,128,128]{3,2,0,1:T(8,128)(2,1)}) %all-gather.8.cloned.1.call-update) | async-done | bytes 2097168 | tf_op jit(solution)/shard_map/all_gather | solution.py:187
  137.6 3.1 fusion.49
  140.6 0.6 fusion.30
  141.3 1.9 multiply_reduce_fusion
  143.5 39.3 %psum.7 = f32[16]{0:T(128)S(1)} all-reduce(f32[16]{0:T(128)S(1)} %compare_select_fusion.3), channel_id=1, replica_groups=mesh['seq'=8,'head'=4] {'seq','head'}, use_global_device_ids=true, to_apply=%region_12.13 | all-reduce | flops 16 | bytes 128 | tf_op jit(solution)/shard_map/psum | solution.py:211
  183.0 0.6 multiply_reduce_fusion.1
  183.8 1.7 multiply_convert_fusion
  185.9 0.9 copy.137
  187.4 1.5 copy.173
  188.9 2.3 copy.174
  191.1 0.6 fusion.4
  191.7 1.0 copy-done.11
  192.7 7.2 %select_convert_fusion.1 = bf16[4,1024,1024]{2,1,0:T(8,128)(2,1)} fusion(bf16[1024,4,128]{0,2,1:T(8,128)(2,1)S(1)} %bitcast.189, pred[1024,1024]{1,0:T(8,128)(4,1)S(1)} %fusion.4, bf16[1024,512]{1,0:T(8,128)(2,1)} %param.18), kind=kOutput, calls=%fused_computation.3 | convolution fusion | flops 1082130432 | bytes 11534336 | tf_op jit(solution)/shard_map/the,she->hts/dot_general | solution.py:281
  199.8 36.6 %all-gather.10.cloned.1.call-done = bf16[16,4,128,128]{3,2,1,0:T(8,128)(2,1)} async-done(((bf16[2,4,128,128]{3,2,1,0:T(8,128)(2,1)}), bf16[16,4,128,128]{3,2,1,0:T(8,128)(2,1)}) %all-gather.10.cloned.1.call-update) | async-done | bytes 2097168 | tf_op jit(solution)/shard_map/all_gather | solution.py:248
  236.4 3.0 fusion.12
  239.4 0.9 fusion.107
  240.3 1.8 fusion.55
  242.1 2.4 copy_bitcast_fusion.1
  245.1 6.5 %fusion.110 = f32[4,1024,128]{1,2,0:T(8,128)} fusion(bf16[1024,4,128]{0,2,1:T(8,128)(2,1)} %bitcast.194, bf16[4,1024,1024]{2,1,0:T(8,128)(2,1)} %select_convert_fusion.1), kind=kOutput, calls=%fused_computation.159 | convolution fusion | flops 1073741824 | bytes 11534336 | tf_op jit(solution)/shard_map/hts,thd->shd/dot_general | solution.py:290
  251.6 7.0 %fusion.7 = f32[4,1024,128]{1,2,0:T(8,128)} fusion(bf16[1024,4,128]{0,2,1:T(8,128)(2,1)S(1)} %bitcast.191, bf16[1024,4,128]{0,2,1:T(8,128)(2,1)} %bitcast.195, pred[1024,1024]{1,0:T(8,128)(4,1)} %copy-done.11, bf16[1024,512]{1,0:T(8,128)(2,1)S(1)} %copy-done), kind=kOutput, calls=%fused_computation.14 | convolution fusion | flops 2155872256 | bytes 6291456 | tf_op jit(solution)/shard_map/hts,the->she/dot_general | solution.py:295
  258.6 6.5 %fusion.105 = f32[4,1024,128]{1,2,0:T(8,128)S(1)} fusion(bf16[4,1024,1024]{2,1,0:T(8,128)(2,1)} %select_convert_fusion.1, bf16[1024,512]{1,0:T(8,128)(2,1)S(1)} %copy-done), kind=kOutput, calls=%fused_computation.155 | convolution fusion | flops 1073741824 | bytes 11534336 | tf_op jit(solution)/shard_map/hts,shd->thd/dot_general | solution.py:286
  265.1 1.4 fusion.11
  266.6 2.5 copy.153
  269.3 0.6 convolution_bitcast_fusion.2
  269.9 2.1 select_convert_fusion.2
  272.1 1.6 fusion.37
  273.7 2.1 copy.156
  275.7 2.3 fusion.39
  278.0 2.0 copy.157
  280.1 2.2 fusion.38
  282.3 1.0 copy.158
  283.9 6.1 %all-gather.12.cloned.1.call-done = f32[32,128,128]{2,1,0:T(8,128)} async-done(((f32[4,128,128]{2,1,0:T(8,128)}), f32[32,128,128]{2,1,0:T(8,128)}) %all-gather.12.cloned.1.call-update) | async-done | bytes 2097168 | tf_op jit(solution)/shard_map/all_gather | solution.py:19
  290.1 16.2 %while.27 = (s32[]{:T(128)}, f32[4,128,128]{2,1,0:T(8,128)S(1)}, s32[]{:T(128)}, f32[8,4,128,128]{3,2,1,0:T(8,128)}, f32[8]{0:T(128)S(1)}, /*index=5*/s32[]{:T(128)}, s32[]{:T(128)}, s32[]{:T(128)}, s32[]{:T(128)}, f32[1]{0:T(128)}) while((s32[]{:T(128)}, f32[4,128,128]{2,1,0:T(8,128)S(1)}, s32[]{:T(128)}, f32[8,4,128,128]{3,2,1,0:T(8,128)}, ...), condition=%wide.region_18.19_spmd, body=%wide.region_17.18_spmd.sunk | while | flops 131079 | bytes 786619 | solution.py:28
  290.1 0.6 dynamic_slice.44
  291.3 1.0 bitcast_add_fusion.8
  293.7 1.0 bitcast_add_fusion.8
  296.0 1.0 bitcast_add_fusion.8
  298.3 1.0 bitcast_add_fusion.8
  300.6 1.0 bitcast_add_fusion.8
  301.7 0.6 dynamic_slice.44
  302.9 1.0 bitcast_add_fusion.8
  305.2 1.0 bitcast_add_fusion.8
  306.3 3.0 fusion.9
  309.3 1.3 copy.154
  310.7 3.1 fusion.8
  313.7 1.3 copy.155
  (98 shorter events, 7.7 us)
Async XLA Ops:
  7.2 4.8 %copy-start = (bf16[1024,512]{1,0:T(8,128)(2,1)S(1)}, bf16[1024,512]{1,0:T(8,128)(2,1)}, u32[]{:S(2)}) copy-start(bf16[1024,512]{1,0:T(8,128)(2,1)} %param.17) | copy-start | bytes 3145732
  7.2 5.7 %copy-start.18 = (s32[8]{0:T(128)S(1)}, s32[8]{0:T(128)}, u32[]{:S(2)}) copy-start(s32[8]{0:T(128)} %param.24) | copy-start | bytes 100
  7.2 7.3 %copy-start.2 = (bf16[1024,512]{1,0:T(8,128)(2,1)S(1)}, bf16[1024,512]{1,0:T(8,128)(2,1)}, u32[]{:S(2)}) copy-start(bf16[1024,512]{1,0:T(8,128)(2,1)} %param.18) | copy-start | bytes 3145732
  7.2 65.3 %all-gather.6.cloned.1.call-start = ((), (), s32[]{:S(2)}) async-start(), calls=%async_computation | async-start | bytes 2359296 | tf_op jit(solution)/shard_map/all_gather | solution.py:19
  12.2 6.3 %copy-start.8 = (bf16[1024,4,128]{2,0,1:T(8,128)(2,1)}, bf16[1024,4,128]{2,0,1:T(8,128)(2,1)S(1)}, u32[]{:S(2)}) copy-start(bf16[1024,4,128]{2,0,1:T(8,128)(2,1)S(1)} %copy_bitcast_fusion) | copy-start | bytes 3145732
  15.6 7.2 %copy-start.22 = (u32[32]{0:T(128)S(1)}, u32[32]{0:T(128)}, u32[]{:S(2)}) copy-start(u32[32]{0:T(128)} %constant.148) | copy-start | bytes 388
  18.5 0.9 copy-start.12
  20.1 117.4 %all-gather.8.cloned.1.call-start = ((), (), s32[]{:S(2)}) async-start(), calls=%async_computation.1 | async-start | bytes 2359296 | tf_op jit(solution)/shard_map/all_gather | solution.py:187
  72.5 1.1 copy-start.13
  72.5 2.0 copy-start.20
  72.5 3.5 %copy-start.16 = (s32[16]{0:T(128)S(1)}, s32[16]{0:T(128)}, u32[]{:S(2)}) copy-start(s32[16]{0:T(128)} %param.26) | copy-start | bytes 196
  72.5 4.0 %copy-start.5 = (bf16[512,512]{1,0:T(8,128)(2,1)S(1)}, bf16[512,512]{1,0:T(8,128)(2,1)}, u32[]{:S(2)}) copy-start(bf16[512,512]{1,0:T(8,128)(2,1)} %param.20) | copy-start | bytes 1572868
  74.5 162.0 %all-gather.10.cloned.1.call-start = ((), (), s32[]{:S(2)}) async-start(), calls=%async_computation.2 | async-start | bytes 2359296 | tf_op jit(solution)/shard_map/all_gather | solution.py:248
  76.0 2.8 copy-start.6
  76.6 2.2 copy-start.14
  78.8 62.5 %copy-start.17 = (f32[512]{0:T(512)S(1)}, f32[512]{0:T(512)}, u32[]{:S(2)}) copy-start(f32[512]{0:T(512)} %param.23) | copy-start | bytes 6148
  78.8 62.5 %copy-start.21 = (bf16[512,512]{1,0:T(8,128)(2,1)S(1)}, bf16[512,512]{1,0:T(8,128)(2,1)}, u32[]{:S(2)}) copy-start(bf16[512,512]{1,0:T(8,128)(2,1)} %param.22) | copy-start | bytes 1572868
  137.6 3.7 %copy-start.4 = (bf16[4,512,512]{2,1,0:T(8,128)(2,1)S(1)}, bf16[4,512,512]{2,1,0:T(8,128)(2,1)}, u32[]{:S(2)}) copy-start(bf16[4,512,512]{2,1,0:T(8,128)(2,1)} %select_convert_fusion.3) | copy-start | bytes 6291460
  141.3 2.2 copy-start.19
  185.4 83.6 %copy-start.1 = (bf16[512,4,128]{0,2,1:T(8,128)(2,1)}, bf16[512,4,128]{0,2,1:T(8,128)(2,1)S(1)}, u32[]{:S(2)}) copy-start(bf16[512,4,128]{0,2,1:T(8,128)(2,1)S(1)} %multiply_convert_fusion) | copy-start | bytes 1572868
  186.8 103.2 %all-gather.12.cloned.1.call-start = ((), (), s32[]{:S(2)}) async-start(), calls=%async_computation.3 | async-start | bytes 2359296 | tf_op jit(solution)/shard_map/all_gather | solution.py:19
  191.7 1.0 copy-start.11
  236.4 3.8 %copy-start.3 = (bf16[1024,512]{0,1:T(8,128)(2,1)S(1)}, bf16[1024,512]{0,1:T(8,128)(2,1)}, u32[]{:S(2)}) copy-start(bf16[1024,512]{0,1:T(8,128)(2,1)} %copy.174) | copy-start | bytes 3145732
  266.5 3.4 %copy-start.15 = (pred[512,512]{1,0:T(8,128)(4,1)S(1)}, pred[512,512]{1,0:T(8,128)(4,1)}, u32[]{:S(2)}) copy-start(pred[512,512]{1,0:T(8,128)(4,1)} %copy-done.14) | copy-start | bytes 786436
  269.9 2.1 copy-start.7
  290.1 16.2 %copy-start.10 = (bf16[1024,4,128]{2,0,1:T(8,128)(2,1)S(1)}, bf16[1024,4,128]{2,0,1:T(8,128)(2,1)}, u32[]{:S(2)}) copy-start(bf16[1024,4,128]{2,0,1:T(8,128)(2,1)} %copy_bitcast_fusion.1) | copy-start | bytes 3145732
  309.3 1.3 copy-start.9
Sparse Core Ops, SparseCore 0:
  20.3 52.1 all-gather.5
  75.2 62.3 all-gather.7
  186.9 49.4 all-gather.9
  242.2 47.7 all-gather.11
where the time goes:
time: 324 us; the launch traced here: 323 us
  waiting for transfers between devices  126 us (39%)
  blocking collectives  62.5 us (19%)
  matrix products  59.3 us (18%)
  local copies, waits for them, and re-layouts  30.1 us (9%)
  other arithmetic  21.5 us (7%)
  between operations  18.6 us (6%)
  loops' own time  4.74 us (1%)
    all_gather x1, waiting for transfers between devices, per_device(): lax.all_gather(end_slots.astype(jnp.bfloat16), 'seq', axis=0, tiled=True)  58.8 us
    psum x1, blocking collectives, per_device(): raw_scores = lax.psum(placed, ('seq', 'head'))  39.3 us
    all_gather x1, waiting for transfers between devices, per_device(): lax.all_gather(state_grads, 'seq', axis=0, tiled=True)  36.6 us
    all_gather x2, waiting for transfers between devices, prefix(): gathered = jax.tree.map(lambda a: lax.all_gather(a, axis), part)  30.5 us
    unnamed x1, blocking collectives  23.2 us
    unnamed x56, local copies, waits for them, and re-layouts  14.5 us
    add x7, other arithmetic, chain_combine(): later[0] + (1.0 - later[1]) * earlier[0]  7.35 us
    dot_general x1, matrix products, per_device(): jnp.einsum('the,she->hts', grads_in, values_in, preferred_element_type=jn...  7.15 us
  transfers between devices with their start and end apart: 4, of which 4 were waited for; matrix products, arithmetic and copies ran while one was open for 18% of the time, Pallas kernels for 0%

commit v1 on v0

--- a/solution.py
+++ b/solution.py
@@ -163,7 +163,8 @@
     zero_state = jnp.zeros_like(tail_state)
     valid_float = slot_valid.astype(jnp.float32)
     lengths = cand_lengths[0]
-    bounds = jnp.cumsum(lengths)
+    spots = jnp.arange(per_slab, dtype=jnp.int32)
+    bounds = jnp.sum(jnp.where(spots[None, :] <= spots[:, None], lengths[None, :], 0), axis=1)
     tok_pos = jnp.arange(cand_width, dtype=jnp.int32)
     cand_id = jnp.sum((bounds[None, :] <= tok_pos[:, None]).astype(jnp.int32), axis=1)
     cand_masks = cand_id[None, :] == jnp.arange(per_slab, dtype=jnp.int32)[:, None]

time: 324 us -> 324 us (level)
  no operation moved by 1% of the time
where the time goes in v1:
time: 324 us; the launch traced here: 323 us
  waiting for transfers between devices  126 us (39%)
  blocking collectives  62.5 us (19%)
  matrix products  59.3 us (18%)
  local copies, waits for them, and re-layouts  30.1 us (9%)
  other arithmetic  21.4 us (7%)
  between operations  18.6 us (6%)
  loops' own time  4.74 us (1%)
    all_gather x1, waiting for transfers between devices, per_device(): lax.all_gather(end_slots.astype(jnp.bfloat16), 'seq', axis=0, tiled=True)  58.8 us
    psum x1, blocking collectives, per_device(): raw_scores = lax.psum(placed, ('seq', 'head'))  39.3 us
    all_gather x1, waiting for transfers between devices, per_device(): lax.all_gather(state_grads, 'seq', axis=0, tiled=True)  36.6 us
    all_gather x2, waiting for transfers between devices, prefix(): gathered = jax.tree.map(lambda a: lax.all_gather(a, axis), part)  30.5 us
    unnamed x1, blocking collectives  23.2 us
    unnamed x56, local copies, waits for them, and re-layouts  14.5 us
    add x7, other arithmetic, chain_combine(): later[0] + (1.0 - later[1]) * earlier[0]  7.35 us
    dot_general x1, matrix products, per_device(): jnp.einsum('the,she->hts', grads_in, values_in, preferred_element_type=jn...  7.15 us
  transfers between devices with their start and end apart: 4, of which 4 were waited for; matrix products, arithmetic and copies ran while one was open for 18% of the time, Pallas kernels for 0%

profile of v1, /device:TPU:0, one launch (start us, length us, event | category | flops | bytes accessed | tf_op | source)
XLA Modules:
  0.0 322.7 jit_solution(8880196470123459439)
XLA Ops:
  7.3 0.9 convert_reduce_fusion
  8.7 2.0 fusion.95
  10.7 1.3 fusion.109
  12.2 0.7 iota_add_fusion.1
  13.1 1.3 and_convert_fusion
  14.5 1.1 reshape.319
  15.6 2.8 fusion.40
  18.5 0.9 copy-done.12
  19.4 0.7 slice.24
  21.5 0.6 compare_reduce_fusion
  23.4 0.7 fusion.104
  24.1 0.8 dynamic-update-slice
  24.9 23.2 %all-reduce.2 = (f32[8]{0:T(128)S(1)}, f32[8]{0:T(128)S(1)}) all-reduce(f32[8]{0:T(128)S(1)} %dynamic-update-slice, f32[8]{0:T(128)S(1)} %fusion.104), channel_id=1, replica_groups=mesh['seq'=8,'head'=4] {'seq'}, use_global_device_ids=true, to_apply=%add | all-reduce | flops 16 | bytes 128
  48.1 24.4 %all-gather.6.cloned.1.call-done = f32[8,4,128,128]{3,2,0,1:T(8,128)} async-done(((f32[1,4,128,128]{3,2,0,1:T(8,128)}), f32[8,4,128,128]{3,2,0,1:T(8,128)}) %all-gather.6.cloned.1.call-update) | async-done | bytes 2097168 | tf_op jit(solution)/shard_map/all_gather | solution.py:19
  72.6 1.0 copy-done.13
  73.6 0.8 fusion.63
  74.5 1.3 copy.175
  76.6 2.1 select_convert_fusion.3
  78.7 58.8 %all-gather.8.cloned.1.call-done = bf16[16,4,128,128]{3,2,0,1:T(8,128)(2,1)} async-done(((bf16[2,4,128,128]{3,2,0,1:T(8,128)(2,1)}), bf16[16,4,128,128]{3,2,0,1:T(8,128)(2,1)}) %all-gather.8.cloned.1.call-update) | async-done | bytes 2097168 | tf_op jit(solution)/shard_map/all_gather | solution.py:188
  137.6 3.1 fusion.49
  140.6 0.6 fusion.30
  141.3 1.9 multiply_reduce_fusion
  143.5 39.3 %psum.7 = f32[16]{0:T(128)S(1)} all-reduce(f32[16]{0:T(128)S(1)} %compare_select_fusion.3), channel_id=1, replica_groups=mesh['seq'=8,'head'=4] {'seq','head'}, use_global_device_ids=true, to_apply=%region_12.13 | all-reduce | flops 16 | bytes 128 | tf_op jit(solution)/shard_map/psum | solution.py:212
  183.0 0.6 multiply_reduce_fusion.1
  183.8 1.7 multiply_convert_fusion
  185.9 0.9 copy.137
  187.4 1.5 copy.173
  188.9 2.3 copy.174
  191.1 0.6 fusion.4
  191.7 1.0 copy-done.11
  192.7 7.2 %select_convert_fusion.1 = bf16[4,1024,1024]{2,1,0:T(8,128)(2,1)} fusion(bf16[1024,4,128]{0,2,1:T(8,128)(2,1)S(1)} %bitcast.187, pred[1024,1024]{1,0:T(8,128)(4,1)S(1)} %fusion.4, bf16[1024,512]{1,0:T(8,128)(2,1)} %param.18), kind=kOutput, calls=%fused_computation.3 | convolution fusion | flops 1082130432 | bytes 11534336 | tf_op jit(solution)/shard_map/the,she->hts/dot_general | solution.py:282
  199.8 36.6 %all-gather.10.cloned.1.call-done = bf16[16,4,128,128]{3,2,1,0:T(8,128)(2,1)} async-done(((bf16[2,4,128,128]{3,2,1,0:T(8,128)(2,1)}), bf16[16,4,128,128]{3,2,1,0:T(8,128)(2,1)}) %all-gather.10.cloned.1.call-update) | async-done | bytes 2097168 | tf_op jit(solution)/shard_map/all_gather | solution.py:249
  236.4 3.0 fusion.12
  239.4 0.9 fusion.108
  240.3 1.8 fusion.55
  242.1 2.4 copy_bitcast_fusion.1
  245.1 6.5 %fusion.111 = f32[4,1024,128]{1,2,0:T(8,128)} fusion(bf16[1024,4,128]{0,2,1:T(8,128)(2,1)} %bitcast.192, bf16[4,1024,1024]{2,1,0:T(8,128)(2,1)} %select_convert_fusion.1), kind=kOutput, calls=%fused_computation.161 | convolution fusion | flops 1073741824 | bytes 11534336 | tf_op jit(solution)/shard_map/hts,thd->shd/dot_general | solution.py:291
  251.6 7.0 %fusion.7 = f32[4,1024,128]{1,2,0:T(8,128)} fusion(bf16[1024,4,128]{0,2,1:T(8,128)(2,1)S(1)} %bitcast.189, bf16[1024,4,128]{0,2,1:T(8,128)(2,1)} %bitcast.193, pred[1024,1024]{1,0:T(8,128)(4,1)} %copy-done.11, bf16[1024,512]{1,0:T(8,128)(2,1)S(1)} %copy-done), kind=kOutput, calls=%fused_computation.14 | convolution fusion | flops 2155872256 | bytes 6291456 | tf_op jit(solution)/shard_map/hts,the->she/dot_general | solution.py:296
  258.6 6.5 %fusion.106 = f32[4,1024,128]{1,2,0:T(8,128)S(1)} fusion(bf16[4,1024,1024]{2,1,0:T(8,128)(2,1)} %select_convert_fusion.1, bf16[1024,512]{1,0:T(8,128)(2,1)S(1)} %copy-done), kind=kOutput, calls=%fused_computation.157 | convolution fusion | flops 1073741824 | bytes 11534336 | tf_op jit(solution)/shard_map/hts,shd->thd/dot_general | solution.py:287
  265.1 1.4 fusion.11
  266.6 2.5 copy.153
  269.3 0.6 convolution_bitcast_fusion.2
  269.9 2.1 select_convert_fusion.2
  272.1 1.6 fusion.37
  273.7 2.1 copy.156
  275.7 2.3 fusion.39
  278.0 2.0 copy.157
  280.1 2.2 fusion.38
  282.3 1.0 copy.158
  283.9 6.1 %all-gather.12.cloned.1.call-done = f32[32,128,128]{2,1,0:T(8,128)} async-done(((f32[4,128,128]{2,1,0:T(8,128)}), f32[32,128,128]{2,1,0:T(8,128)}) %all-gather.12.cloned.1.call-update) | async-done | bytes 2097168 | tf_op jit(solution)/shard_map/all_gather | solution.py:19
  290.1 16.2 %while.27 = (s32[]{:T(128)}, f32[4,128,128]{2,1,0:T(8,128)S(1)}, s32[]{:T(128)}, f32[8,4,128,128]{3,2,1,0:T(8,128)}, f32[8]{0:T(128)S(1)}, /*index=5*/s32[]{:T(128)}, s32[]{:T(128)}, s32[]{:T(128)}, s32[]{:T(128)}, f32[1]{0:T(128)}) while((s32[]{:T(128)}, f32[4,128,128]{2,1,0:T(8,128)S(1)}, s32[]{:T(128)}, f32[8,4,128,128]{3,2,1,0:T(8,128)}, ...), condition=%wide.region_18.19_spmd, body=%wide.region_17.18_spmd.sunk | while | flops 131079 | bytes 786619 | solution.py:28
  290.1 0.6 dynamic_slice.44
  291.3 1.0 bitcast_add_fusion.8
  293.7 1.0 bitcast_add_fusion.8
  296.0 1.0 bitcast_add_fusion.8
  298.3 1.0 bitcast_add_fusion.8
  300.6 1.0 bitcast_add_fusion.8
  301.7 0.6 dynamic_slice.44
  302.9 1.0 bitcast_add_fusion.8
  305.2 1.0 bitcast_add_fusion.8
  306.3 3.0 fusion.9
  309.3 1.3 copy.154
  310.7 3.1 fusion.8
  313.7 1.3 copy.155
  (98 shorter events, 7.7 us)
Async XLA Ops:
  7.2 4.8 %copy-start = (bf16[1024,512]{1,0:T(8,128)(2,1)S(1)}, bf16[1024,512]{1,0:T(8,128)(2,1)}, u32[]{:S(2)}) copy-start(bf16[1024,512]{1,0:T(8,128)(2,1)} %param.17) | copy-start | bytes 3145732
  7.2 5.7 %copy-start.18 = (s32[8]{0:T(128)S(1)}, s32[8]{0:T(128)}, u32[]{:S(2)}) copy-start(s32[8]{0:T(128)} %param.24) | copy-start | bytes 100
  7.2 7.3 %copy-start.2 = (bf16[1024,512]{1,0:T(8,128)(2,1)S(1)}, bf16[1024,512]{1,0:T(8,128)(2,1)}, u32[]{:S(2)}) copy-start(bf16[1024,512]{1,0:T(8,128)(2,1)} %param.18) | copy-start | bytes 3145732
  7.2 65.3 %all-gather.6.cloned.1.call-start = ((), (), s32[]{:S(2)}) async-start(), calls=%async_computation | async-start | bytes 2359296 | tf_op jit(solution)/shard_map/all_gather | solution.py:19
  12.2 6.3 %copy-start.8 = (bf16[1024,4,128]{2,0,1:T(8,128)(2,1)}, bf16[1024,4,128]{2,0,1:T(8,128)(2,1)S(1)}, u32[]{:S(2)}) copy-start(bf16[1024,4,128]{2,0,1:T(8,128)(2,1)S(1)} %copy_bitcast_fusion) | copy-start | bytes 3145732
  15.6 7.2 %copy-start.22 = (u32[32]{0:T(128)S(1)}, u32[32]{0:T(128)}, u32[]{:S(2)}) copy-start(u32[32]{0:T(128)} %constant.145) | copy-start | bytes 388
  18.5 0.9 copy-start.12
  20.1 117.4 %all-gather.8.cloned.1.call-start = ((), (), s32[]{:S(2)}) async-start(), calls=%async_computation.1 | async-start | bytes 2359296 | tf_op jit(solution)/shard_map/all_gather | solution.py:188
  72.5 1.1 copy-start.13
  72.5 3.3 %copy-start.16 = (s32[16]{0:T(128)S(1)}, s32[16]{0:T(128)}, u32[]{:S(2)}) copy-start(s32[16]{0:T(128)} %param.26) | copy-start | bytes 196
  72.5 3.4 %copy-start.20 = (s32[1,2]{1,0:T(1,128)S(1)}, s32[1,2]{1,0:T(1,128)}, u32[]{:S(2)}) copy-start(s32[1,2]{1,0:T(1,128)} %param.25) | copy-start | bytes 28
  72.5 4.0 %copy-start.5 = (bf16[512,512]{1,0:T(8,128)(2,1)S(1)}, bf16[512,512]{1,0:T(8,128)(2,1)}, u32[]{:S(2)}) copy-start(bf16[512,512]{1,0:T(8,128)(2,1)} %param.20) | copy-start | bytes 1572868
  74.5 162.0 %all-gather.10.cloned.1.call-start = ((), (), s32[]{:S(2)}) async-start(), calls=%async_computation.2 | async-start | bytes 2359296 | tf_op jit(solution)/shard_map/all_gather | solution.py:249
  75.8 2.9 copy-start.6
  76.5 2.2 copy-start.14
  78.7 62.6 %copy-start.17 = (f32[512]{0:T(512)S(1)}, f32[512]{0:T(512)}, u32[]{:S(2)}) copy-start(f32[512]{0:T(512)} %param.23) | copy-start | bytes 6148
  78.7 62.6 %copy-start.21 = (bf16[512,512]{1,0:T(8,128)(2,1)S(1)}, bf16[512,512]{1,0:T(8,128)(2,1)}, u32[]{:S(2)}) copy-start(bf16[512,512]{1,0:T(8,128)(2,1)} %param.22) | copy-start | bytes 1572868
  137.6 3.7 %copy-start.4 = (bf16[4,512,512]{2,1,0:T(8,128)(2,1)S(1)}, bf16[4,512,512]{2,1,0:T(8,128)(2,1)}, u32[]{:S(2)}) copy-start(bf16[4,512,512]{2,1,0:T(8,128)(2,1)} %select_convert_fusion.3) | copy-start | bytes 6291460
  141.3 2.2 copy-start.19
  185.4 83.6 %copy-start.1 = (bf16[512,4,128]{0,2,1:T(8,128)(2,1)}, bf16[512,4,128]{0,2,1:T(8,128)(2,1)S(1)}, u32[]{:S(2)}) copy-start(bf16[512,4,128]{0,2,1:T(8,128)(2,1)S(1)} %multiply_convert_fusion) | copy-start | bytes 1572868
  186.8 103.2 %all-gather.12.cloned.1.call-start = ((), (), s32[]{:S(2)}) async-start(), calls=%async_computation.3 | async-start | bytes 2359296 | tf_op jit(solution)/shard_map/all_gather | solution.py:19
  191.7 1.0 copy-start.11
  236.4 3.8 %copy-start.3 = (bf16[1024,512]{0,1:T(8,128)(2,1)S(1)}, bf16[1024,512]{0,1:T(8,128)(2,1)}, u32[]{:S(2)}) copy-start(bf16[1024,512]{0,1:T(8,128)(2,1)} %copy.174) | copy-start | bytes 3145732
  266.5 3.4 %copy-start.15 = (pred[512,512]{1,0:T(8,128)(4,1)S(1)}, pred[512,512]{1,0:T(8,128)(4,1)}, u32[]{:S(2)}) copy-start(pred[512,512]{1,0:T(8,128)(4,1)} %copy-done.14) | copy-start | bytes 786436
  269.9 2.1 copy-start.7
  290.1 16.2 %copy-start.10 = (bf16[1024,4,128]{2,0,1:T(8,128)(2,1)S(1)}, bf16[1024,4,128]{2,0,1:T(8,128)(2,1)}, u32[]{:S(2)}) copy-start(bf16[1024,4,128]{2,0,1:T(8,128)(2,1)} %copy_bitcast_fusion.1) | copy-start | bytes 3145732
  309.3 1.3 copy-start.9
Sparse Core Ops, SparseCore 0:
  20.3 52.1 all-gather.5
  75.2 62.3 all-gather.7
  186.9 49.4 all-gather.9
  242.2 47.7 all-gather.11

commit v2 on v0

v2 whole, which is shorter than its diff:
```python
import math

import jax
import jax.numpy as jnp
from jax import lax
from jax.experimental import pallas as pl
from jax.experimental.pallas import tpu as pltpu
from jax.sharding import PartitionSpec as P

E = 128
ENDS = 2
PIECES = ENDS + 1
STRIP = 256
grad_scale = 1048576.0
f32 = jnp.float32
bf16 = jnp.bfloat16
SMEM = pl.BlockSpec(memory_space=pltpu.SMEM)
VMEM = pl.BlockSpec(memory_space=pltpu.VMEM)


def dot(a, b, ca, cb):
    return lax.dot_general(a, b, (((ca,), (cb,)), ((), ())), preferred_element_type=f32)


def call(body, **kw):
    return pl.pallas_call(
        body,
        compiler_params=pltpu.CompilerParams(vmem_limit_bytes=48 * 1024 * 1024),
        **kw,
    )


def count_ends(ends, limit):
    total = jnp.int32(0)
    for p in range(ends.shape[0]):
        total += (ends[p] <= limit).astype(jnp.int32)
    return total


def end_of(ends, pid, none):
    last = ends.shape[0] - 1
    return jnp.where(pid <= last, ends[jnp.minimum(pid, last)], none)


def slab_bounds(ends, slab, width):
    start = slab * width
    first = count_ends(ends, start)
    far = start + width
    return [jnp.minimum(end_of(ends, first + m, far) - start, width) for m in range(ENDS)]


def pick_rows(rows, bounds, options):
    out = options[-1]
    for b, o in zip(reversed(bounds), reversed(options[:-1])):
        out = jnp.where(rows < b, o, out)
    return out


def rows_of(shape, start=0):
    return lax.broadcasted_iota(jnp.int32, shape, 0) + start


def strip_mask(lo, size, width, bounds):
    s = rows_of((size, 1), lo)
    t = lax.broadcasted_iota(jnp.int32, (size, width - lo), 1) + lo
    stop = pick_rows(s, bounds, [jnp.full((size, 1), b, jnp.int32) for b in bounds] + [width])
    return jnp.logical_and(t >= s, t < stop)


def store_parts(out, place, mat):
    parts, rows = out.shape[0], out.shape[2]
    for o in range(parts):
        out[o, place] = mat[o * rows : (o + 1) * rows].astype(bf16)


def load_matrix(ref, place):
    return jnp.concatenate([ref[o, place] for o in range(ref.shape[0])], axis=0)


def sums_kernel(ends, q, k, v, g, out):
    width = q.shape[0]
    bounds = slab_bounds(ends, lax.axis_index("seq"), width)
    scaling = 1.0 / math.sqrt(E * width)
    rows = rows_of((width, E))
    zero = jnp.zeros((width, E), f32)
    values = v[...].astype(f32)
    pieces = []
    low = 0
    for b in bounds + [width]:
        inside = jnp.logical_and(rows >= low, rows < b)
        pieces.append(jnp.where(inside, values, zero).astype(bf16))
        low = b
    sums = dot(k[...], jnp.concatenate(pieces, axis=1), 0, 0)
    for m in range(PIECES):
        store_parts(out, m, sums[:, m * E : (m + 1) * E])
    first = jnp.where(rows < bounds[0], g[...].astype(f32), zero).astype(bf16)
    store_parts(out, PIECES, scaling * dot(q[...], first, 0, 0))


def chain_kernel(ends, cand_prompt, parts, out, held, *, width):
    count = parts.shape[0]
    per_slab = cand_prompt.shape[0] // count
    running = jnp.zeros(parts.shape[2:], f32)
    for e in range(count):
        start = e * width
        first = count_ends(ends, start)
        last = count_ends(ends, start + width - 1)
        begins = jnp.bool_(True) if e == 0 else ends[jnp.maximum(first - 1, 0)] == start
        if e > 0:
            begins = jnp.logical_and(first > 0, begins)
        incoming = jnp.where(begins, 0.0, running)
        out[e, per_slab] = incoming.astype(bf16)
        firsts = parts[e, 0].astype(f32) + incoming
        second = parts[e, 1].astype(f32)
        third = parts[e, 2].astype(f32)
        spare = ends.shape[0]
        for m, piece in enumerate((firsts, second)):
            ended = end_of(ends, first + m, start + width + 1) <= start + width
            held[jnp.where(ended, first + m, spare)] = piece
        running = jnp.where(last == first, firsts, jnp.where(last == first + 1, second, third))
    for c in range(cand_prompt.shape[0]):
        out[c // per_slab, c % per_slab] = held[cand_prompt[c]].astype(bf16)


def inside_kernel(lengths, q, k, v, out):
    width = q.shape[0]
    bounds = cand_bounds(lengths)
    for lo in range(0, width, STRIP):
        hi = lo + STRIP
        scores = dot(q[lo:hi], k[:hi], 1, 1)
        t = rows_of((STRIP, hi), lo)
        s = lax.broadcasted_iota(jnp.int32, (STRIP, hi), 1)
        begin = pick_rows(t[:, :1], bounds, [0] + [jnp.full((STRIP, 1), b, jnp.int32) for b in bounds])
        keep = jnp.logical_and(s <= t, s >= begin)
        out[lo:hi] = dot(jnp.where(keep, scores, 0.0).astype(bf16), v[:hi], 1, 0)


def cand_bounds(lengths):
    bounds = []
    total = jnp.int32(0)
    for j in range(lengths.shape[1] - 1):
        total += lengths[0, j]
        bounds.append(total)
    return bounds


def scores_kernel(lengths, q, inside, readout, states, slope_out, raw_out, grads_out, *, scaling):
    h = pl.program_id(0)
    width = q.shape[0]
    per_slab = lengths.shape[1]
    bounds = cand_bounds(lengths)
    rows = rows_of((width, E))
    wide = jnp.concatenate([load_matrix(states, j) for j in range(per_slab)], axis=1)
    crossed = dot(q[...], wide, 1, 0)
    crossed = pick_rows(rows, bounds, [crossed[:, j * E : (j + 1) * E] for j in range(per_slab)])
    out = scaling * (inside[...] + crossed)
    inverse = [1.0 / jnp.full((1, E), lengths[0, j], jnp.int32).astype(f32) for j in range(per_slab)]
    weight = pick_rows(rows, bounds, inverse) * readout[...]
    sigma = jax.nn.sigmoid(out)
    silu = out * sigma * weight
    slope = weight * sigma * (1.0 + out * (1.0 - sigma))
    slope_out[...] = slope
    zero = jnp.zeros((width, E), f32)
    masked = []
    totals = []
    low = 0
    for b in bounds + [width]:
        mine = jnp.logical_and(rows >= low, rows < b)
        masked.append(jnp.where(mine, slope, zero).astype(bf16))
        column = jnp.sum(jnp.where(mine, silu, zero), axis=0, keepdims=True)
        totals.append(jnp.broadcast_to(jnp.sum(column, axis=1, keepdims=True), (1, E)))
        low = b
    grads = scaling * dot(q[...], jnp.concatenate(masked, axis=1), 0, 0)
    for j in range(per_slab):
        store_parts(grads_out, j, grads[:, j * E : (j + 1) * E])
    spare = jnp.zeros((8 - per_slab, E), f32)
    tile = jnp.concatenate(totals + [spare], axis=0)

    @pl.when(h == 0)
    def _():
        raw_out[...] = jnp.broadcast_to(tile[None], raw_out.shape)

    @pl.when(h > 0)
    def _():
        raw_out[...] += jnp.broadcast_to(tile[None], raw_out.shape)


def listwise_kernel(
    ends,
    prompts,
    prompt_row,
    rank_row,
    raws,
    grads,
    parts,
    out,
    coef_out,
    loss_out,
    raw_held,
    coef_held,
    held,
    *,
    width,
):
    count = grads.shape[0]
    per_slab = grads.shape[1]
    groups = raws.shape[0] // count
    cands = count * per_slab
    prompt_count = ends.shape[0]
    for e in range(count):
        total = raws[e * groups, :per_slab]
        for i in range(1, groups):
            total += raws[e * groups + i, :per_slab]
        raw_held[e * per_slab : (e + 1) * per_slab] = total
    raw = raw_held[...]
    square = (cands, cands)
    down = lax.broadcasted_iota(jnp.int32, square, 0)
    across = lax.broadcasted_iota(jnp.int32, square, 1)
    same_spot = down == across
    own = jnp.broadcast_to(prompt_row[...], square)
    own_down = jnp.sum(jnp.where(same_spot, own, 0.0), axis=1, keepdims=True)
    group = own == own_down
    rank_weight = jnp.broadcast_to(jnp.exp(-rank_row[...]), square)
    rank_down = jnp.sum(jnp.where(same_spot, rank_weight, 0.0), axis=1, keepdims=True)
    target = rank_down / jnp.sum(jnp.where(group, rank_weight, 0.0), axis=1, keepdims=True)
    tanh_raw = jnp.tanh(raw)
    squashed = 3.0 * tanh_raw
    exp_scores = jnp.exp(squashed)
    exp_across = jnp.sum(jnp.where(same_spot, exp_scores[:, :cands], 0.0), axis=0, keepdims=True)
    denom = jnp.sum(jnp.where(group, jnp.broadcast_to(exp_across, square), 0.0), axis=1, keepdims=True)
    terms = target * (squashed - jnp.log(denom))
    loss_out[...] = -jnp.sum(terms, axis=0, keepdims=True) / prompt_count
    coef = grad_scale / prompt_count * (exp_scores / denom - target) * 3.0 * (1.0 - tanh_raw * tanh_raw)
    coef_held[...] = coef
    me = lax.axis_index("seq")
    for j in range(per_slab):
        coef_out[j : j + 1] = coef_held[pl.ds(me * per_slab + j, 1)]
    held[...] = jnp.zeros_like(held)
    for c in range(cands):
        piece = grads[c // per_slab, c % per_slab].astype(f32) * coef[c : c + 1]
        held[prompts[c]] += piece.astype(bf16).astype(f32)
    running = jnp.zeros(parts.shape[2:], f32)
    for e in reversed(range(count)):
        start = e * width
        far = start + width
        first = count_ends(ends, start)
        last = count_ends(ends, far - 1)
        goes_on = ends[last] != far
        from_right = jnp.where(goes_on, running, 0.0)
        from_right_bf = from_right.astype(bf16)
        for m in range(ENDS):
            pid = first + m
            ended = end_of(ends, pid, far + 1) <= far
            here = held[jnp.minimum(pid, prompt_count - 1)]
            out[e, m] = jnp.where(ended, here, from_right).astype(bf16)
            if m == 0:
                running = parts[e, PIECES].astype(f32) + jnp.where(ended, here, running)
        out[e, ENDS] = from_right_bf


def cand_kernel(lengths, coef, q, k, v, slope, states, dq, dk, dv, *, scaling):
    width = q.shape[0]
    per_slab = lengths.shape[1]
    bounds = cand_bounds(lengths)
    rows = rows_of((width, E))
    dout = (pick_rows(rows, bounds, [coef[j : j + 1] for j in range(per_slab)]) * slope[...]).astype(bf16)
    wide = jnp.concatenate([load_matrix(states, j) for j in range(per_slab)], axis=0)
    crossed = dot(dout, wide, 1, 1)
    total = pick_rows(rows, bounds, [crossed[:, j * E : (j + 1) * E] for j in range(per_slab)])
    blocks = []
    for lo in range(0, width, STRIP):
        hi = lo + STRIP
        keep = strip_mask(lo, STRIP, width, bounds)
        keys = k[lo:hi]
        attn = jnp.where(keep, dot(keys, q[lo:], 1, 1), 0.0).astype(bf16)
        gw = jnp.where(keep, dot(v[lo:hi], dout[lo:], 1, 1), 0.0).astype(bf16)
        dk[lo:hi] = (scaling * dot(gw, q[lo:], 1, 0)).astype(bf16)
        dv[lo:hi] = (scaling * dot(attn, dout[lo:], 1, 0)).astype(bf16)
        total = total + dot(gw, keys, 0, 0)
        blocks.append((lo, hi, total[:STRIP]))
        total = total[STRIP:]
    for lo, hi, block in blocks:
        dq[lo:hi] = (scaling * block).astype(bf16)


def prompt_kernel(ends, q, k, v, g, dq, dk, dv):
    width = q.shape[0]
    scaling = 1.0 / math.sqrt(E * width)
    bounds = slab_bounds(ends, lax.axis_index("seq"), width)
    for lo in range(0, width, STRIP):
        hi = lo + STRIP
        keep = strip_mask(lo, STRIP, width, bounds)
        keys = k[lo:hi]
        attn = jnp.where(keep, dot(keys, q[lo:], 1, 1), 0.0).astype(bf16)
        gw = jnp.where(keep, dot(v[lo:hi], g[lo:], 1, 1), 0.0).astype(bf16)
        dk[lo:hi] = scaling * dot(gw, q[lo:], 1, 0)
        dv[lo:hi] = scaling * dot(attn, g[lo:], 1, 0)
        part = dot(gw, keys, 0, 0)
        if lo == 0:
            dq[...] = part
        else:
            dq[lo:] += part


def query_kernel(ends, part, g, states, dq):
    width = g.shape[0]
    scaling = 1.0 / math.sqrt(E * width)
    bounds = slab_bounds(ends, lax.axis_index("seq"), width)
    carry = load_matrix(states, states.shape[1] - 1)
    crossed = dot(g[...], carry, 1, 1)
    rows = rows_of((width, E))
    dq[...] = (scaling * (part[...] + jnp.where(rows < bounds[0], crossed, 0.0))).astype(bf16)


def right_kernel(ends, dk_part, dv_part, k, v, states, dk, dv):
    width = k.shape[0]
    bounds = slab_bounds(ends, lax.axis_index("seq"), width)
    rows = rows_of((width, E))
    mats = [load_matrix(states, m) for m in range(PIECES)]
    by_v = dot(v[...], jnp.concatenate(mats, axis=0), 1, 1)
    by_k = dot(k[...], jnp.concatenate(mats, axis=1), 1, 0)
    cut = lambda a: [a[:, m * E : (m + 1) * E] for m in range(PIECES)]
    dk[...] = (dk_part[...] + pick_rows(rows, bounds, cut(by_v))).astype(bf16)
    dv[...] = (dv_part[...] + pick_rows(rows, bounds, cut(by_k))).astype(bf16)


def exchange(a):
    return lax.all_to_all(a, "seq", 0, 0, tiled=True)


def per_device(
    prompt_q,
    prompt_k,
    prompt_v,
    prompt_grad,
    cand_q,
    cand_k,
    cand_v,
    readout,
    prompt_ends,
    cand_lengths,
    cand_prompt,
    cand_ranks,
):
    width = prompt_q.shape[0]
    cand_width = cand_q.shape[0]
    flat = prompt_q.shape[1]
    heads = flat // E
    count = lax.axis_size("seq")
    groups = lax.axis_size("head")
    per_slab = cand_lengths.shape[1]
    cands = cand_prompt.shape[0]
    scaling = 1.0 / math.sqrt(E * width)
    rows = flat // count
    share = count // heads
    whole = pl.BlockSpec((width, E), lambda h: (0, h))
    cand_block = pl.BlockSpec((cand_width, E), lambda h: (0, h))
    like = jax.ShapeDtypeStruct

    def parts_block(n):
        return pl.BlockSpec((share, n, rows, E), lambda h: (h, 0, 0, 0))

    pieces = call(
        sums_kernel,
        grid=(heads,),
        in_specs=[SMEM] + [whole] * 4,
        out_specs=parts_block(PIECES + 1),
        out_shape=like((count, PIECES + 1, rows, E), bf16),
        name="sums",
    )(prompt_ends, prompt_q, prompt_k, prompt_v, prompt_grad)
    parts = exchange(pieces)

    dq_part, dk_part, dv_part = call(
        prompt_kernel,
        grid=(heads,),
        in_specs=[SMEM] + [whole] * 4,
        out_specs=[whole] * 3,
        out_shape=[like((width, flat), f32)] * 3,
        name="prompt",
    )(prompt_ends, prompt_q, prompt_k, prompt_v, prompt_grad)

    chained = call(
        lambda *refs: chain_kernel(*refs, width=width),
        in_specs=[SMEM, SMEM, VMEM],
        out_specs=VMEM,
        out_shape=like((count, per_slab + 1, rows, E), bf16),
        scratch_shapes=[pltpu.VMEM((prompt_ends.shape[0] + 1, rows, E), f32)],
        name="chain",
    )(prompt_ends, cand_prompt, parts)
    states = exchange(chained)

    inside = call(
        inside_kernel,
        grid=(heads,),
        in_specs=[SMEM] + [cand_block] * 3,
        out_specs=cand_block,
        out_shape=like((cand_width, flat), f32),
        name="inside",
    )(cand_lengths, cand_q, cand_k, cand_v)

    slope, raw, grads = call(
        lambda *refs: scores_kernel(*refs, scaling=scaling),
        grid=(heads,),
        in_specs=[
            SMEM,
            cand_block,
            cand_block,
            pl.BlockSpec((1, E), lambda h: (0, h)),
            parts_block(per_slab + 1),
        ],
        out_specs=[
            cand_block,
            pl.BlockSpec((count * groups, 8, E), lambda h: (0, 0, 0)),
            parts_block(per_slab),
        ],
        out_shape=[
            like((cand_width, flat), f32),
            like((count * groups, 8, E), f32),
            like((count, per_slab, rows, E), bf16),
        ],
        name="scores",
    )(cand_lengths, cand_q, inside, readout.reshape(1, flat), states)
    raws = lax.all_to_all(raw, ("seq", "head"), 0, 0, tiled=True)
    all_grads = exchange(grads)

    prompt_dq = call(
        query_kernel,
        grid=(heads,),
        in_specs=[SMEM, whole, whole, parts_block(per_slab + 1)],
        out_specs=whole,
        out_shape=like((width, flat), bf16),
        name="query",
    )(prompt_ends, dq_part, prompt_grad, states)

    right, coef, loss = call(
        lambda *refs: listwise_kernel(*refs, width=width),
        in_specs=[SMEM, SMEM] + [VMEM] * 5,
        out_specs=[VMEM] * 3,
        out_shape=[
            like((count, PIECES, rows, E), bf16),
            like((8, E), f32),
            like((1, E), f32),
        ],
        scratch_shapes=[
            pltpu.VMEM((cands, E), f32),
            pltpu.VMEM((cands, E), f32),
            pltpu.VMEM((prompt_ends.shape[0], rows, E), f32),
        ],
        name="listwise",
    )(
        prompt_ends,
        cand_prompt,
        cand_prompt.astype(f32).reshape(1, cands),
        cand_ranks.astype(f32).reshape(1, cands),
        raws,
        all_grads,
        parts,
    )
    rights = exchange(right)

    cand_dq, cand_dk, cand_dv = call(
        lambda *refs: cand_kernel(*refs, scaling=scaling),
        grid=(heads,),
        in_specs=[SMEM, pl.BlockSpec((8, E), lambda h: (0, 0))]
        + [cand_block] * 4
        + [parts_block(per_slab + 1)],
        out_specs=[cand_block] * 3,
        out_shape=[like((cand_width, flat), bf16)] * 3,
        name="cand",
    )(cand_lengths, coef, cand_q, cand_k, cand_v, slope, states)

    prompt_dk, prompt_dv = call(
        right_kernel,
        grid=(heads,),
        in_specs=[SMEM] + [whole] * 4 + [parts_block(PIECES)],
        out_specs=[whole] * 2,
        out_shape=[like((width, flat), bf16)] * 2,
        name="right",
    )(prompt_ends, dk_part, dv_part, prompt_k, prompt_v, rights)
    return (
        prompt_dq,
        prompt_dk,
        prompt_dv,
        cand_dq,
        cand_dk,
        cand_dv,
        loss[0, 0],
    )


def solution(mesh):
    tile = P("seq", "head")
    return jax.shard_map(
        per_device,
        mesh=mesh,
        in_specs=(tile,) * 7 + (P("head"), P(), P("seq", None), P(), P()),
        out_specs=(tile,) * 6 + (P(),),
        check_vma=False,
    )
```

time: 324 us -> 120 us (0.37)
  waiting for transfers between devices: 126 us -> 15.2 us
  matrix products: 59.3 us -> 0 us
  Pallas kernels: 0 us -> 37.1 us
  blocking collectives: 62.5 us -> 33.5 us
  other arithmetic: 21.5 us -> 1.68 us
  between operations: 18.6 us -> 0.84 us
  starting transfers between devices: 0.16 us -> 11.7 us
  local copies, waits for them, and re-layouts: 30.1 us -> 19 us
  loops' own time: 4.74 us -> 0 us
    all_gather x4 -> x0, waiting for transfers between devices: 126 us -> none  [the longest x1 58.8 us: per_device(): lax.all_gather(end_slots.astype(jnp.bfloat16), 'seq', axis=0, tiled=True)]
    dot_general x20 -> x0, matrix products: 59.3 us -> none  [the longest x1 7.15 us: per_device(): jnp.einsum('the,she->hts', grads_in, values_in, preferred_element_type=jn...]
    psum x1 -> x0, blocking collectives: 39.3 us -> none  [per_device(): raw_scores = lax.psum(placed, ('seq', 'head'))]
    pallas_call x0 -> x9, Pallas kernels: none -> 37.1 us  [the longest x1 11.1 us: per_device(): call(prompt_kernel, grid=(heads,), in_specs=[SMEM] + [whole] * 4, out_spe...]
    all_to_all x0 -> x2, blocking collectives: none -> 33.5 us  [the longest x1 21.7 us: exchange(): return lax.all_to_all(a, 'seq', 0, 0, tiled=True)]
    unnamed x1 -> x0, blocking collectives: 23.2 us -> none
    all_to_all x0 -> x3, waiting for transfers between devices: none -> 15.2 us  [exchange(): return lax.all_to_all(a, 'seq', 0, 0, tiled=True)]
    all_to_all x0 -> x3, starting transfers between devices: none -> 11.7 us  [exchange(): return lax.all_to_all(a, 'seq', 0, 0, tiled=True)]
  transfers between devices with their start and end apart: 4 -> 3, of which waited for: 4 -> 2; matrix products, arithmetic and copies ran while one was open for 18% -> 1% of each run, Pallas kernels for 0% -> 19%
where the time goes in v2:
time: 120 us; the launch traced here: 119 us
  Pallas kernels  37.1 us (31%)
  blocking collectives  33.5 us (28%)
  local copies, waits for them, and re-layouts  19 us (16%)
  waiting for transfers between devices  15.2 us (13%)
  starting transfers between devices  11.7 us (10%)
  other arithmetic  1.68 us (1%)
    all_to_all x1, blocking collectives, exchange(): return lax.all_to_all(a, 'seq', 0, 0, tiled=True)  21.7 us
    unnamed x66, local copies, waits for them, and re-layouts  19 us
    all_to_all x3, waiting for transfers between devices, exchange(): return lax.all_to_all(a, 'seq', 0, 0, tiled=True)  15.2 us
    all_to_all x1, blocking collectives, per_device(): raws = lax.all_to_all(raw, ('seq', 'head'), 0, 0, tiled=True)  11.8 us
    all_to_all x3, starting transfers between devices, exchange(): return lax.all_to_all(a, 'seq', 0, 0, tiled=True)  11.7 us
    pallas_call x1, Pallas kernels, per_device(): call(prompt_kernel, grid=(heads,), in_specs=[SMEM] + [whole] * 4, out_spe...  11.1 us
    pallas_call x1, Pallas kernels, per_device(): call(lambda *refs: cand_kernel(*refs, scaling=scaling), grid=(heads,), in...  5.38 us
    pallas_call x1, Pallas kernels, per_device(): call(right_kernel, grid=(heads,), in_specs=[SMEM] + [whole] * 4 + [parts_...  5 us
  transfers between devices with their start and end apart: 3, of which 2 were waited for; matrix products, arithmetic and copies ran while one was open for 1% of the time, Pallas kernels for 19%

profile of v2, /device:TPU:0, one launch (start us, length us, event | category | flops | bytes accessed | tf_op | source)
XLA Modules:
  0.0 119.0 jit_solution(16720407608900425525)
XLA Ops:
  0.6 0.0 copy-start
  0.6 1.2 %copy-done = bf16[1024,512]{1,0:T(8,128)(2,1)S(1)} copy-done((bf16[1024,512]{1,0:T(8,128)(2,1)S(1)}, bf16[1024,512]{1,0:T(8,128)(2,1)}, u32[]{:S(2)}) %copy-start) | copy-done | bytes 1048600
  1.9 0.0 copy-start.2
  1.9 1.2 %copy-done.2 = bf16[1024,512]{1,0:T(8,128)(2,1)S(1)} copy-done((bf16[1024,512]{1,0:T(8,128)(2,1)S(1)}, bf16[1024,512]{1,0:T(8,128)(2,1)}, u32[]{:S(2)}) %copy-start.2) | copy-done | bytes 1048600
  3.1 0.0 copy-start.4
  3.1 1.2 %copy-done.4 = bf16[1024,512]{1,0:T(8,128)(2,1)S(1)} copy-done((bf16[1024,512]{1,0:T(8,128)(2,1)S(1)}, bf16[1024,512]{1,0:T(8,128)(2,1)}, u32[]{:S(2)}) %copy-start.4) | copy-done | bytes 1048600
  4.3 0.0 copy-start.11
  4.3 1.2 %copy-done.11 = bf16[1024,512]{1,0:T(8,128)(2,1)S(1)} copy-done((bf16[1024,512]{1,0:T(8,128)(2,1)S(1)}, bf16[1024,512]{1,0:T(8,128)(2,1)}, u32[]{:S(2)}) %copy-start.11) | copy-done | bytes 1048600
  5.5 0.0 copy-start.26
  5.5 0.7 copy-done.26
  6.2 3.1 %sums.1 = bf16[8,4,64,128]{3,2,1,0:T(8,128)(2,1)S(1)} custom-call(s32[8]{0:T(128)S(1)} %copy-done.26, bf16[1024,512]{1,0:T(8,128)(2,1)S(1)} %copy-done.11, bf16[1024,512]{1,0:T(8,128)(2,1)S(1)} %copy-done.2, bf16[1024,512]{1,0:T(8,128)(2,1)S(1)} %copy-done.4, bf16[1024,512]{1,0:T(8,128)(2,1)S(1)} %copy-done), custom_call_target="tpu_custom_call" | custom-call | tf_op jit(solution)/shard_map/sums/pallas_call | solution.py:363
  9.3 0.0 copy-start.6
  9.3 0.0 copy-start.17
  9.3 0.0 copy-start.19
  9.3 0.0 copy-start.28
  9.3 21.7 %all_to_all.25.refs_2_.refs_6_ = bf16[8,4,64,128]{3,2,1,0:T(8,128)(2,1)S(1)} all-to-all(bf16[8,4,64,128]{3,2,1,0:T(8,128)(2,1)S(1)} %sums.1), channel_id=1, replica_groups=mesh['seq'=8,'head'=4] {'seq'}, dimensions={0} | all-to-all | bytes 1048576 | tf_op jit(solution)/shard_map/all_to_all | solution.py:328
  31.1 0.0 copy-done.27
  31.1 0.0 copy-done.29
  31.1 1.5 %chain.1 = bf16[8,3,64,128]{3,2,1,0:T(8,128)(2,1)} custom-call(s32[8]{0:T(128)S(1)} %copy-done.27, s32[16]{0:T(128)S(1)} %copy-done.29, bf16[8,4,64,128]{3,2,1,0:T(8,128)(2,1)S(1)} %all_to_all.25.refs_2_.refs_6_), custom_call_target="tpu_custom_call" | custom-call | tf_op jit(solution)/shard_map/chain/pallas_call | solution.py:382
  32.6 0.8 copy-done.9
  33.4 3.6 %all-to-all-start.1 = ((bf16[8,3,64,128]{3,2,1,0:T(8,128)(2,1)}), bf16[8,3,64,128]{3,2,1,0:T(8,128)(2,1)S(1)}, u32[]{:S(2)}, u32[]{:S(2)}) async-start(bf16[8,3,64,128]{3,2,1,0:T(8,128)(2,1)} %chain.1), calls=%async_computation.1 | async-start | bytes 786432 | tf_op jit(solution)/shard_map/all_to_all | solution.py:328
  37.0 0.0 copy-done.6
  37.0 0.0 copy-done.17
  37.0 0.0 copy-done.19
  37.0 0.0 copy-done.28
  37.0 3.1 %inside.1.refs_2_ = f32[512,512]{1,0:T(8,128)S(1)} custom-call(s32[1,2]{1,0:T(1,128)S(1)} %copy-done.28, bf16[512,512]{1,0:T(8,128)(2,1)S(1)} %copy-done.6, bf16[512,512]{1,0:T(8,128)(2,1)S(1)} %copy-done.17, bf16[512,512]{1,0:T(8,128)(2,1)S(1)} %copy-done.19), custom_call_target="tpu_custom_call" | custom-call | tf_op jit(solution)/shard_map/inside/pallas_call | solution.py:392
  40.1 0.0 copy-start.13
  40.1 1.0 copy-done.13
  41.1 7.3 %all-to-all-done.1.states.refs_4_.refs_6_ = bf16[8,3,64,128]{3,2,1,0:T(8,128)(2,1)S(1)} async-done(((bf16[8,3,64,128]{3,2,1,0:T(8,128)(2,1)}), bf16[8,3,64,128]{3,2,1,0:T(8,128)(2,1)S(1)}, u32[]{:S(2)}, u32[]{:S(2)}) %all-to-all-start.1) | async-done | bytes 393248 | tf_op jit(solution)/shard_map/all_to_all | solution.py:328
  48.4 0.0 copy-done.30
  48.4 1.0 copy-done.7
  49.4 1.2 %copy-done.14 = f32[512,512]{1,0:T(8,128)S(1)} copy-done((f32[512,512]{1,0:T(8,128)S(1)}, f32[512,512]{1,0:T(8,128)}, u32[]{:S(2)}) %copy-start.14) | copy-done | bytes 1048600
  50.6 3.0 %scores.1 = (f32[512,512]{1,0:T(8,128)S(1)}, f32[32,8,128]{2,1,0:T(8,128)S(1)}, bf16[8,2,64,128]{3,2,1,0:T(8,128)(2,1)S(1)}) custom-call(s32[1,2]{1,0:T(1,128)S(1)} %copy-done.28, bf16[512,512]{1,0:T(8,128)(2,1)S(1)} %copy-done.7, f32[512,512]{1,0:T(8,128)S(1)} %copy-done.14, f32[1,512]{1,0:T(1,128)S(1)} %bitcast.7, ...), custom_call_target="tpu_custom_call" | custom-call | tf_op jit(solution)/shard_map/scores/pallas_call | solution.py:401
  53.6 0.0 copy-start.21
  53.6 1.0 copy-done.21
  54.6 11.8 %all_to_all.26.refs_4_ = f32[32,8,128]{2,1,0:T(8,128)} all-to-all(f32[32,8,128]{2,1,0:T(8,128)S(1)} %get-tuple-element.24), channel_id=1, replica_groups=mesh['seq'=8,'head'=4] {'seq','head'}, dimensions={0} | all-to-all | bytes 262144 | tf_op jit(solution)/shard_map/all_to_all | solution.py:423
  66.4 0.0 copy-done.25
  66.4 4.0 %all-to-all-start.3 = ((bf16[8,2,64,128]{3,2,1,0:T(8,128)(2,1)}), bf16[8,2,64,128]{3,2,1,0:T(8,128)(2,1)}, u32[]{:S(2)}, u32[]{:S(2)}) async-start(bf16[8,2,64,128]{3,2,1,0:T(8,128)(2,1)} %copy-done.25), calls=%async_computation.3 | async-start | bytes 524288 | tf_op jit(solution)/shard_map/all_to_all | solution.py:328
  70.4 0.5 convert_bitcast_fusion.1.refs_2_
  71.0 1.2 convert_bitcast_fusion.refs_3_
  72.1 7.9 %all-to-all-done.3.refs_5_ = bf16[8,2,64,128]{3,2,1,0:T(8,128)(2,1)} async-done(((bf16[8,2,64,128]{3,2,1,0:T(8,128)(2,1)}), bf16[8,2,64,128]{3,2,1,0:T(8,128)(2,1)}, u32[]{:S(2)}, u32[]{:S(2)}) %all-to-all-start.3) | async-done | bytes 262176 | tf_op jit(solution)/shard_map/all_to_all | solution.py:328
  80.0 1.0 copy-done.10
  81.1 0.9 copy-done.23
  82.0 0.7 copy-done.31
  82.6 0.7 copy-done.32
  83.3 1.9 %listwise.1 = (bf16[8,3,64,128]{3,2,1,0:T(8,128)(2,1)S(1)}, f32[8,128]{1,0:T(8,128)S(1)}, f32[1,128]{1,0:T(1,128)}) custom-call(s32[8]{0:T(128)S(1)} %copy-done.27, s32[16]{0:T(128)S(1)} %copy-done.29, f32[1,16]{1,0:T(1,128)S(1)} %copy-done.31, f32[1,16]{1,0:T(1,128)S(1)} %copy-done.32, f32[32,8,128]{2,1,0:T(8,128)S(1)} %copy-done.23, ...), custom_call_target="tpu_custom_call" | custom-call | tf_op jit(solution)/shard_map/listwise/pallas_call | solution.py:435
  85.2 0.7 copy-done.24
  85.9 4.1 %all-to-all-start.4 = ((bf16[8,3,64,128]{3,2,1,0:T(8,128)(2,1)}), bf16[8,3,64,128]{3,2,1,0:T(8,128)(2,1)}, u32[]{:S(2)}, u32[]{:S(2)}) async-start(bf16[8,3,64,128]{3,2,1,0:T(8,128)(2,1)} %copy-done.24), calls=%async_computation.4 | async-start | bytes 786432 | tf_op jit(solution)/shard_map/all_to_all | solution.py:328
  90.0 0.0 copy-done.1
  90.1 0.0 copy-done.3
  90.1 0.0 copy-done.5
  90.1 0.0 copy-start.12
  90.1 1.2 %copy-done.12 = bf16[1024,512]{1,0:T(8,128)(2,1)S(1)} copy-done((bf16[1024,512]{1,0:T(8,128)(2,1)S(1)}, bf16[1024,512]{1,0:T(8,128)(2,1)}, u32[]{:S(2)}) %copy-start.12) | copy-done | bytes 1048600
  91.3 11.1 %prompt.1 = (f32[1024,512]{1,0:T(8,128)}, f32[1024,512]{1,0:T(8,128)}, f32[1024,512]{1,0:T(8,128)}) custom-call(s32[8]{0:T(128)S(1)} %copy-done.27, bf16[1024,512]{1,0:T(8,128)(2,1)S(1)} %copy-done.12, bf16[1024,512]{1,0:T(8,128)(2,1)S(1)} %copy-done.3, bf16[1024,512]{1,0:T(8,128)(2,1)S(1)} %copy-done.5, bf16[1024,512]{1,0:T(8,128)(2,1)S(1)} %copy-done.1), custom_call_target="tpu_custom_call" | custom-call | tf_op jit(solution)/shard_map/prompt/pallas_call | solution.py:373
  102.4 1.6 %copy-done.15 = f32[1024,512]{1,0:T(8,128)S(1)} copy-done((f32[1024,512]{1,0:T(8,128)S(1)}, f32[1024,512]{1,0:T(8,128)}, u32[]{:S(2)}) %copy-start.15) | copy-done | bytes 2097176
  104.0 3.0 %query.1 = bf16[1024,512]{1,0:T(8,128)(2,1)} custom-call(s32[8]{0:T(128)S(1)} %copy-done.27, f32[1024,512]{1,0:T(8,128)S(1)} %copy-done.15, bf16[1024,512]{1,0:T(8,128)(2,1)S(1)} %copy-done.1, bf16[8,3,64,128]{3,2,1,0:T(8,128)(2,1)S(1)} %all-to-all-done.1.states.refs_4_.refs_6_), custom_call_target="tpu_custom_call" | custom-call | tf_op jit(solution)/shard_map/query/pallas_call | solution.py:426
  107.0 0.0 copy-done.8
  107.0 0.0 copy-done.18
  107.0 0.0 copy-done.20
  107.0 0.0 copy-done.22
  107.1 5.4 %cand.1 = (bf16[512,512]{1,0:T(8,128)(2,1)}, bf16[512,512]{1,0:T(8,128)(2,1)}, bf16[512,512]{1,0:T(8,128)(2,1)}) custom-call(s32[1,2]{1,0:T(1,128)S(1)} %copy-done.28, f32[8,128]{1,0:T(8,128)S(1)} %get-tuple-element.29.refs_1_, bf16[512,512]{1,0:T(8,128)(2,1)S(1)} %copy-done.8, bf16[512,512]{1,0:T(8,128)(2,1)S(1)} %copy-done.18, ...), custom_call_target="tpu_custom_call" | custom-call | tf_op jit(solution)/shard_map/cand/pallas_call | solution.py:461
  112.4 0.0 all-to-all-done.4.states
  112.4 1.6 %copy-done.16 = f32[1024,512]{1,0:T(8,128)S(1)} copy-done((f32[1024,512]{1,0:T(8,128)S(1)}, f32[1024,512]{1,0:T(8,128)}, u32[]{:S(2)}) %copy-start.16) | copy-done | bytes 2097176
  114.0 5.0 %right.1 = (bf16[1024,512]{1,0:T(8,128)(2,1)}, bf16[1024,512]{1,0:T(8,128)(2,1)}) custom-call(s32[8]{0:T(128)S(1)} %copy-done.27, f32[1024,512]{1,0:T(8,128)S(1)} %copy-done.16, f32[1024,512]{1,0:T(8,128)} %get-tuple-element.23.dv_part, bf16[1024,512]{1,0:T(8,128)(2,1)S(1)} %copy-done.3, bf16[1024,512]{1,0:T(8,128)(2,1)S(1)} %copy-done.5, ...), custom_call_target="tpu_custom_call" | custom-call | tf_op jit(solution)/shard_map/right/pallas_call | solution.py:472
  (21 shorter events, 0.0 us)
Async XLA Ops:
  0.6 1.2 %copy-start = (bf16[1024,512]{1,0:T(8,128)(2,1)S(1)}, bf16[1024,512]{1,0:T(8,128)(2,1)}, u32[]{:S(2)}) copy-start(bf16[1024,512]{1,0:T(8,128)(2,1)} %g.5) | copy-start | bytes 3145732
  1.9 1.2 %copy-start.2 = (bf16[1024,512]{1,0:T(8,128)(2,1)S(1)}, bf16[1024,512]{1,0:T(8,128)(2,1)}, u32[]{:S(2)}) copy-start(bf16[1024,512]{1,0:T(8,128)(2,1)} %k.7) | copy-start | bytes 3145732
  3.1 1.2 %copy-start.4 = (bf16[1024,512]{1,0:T(8,128)(2,1)S(1)}, bf16[1024,512]{1,0:T(8,128)(2,1)}, u32[]{:S(2)}) copy-start(bf16[1024,512]{1,0:T(8,128)(2,1)} %v.7) | copy-start | bytes 3145732
  4.3 1.2 %copy-start.11 = (bf16[1024,512]{1,0:T(8,128)(2,1)S(1)}, bf16[1024,512]{1,0:T(8,128)(2,1)}, u32[]{:S(2)}) copy-start(bf16[1024,512]{1,0:T(8,128)(2,1)} %q.4) | copy-start | bytes 3145732
  5.5 0.7 copy-start.26
  6.2 24.9 %copy-start.27 = (s32[8]{0:T(128)S(1)}, s32[8]{0:T(128)}, u32[]{:S(2)}) copy-start(s32[8]{0:T(128)} %ends.7) | copy-start | bytes 100
  6.2 24.9 %copy-start.29 = (s32[16]{0:T(128)S(1)}, s32[16]{0:T(128)}, u32[]{:S(2)}) copy-start(s32[16]{0:T(128)} %refs_1_.5) | copy-start | bytes 196
  9.3 27.7 %copy-start.6 = (bf16[512,512]{1,0:T(8,128)(2,1)S(1)}, bf16[512,512]{1,0:T(8,128)(2,1)}, u32[]{:S(2)}) copy-start(bf16[512,512]{1,0:T(8,128)(2,1)} %refs_2_.1) | copy-start | bytes 1572868
  9.3 27.7 %copy-start.17 = (bf16[512,512]{1,0:T(8,128)(2,1)S(1)}, bf16[512,512]{1,0:T(8,128)(2,1)}, u32[]{:S(2)}) copy-start(bf16[512,512]{1,0:T(8,128)(2,1)} %refs_3_.1) | copy-start | bytes 1572868
  9.3 27.7 %copy-start.19 = (bf16[512,512]{1,0:T(8,128)(2,1)S(1)}, bf16[512,512]{1,0:T(8,128)(2,1)}, u32[]{:S(2)}) copy-start(bf16[512,512]{1,0:T(8,128)(2,1)} %refs_4_.1) | copy-start | bytes 1572868
  9.3 27.7 %copy-start.28 = (s32[1,2]{1,0:T(1,128)S(1)}, s32[1,2]{1,0:T(1,128)}, u32[]{:S(2)}) copy-start(s32[1,2]{1,0:T(1,128)} %refs_0_.7) | copy-start | bytes 28
  31.1 17.3 %copy-start.30 = (f32[512]{0:T(512)S(1)}, f32[512]{0:T(512)}, u32[]{:S(2)}) copy-start(f32[512]{0:T(512)} %param.19) | copy-start | bytes 6148
  32.6 0.8 copy-start.9
  33.4 15.0 %all-to-all-start.1 = ((bf16[8,3,64,128]{3,2,1,0:T(8,128)(2,1)}), bf16[8,3,64,128]{3,2,1,0:T(8,128)(2,1)S(1)}, u32[]{:S(2)}, u32[]{:S(2)}) async-start(bf16[8,3,64,128]{3,2,1,0:T(8,128)(2,1)} %chain.1), calls=%async_computation.1 | async-start | bytes 786432 | tf_op jit(solution)/shard_map/all_to_all | solution.py:328
  40.1 1.0 copy-start.13
  48.4 1.0 copy-start.7
  49.4 1.2 %copy-start.14 = (f32[512,512]{1,0:T(8,128)S(1)}, f32[512,512]{1,0:T(8,128)}, u32[]{:S(2)}) copy-start(f32[512,512]{1,0:T(8,128)} %copy-done.13) | copy-start | bytes 3145732
  50.6 39.4 %copy-start.1 = (bf16[1024,512]{1,0:T(8,128)(2,1)S(1)}, bf16[1024,512]{1,0:T(8,128)(2,1)}, u32[]{:S(2)}) copy-start(bf16[1024,512]{1,0:T(8,128)(2,1)} %g.5) | copy-start | bytes 3145732
  50.6 39.4 %copy-start.3 = (bf16[1024,512]{1,0:T(8,128)(2,1)S(1)}, bf16[1024,512]{1,0:T(8,128)(2,1)}, u32[]{:S(2)}) copy-start(bf16[1024,512]{1,0:T(8,128)(2,1)} %k.7) | copy-start | bytes 3145732
  50.6 39.4 %copy-start.5 = (bf16[1024,512]{1,0:T(8,128)(2,1)S(1)}, bf16[1024,512]{1,0:T(8,128)(2,1)}, u32[]{:S(2)}) copy-start(bf16[1024,512]{1,0:T(8,128)(2,1)} %v.7) | copy-start | bytes 3145732
  53.6 1.0 copy-start.21
  54.6 11.8 %copy-start.25 = (bf16[8,2,64,128]{3,2,1,0:T(8,128)(2,1)}, bf16[8,2,64,128]{3,2,1,0:T(8,128)(2,1)S(1)}, u32[]{:S(2)}) copy-start(bf16[8,2,64,128]{3,2,1,0:T(8,128)(2,1)S(1)} %get-tuple-element.25) | copy-start | bytes 786436
  66.4 13.6 %all-to-all-start.3 = ((bf16[8,2,64,128]{3,2,1,0:T(8,128)(2,1)}), bf16[8,2,64,128]{3,2,1,0:T(8,128)(2,1)}, u32[]{:S(2)}, u32[]{:S(2)}) async-start(bf16[8,2,64,128]{3,2,1,0:T(8,128)(2,1)} %copy-done.25), calls=%async_computation.3 | async-start | bytes 524288 | tf_op jit(solution)/shard_map/all_to_all | solution.py:328
  80.0 1.0 copy-start.10
  81.1 0.9 copy-start.23
  82.0 0.7 copy-start.31
  82.6 0.7 copy-start.32
  85.2 0.7 copy-start.24
  85.9 26.5 %all-to-all-start.4 = ((bf16[8,3,64,128]{3,2,1,0:T(8,128)(2,1)}), bf16[8,3,64,128]{3,2,1,0:T(8,128)(2,1)}, u32[]{:S(2)}, u32[]{:S(2)}) async-start(bf16[8,3,64,128]{3,2,1,0:T(8,128)(2,1)} %copy-done.24), calls=%async_computation.4 | async-start | bytes 786432 | tf_op jit(solution)/shard_map/all_to_all | solution.py:328
  90.1 1.2 %copy-start.12 = (bf16[1024,512]{1,0:T(8,128)(2,1)S(1)}, bf16[1024,512]{1,0:T(8,128)(2,1)}, u32[]{:S(2)}) copy-start(bf16[1024,512]{1,0:T(8,128)(2,1)} %q.4) | copy-start | bytes 3145732
  102.4 1.6 %copy-start.15 = (f32[1024,512]{1,0:T(8,128)S(1)}, f32[1024,512]{1,0:T(8,128)}, u32[]{:S(2)}) copy-start(f32[1024,512]{1,0:T(8,128)} %get-tuple-element.21.part) | copy-start | bytes 6291460
  104.0 3.0 %copy-start.8 = (bf16[512,512]{1,0:T(8,128)(2,1)S(1)}, bf16[512,512]{1,0:T(8,128)(2,1)}, u32[]{:S(2)}) copy-start(bf16[512,512]{1,0:T(8,128)(2,1)} %refs_2_.1) | copy-start | bytes 1572868
  104.0 3.0 %copy-start.18 = (bf16[512,512]{1,0:T(8,128)(2,1)S(1)}, bf16[512,512]{1,0:T(8,128)(2,1)}, u32[]{:S(2)}) copy-start(bf16[512,512]{1,0:T(8,128)(2,1)} %refs_3_.1) | copy-start | bytes 1572868
  104.0 3.0 %copy-start.20 = (bf16[512,512]{1,0:T(8,128)(2,1)S(1)}, bf16[512,512]{1,0:T(8,128)(2,1)}, u32[]{:S(2)}) copy-start(bf16[512,512]{1,0:T(8,128)(2,1)} %refs_4_.1) | copy-start | bytes 1572868
  104.0 3.0 %copy-start.22 = (f32[512,512]{1,0:T(8,128)S(1)}, f32[512,512]{1,0:T(8,128)}, u32[]{:S(2)}) copy-start(f32[512,512]{1,0:T(8,128)} %copy-done.21) | copy-start | bytes 3145732
  112.4 1.6 %copy-start.16 = (f32[1024,512]{1,0:T(8,128)S(1)}, f32[1024,512]{1,0:T(8,128)}, u32[]{:S(2)}) copy-start(f32[1024,512]{1,0:T(8,128)} %get-tuple-element.22.dk_part) | copy-start | bytes 6291460

commit v3 on v2

--- a/solution.py
+++ b/solution.py
@@ -16,6 +16,9 @@
 bf16 = jnp.bfloat16
 SMEM = pl.BlockSpec(memory_space=pltpu.SMEM)
 VMEM = pl.BlockSpec(memory_space=pltpu.VMEM)
+ANY = pl.BlockSpec(memory_space=pl.ANY)
+SCORE_ROWS = 16
+SCORE_PARTS = 3
 
 
 def dot(a, b, ca, cb):
@@ -25,7 +28,7 @@
 def call(body, **kw):
     return pl.pallas_call(
         body,
-        compiler_params=pltpu.CompilerParams(vmem_limit_bytes=48 * 1024 * 1024),
+        compiler_params=pltpu.CompilerParams(vmem_limit_bytes=24 * 1024 * 1024),
         **kw,
     )
 
@@ -73,28 +76,47 @@
         out[o, place] = mat[o * rows : (o + 1) * rows].astype(bf16)
 
 
-def load_matrix(ref, place):
-    return jnp.concatenate([ref[o, place] for o in range(ref.shape[0])], axis=0)
-
-
-def sums_kernel(ends, q, k, v, g, out):
-    width = q.shape[0]
+def load_matrix(ref, place, h=0, share=None):
+    share = ref.shape[0] if share is None else share
+    return jnp.concatenate([ref[h * share + o, place] for o in range(share)], axis=0)
+
+
+def sums_kernel(ends, q_in, k_in, v_in, g_in, out, q, k, v, g, sems):
+    width, flat = q.shape
+    heads = flat // E
+    share = out.shape[0] // heads
+    columns = [pl.ds(h * E, E) for h in range(heads)]
+    copies = [
+        [
+            pltpu.make_async_copy(a.at[:, columns[h]], b.at[:, columns[h]], sems.at[h, i])
+            for i, (a, b) in enumerate(((k_in, k), (v_in, v), (q_in, q), (g_in, g)))
+        ]
+        for h in range(heads)
+    ]
+    for group in copies:
+        for c in group:
+            c.start()
     bounds = slab_bounds(ends, lax.axis_index("seq"), width)
     scaling = 1.0 / math.sqrt(E * width)
     rows = rows_of((width, E))
     zero = jnp.zeros((width, E), f32)
-    values = v[...].astype(f32)
-    pieces = []
-    low = 0
-    for b in bounds + [width]:
-        inside = jnp.logical_and(rows >= low, rows < b)
-        pieces.append(jnp.where(inside, values, zero).astype(bf16))
-        low = b
-    sums = dot(k[...], jnp.concatenate(pieces, axis=1), 0, 0)
-    for m in range(PIECES):
-        store_parts(out, m, sums[:, m * E : (m + 1) * E])
-    first = jnp.where(rows < bounds[0], g[...].astype(f32), zero).astype(bf16)
-    store_parts(out, PIECES, scaling * dot(q[...], first, 0, 0))
+    for h in range(heads):
+        for c in copies[h]:
+            c.wait()
+        at = slice(h * E, (h + 1) * E)
+        values = v[:, at].astype(f32)
+        pieces = []
+        low = 0
+        for b in bounds + [width]:
+            inside = jnp.logical_and(rows >= low, rows < b)
+            pieces.append(jnp.where(inside, values, zero).astype(bf16))
+            low = b
+        sums = dot(k[:, at], jnp.concatenate(pieces, axis=1), 0, 0)
+        mine = out.at[pl.ds(h * share, share)]
+        for m in range(PIECES):
+            store_parts(mine, m, sums[:, m * E : (m + 1) * E])
+        first = jnp.where(rows < bounds[0], g[:, at].astype(f32), zero).astype(bf16)
+        store_parts(mine, PIECES, scaling * dot(q[:, at], first, 0, 0))
 
 
 def chain_kernel(ends, cand_prompt, parts, out, held, *, width):
@@ -144,45 +166,83 @@
     return bounds
 
 
-def scores_kernel(lengths, q, inside, readout, states, slope_out, raw_out, grads_out, *, scaling):
-    h = pl.program_id(0)
-    width = q.shape[0]
+def scores_kernel(lengths, q, inside, readout, states, slope_out, raw_out, slope_far, sems, *, scaling):
+    width, flat = q.shape
+    heads = flat // E
     per_slab = lengths.shape[1]
     bounds = cand_bounds(lengths)
     rows = rows_of((width, E))
-    wide = jnp.concatenate([load_matrix(states, j) for j in range(per_slab)], axis=1)
-    crossed = dot(q[...], wide, 1, 0)
-    crossed = pick_rows(rows, bounds, [crossed[:, j * E : (j + 1) * E] for j in range(per_slab)])
-    out = scaling * (inside[...] + crossed)
+    zero = jnp.zeros((width, E), f32)
     inverse = [1.0 / jnp.full((1, E), lengths[0, j], jnp.int32).astype(f32) for j in range(per_slab)]
-    weight = pick_rows(rows, bounds, inverse) * readout[...]
-    sigma = jax.nn.sigmoid(out)
-    silu = out * sigma * weight
-    slope = weight * sigma * (1.0 + out * (1.0 - sigma))
-    slope_out[...] = slope
+    totals = [jnp.zeros((1, E), f32) for j in range(per_slab)]
+    copies = []
+    for h in range(heads):
+        at = slice(h * E, (h + 1) * E)
+        wide = [load_matrix(states, j, h, states.shape[0] // heads) for j in range(per_slab)]
+        crossed = dot(q[:, at], jnp.concatenate(wide, axis=1), 1, 0)
+        crossed = pick_rows(rows, bounds, [crossed[:, j * E : (j + 1) * E] for j in range(per_slab)])
+        out = scaling * (inside[:, at] + crossed)
+        weight = pick_rows(rows, bounds, inverse) * readout[:, at]
+        sigma = jax.nn.sigmoid(out)
+        slope_out[:, at] = weight * sigma * (1.0 + out * (1.0 - sigma))
+        columns = pl.ds(h * E, E)
+        copies.append(pltpu.make_async_copy(slope_out.at[:, columns], slope_far.at[:, columns], sems.at[h]))
+        copies[-1].start()
+        silu = out * sigma * weight
+        low = 0
+        for j, b in enumerate(bounds + [width]):
+            mine = jnp.logical_and(rows >= low, rows < b)
+            totals[j] += jnp.sum(jnp.where(mine, silu, zero), axis=0, keepdims=True)
+            low = b
+    raw_out[...] = jnp.zeros_like(raw_out)
+    for j in range(per_slab):
+        raw_out[j : j + 1] = jnp.broadcast_to(jnp.sum(totals[j], axis=1, keepdims=True), (1, E))
+    for c in copies:
+        c.wait()
+
+
+def grads_kernel(lengths, q, slope, *refs, scaling):
+    raws, out = refs[:-1], refs[-1]
+    width, flat = q.shape
+    heads = flat // E
+    count = out.shape[0]
+    share = count // heads
+    size = flat // count
+    per_slab = lengths.shape[1]
+    bounds = cand_bounds(lengths)
+    rows = rows_of((width, E))
     zero = jnp.zeros((width, E), f32)
-    masked = []
-    totals = []
-    low = 0
-    for b in bounds + [width]:
-        mine = jnp.logical_and(rows >= low, rows < b)
-        masked.append(jnp.where(mine, slope, zero).astype(bf16))
-        column = jnp.sum(jnp.where(mine, silu, zero), axis=0, keepdims=True)
-        totals.append(jnp.broadcast_to(jnp.sum(column, axis=1, keepdims=True), (1, E)))
-        low = b
-    grads = scaling * dot(q[...], jnp.concatenate(masked, axis=1), 0, 0)
+    for h in range(heads):
+        at = slice(h * E, (h + 1) * E)
+        mine = slope[:, at]
+        high, low_part = [], []
+        low = 0
+        for b in bounds + [width]:
+            kept = jnp.where(jnp.logical_and(rows >= low, rows < b), mine, zero)
+            top = kept.astype(bf16)
+            high.append(top)
+            low_part.append((kept - top.astype(f32)).astype(bf16))
+            low = b
+        grads = dot(q[:, at], jnp.concatenate(high + low_part, axis=1), 0, 0)
+        for j in range(per_slab):
+            grad = grads[:, j * E : (j + 1) * E] + grads[:, (per_slab + j) * E : (per_slab + j + 1) * E]
+            grad = (scaling * grad).astype(bf16)
+            for o in range(share):
+                out[h * share + o, j * size : (j + 1) * size] = grad[o * size : (o + 1) * size]
+    total = raws[0][...]
+    for r in raws[1:]:
+        total += r[...]
+    lines = []
     for j in range(per_slab):
-        store_parts(grads_out, j, grads[:, j * E : (j + 1) * E])
-    spare = jnp.zeros((8 - per_slab, E), f32)
-    tile = jnp.concatenate(totals + [spare], axis=0)
-
-    @pl.when(h == 0)
-    def _():
-        raw_out[...] = jnp.broadcast_to(tile[None], raw_out.shape)
-
-    @pl.when(h > 0)
-    def _():
-        raw_out[...] += jnp.broadcast_to(tile[None], raw_out.shape)
+        left = total[j : j + 1]
+        for i in range(SCORE_PARTS):
+            line = left.astype(bf16).astype(f32)
+            lines.append(line)
+            left = left - line
+    lines.append(jnp.zeros((SCORE_ROWS - len(lines), E), f32))
+    tile = jnp.concatenate(lines, axis=0).astype(bf16)
+    for o in range(count):
+        out[o, per_slab * size :] = tile
 
 
 def listwise_kernel(
@@ -190,7 +250,6 @@
     prompts,
     prompt_row,
     rank_row,
-    raws,
     grads,
     parts,
     out,
@@ -203,24 +262,26 @@
     width,
 ):
     count = grads.shape[0]
-    per_slab = grads.shape[1]
-    groups = raws.shape[0] // count
+    size = parts.shape[2]
+    per_slab = prompts.shape[0] // count
     cands = count * per_slab
     prompt_count = ends.shape[0]
     for e in range(count):
-        total = raws[e * groups, :per_slab]
-        for i in range(1, groups):
-            total += raws[e * groups + i, :per_slab]
-        raw_held[e * per_slab : (e + 1) * per_slab] = total
+        tile = grads[e, per_slab * size :].astype(f32)
+        for j in range(per_slab):
+            total = tile[SCORE_PARTS * j : SCORE_PARTS * j + 1]
+            for i in range(1, SCORE_PARTS):
+                total = total + tile[SCORE_PARTS * j + i : SCORE_PARTS * j + i + 1]
+            raw_held[e * per_slab + j : e * per_slab + j + 1] = total
     raw = raw_held[...]
     square = (cands, cands)
     down = lax.broadcasted_iota(jnp.int32, square, 0)
     across = lax.broadcasted_iota(jnp.int32, square, 1)
     same_spot = down == across
-    own = jnp.broadcast_to(prompt_row[...], square)
+    own = jnp.broadcast_to(prompt_row[...].astype(f32), square)
     own_down = jnp.sum(jnp.where(same_spot, own, 0.0), axis=1, keepdims=True)
     group = own == own_down
-    rank_weight = jnp.broadcast_to(jnp.exp(-rank_row[...]), square)
+    rank_weight = jnp.broadcast_to(jnp.exp(-rank_row[...].astype(f32)), square)
     rank_down = jnp.sum(jnp.where(same_spot, rank_weight, 0.0), axis=1, keepdims=True)
     target = rank_down / jnp.sum(jnp.where(group, rank_weight, 0.0), axis=1, keepdims=True)
     tanh_raw = jnp.tanh(raw)
@@ -237,8 +298,8 @@
         coef_out[j : j + 1] = coef_held[pl.ds(me * per_slab + j, 1)]
     held[...] = jnp.zeros_like(held)
     for c in range(cands):
-        piece = grads[c // per_slab, c % per_slab].astype(f32) * coef[c : c + 1]
-        held[prompts[c]] += piece.astype(bf16).astype(f32)
+        j = c % per_slab
+        held[prompts[c]] += grads[c // per_slab, j * size : (j + 1) * size].astype(f32) * coef[c : c + 1]
     running = jnp.zeros(parts.shape[2:], f32)
     for e in reversed(range(count)):
         start = e * width
@@ -312,16 +373,34 @@
     dq[...] = (scaling * (part[...] + jnp.where(rows < bounds[0], crossed, 0.0))).astype(bf16)
 
 
-def right_kernel(ends, dk_part, dv_part, k, v, states, dk, dv):
-    width = k.shape[0]
+def right_kernel(ends, dk_in, dv_in, k, v, states, dk_out, dv_out, dk_part, dv_part, dk, dv, sems):
+    width, flat = k.shape
+    heads = flat // E
     bounds = slab_bounds(ends, lax.axis_index("seq"), width)
     rows = rows_of((width, E))
-    mats = [load_matrix(states, m) for m in range(PIECES)]
-    by_v = dot(v[...], jnp.concatenate(mats, axis=0), 1, 1)
-    by_k = dot(k[...], jnp.concatenate(mats, axis=1), 1, 0)
     cut = lambda a: [a[:, m * E : (m + 1) * E] for m in range(PIECES)]
-    dk[...] = (dk_part[...] + pick_rows(rows, bounds, cut(by_v))).astype(bf16)
-    dv[...] = (dv_part[...] + pick_rows(rows, bounds, cut(by_k))).astype(bf16)
+    copies = []
+    fetches = []
+    for h in range(heads):
+        columns = pl.ds(h * E, E)
+        for i, (a, b) in enumerate(((dk_in, dk_part), (dv_in, dv_part))):
+            fetches.append(pltpu.make_async_copy(a.at[:, columns], b.at[:, columns], sems.at[h, 2 + i]))
+            fetches[-1].start()
+    for h in range(heads):
+        at = slice(h * E, (h + 1) * E)
+        mats = [load_matrix(states, m, h, states.shape[0] // heads) for m in range(PIECES)]
+        by_v = dot(v[:, at], jnp.concatenate(mats, axis=0), 1, 1)
+        fetches[2 * h].wait()
+        dk[:, at] = (dk_part[:, at] + pick_rows(rows, bounds, cut(by_v))).astype(bf16)
+        by_k = dot(k[:, at], jnp.concatenate(mats, axis=1), 1, 0)
+        fetches[2 * h + 1].wait()
+        dv[:, at] = (dv_part[:, at] + pick_rows(rows, bounds, cut(by_k))).astype(bf16)
+        columns = pl.ds(h * E, E)
+        for i, (a, b) in enumerate(((dk, dk_out), (dv, dv_out))):
+            copies.append(pltpu.make_async_copy(a.at[:, columns], b.at[:, columns], sems.at[h, i]))
+            copies[-1].start()
+    for c in copies:
+        c.wait()
 
 
 def exchange(a):
@@ -360,24 +439,33 @@
     def parts_block(n):
         return pl.BlockSpec((share, n, rows, E), lambda h: (h, 0, 0, 0))
 
+    def hbm(*arrays):
+        return [pltpu.with_memory_space_constraint(a, pltpu.HBM) for a in arrays]
+
+    def near(*arrays):
+        return [pltpu.with_memory_space_constraint(a, pltpu.VMEM) for a in arrays]
+
+    prompt_in = (prompt_q, prompt_k, prompt_v, prompt_grad)
     pieces = call(
         sums_kernel,
-        grid=(heads,),
-        in_specs=[SMEM] + [whole] * 4,
-        out_specs=parts_block(PIECES + 1),
+        in_specs=[SMEM] + [ANY] * 4,
+        out_specs=VMEM,
         out_shape=like((count, PIECES + 1, rows, E), bf16),
+        scratch_shapes=[pltpu.VMEM((width, flat), bf16)] * 4 + [pltpu.SemaphoreType.DMA((heads, 4))],
         name="sums",
-    )(prompt_ends, prompt_q, prompt_k, prompt_v, prompt_grad)
+    )(prompt_ends, *hbm(*prompt_in))
     parts = exchange(pieces)
 
+    pieces, late_in = lax.optimization_barrier((pieces, prompt_in))
     dq_part, dk_part, dv_part = call(
         prompt_kernel,
         grid=(heads,),
         in_specs=[SMEM] + [whole] * 4,
         out_specs=[whole] * 3,
-        out_shape=[like((width, flat), f32)] * 3,
+        out_shape=[pltpu.HBM((width, flat), f32)] * 3,
         name="prompt",
-    )(prompt_ends, prompt_q, prompt_k, prompt_v, prompt_grad)
+    )(prompt_ends, *hbm(*late_in))
+    parts, dq_part, dk_part, dv_part = lax.optimization_barrier((parts, dq_part, dk_part, dv_part))
 
     chained = call(
         lambda *refs: chain_kernel(*refs, width=width),
@@ -389,6 +477,7 @@
     )(prompt_ends, cand_prompt, parts)
     states = exchange(chained)
 
+    chained, cand_in = lax.optimization_barrier((chained, (cand_q, cand_k, cand_v)))
     inside = call(
         inside_kernel,
         grid=(heads,),
@@ -396,45 +485,47 @@
         out_specs=cand_block,
         out_shape=like((cand_width, flat), f32),
         name="inside",
-    )(cand_lengths, cand_q, cand_k, cand_v)
-
-    slope, raw, grads = call(
+    )(cand_lengths, *hbm(*cand_in))
+
+    near_q = near(cand_in[0])[0]
+    slope, raw, slope_far = call(
         lambda *refs: scores_kernel(*refs, scaling=scaling),
-        grid=(heads,),
-        in_specs=[
-            SMEM,
-            cand_block,
-            cand_block,
-            pl.BlockSpec((1, E), lambda h: (0, h)),
-            parts_block(per_slab + 1),
+        in_specs=[SMEM] + [VMEM] * 4,
+        out_specs=[VMEM, VMEM, ANY],
+        out_shape=[
+            pltpu.VMEM((cand_width, flat), f32),
+            like((8, E), f32),
+            pltpu.HBM((cand_width, flat), f32),
         ],
-        out_specs=[
-            cand_block,
-            pl.BlockSpec((count * groups, 8, E), lambda h: (0, 0, 0)),
-            parts_block(per_slab),
-        ],
-        out_shape=[
-            like((cand_width, flat), f32),
-            like((count * groups, 8, E), f32),
-            like((count, per_slab, rows, E), bf16),
-        ],
+        scratch_shapes=[pltpu.SemaphoreType.DMA((heads,))],
         name="scores",
-    )(cand_lengths, cand_q, inside, readout.reshape(1, flat), states)
-    raws = lax.all_to_all(raw, ("seq", "head"), 0, 0, tiled=True)
+    )(cand_lengths, near_q, inside, readout.reshape(1, flat), states)
+    raws = [raw]
+    for step in range(1, groups):
+        raws.append(lax.ppermute(raw, "head", [(i, (i + step) % groups) for i in range(groups)]))
+    grads = call(
+        lambda *refs: grads_kernel(*refs, scaling=scaling),
+        in_specs=[SMEM] + [VMEM] * (2 + groups),
+        out_specs=VMEM,
+        out_shape=like((count, per_slab * rows + SCORE_ROWS, E), bf16),
+        name="grads",
+    )(cand_lengths, near_q, *near(slope), *raws)
     all_grads = exchange(grads)
 
+    grads, late_grad = lax.optimization_barrier((grads, prompt_grad))
     prompt_dq = call(
         query_kernel,
         grid=(heads,),
         in_specs=[SMEM, whole, whole, parts_block(per_slab + 1)],
         out_specs=whole,
-        out_shape=like((width, flat), bf16),
+        out_shape=pltpu.HBM((width, flat), bf16),
         name="query",
-    )(prompt_ends, dq_part, prompt_grad, states)
+    )(prompt_ends, *hbm(dq_part, late_grad), states)
+    all_grads, prompt_dq = lax.optimization_barrier((all_grads, prompt_dq))
 
     right, coef, loss = call(
         lambda *refs: listwise_kernel(*refs, width=width),
-        in_specs=[SMEM, SMEM] + [VMEM] * 5,
+        in_specs=[SMEM, SMEM] + [VMEM] * 4,
         out_specs=[VMEM] * 3,
         out_shape=[
             like((count, PIECES, rows, E), bf16),
@@ -450,9 +541,8 @@
     )(
         prompt_ends,
         cand_prompt,
-        cand_prompt.astype(f32).reshape(1, cands),
-        cand_ranks.astype(f32).reshape(1, cands),
-        raws,
+        cand_prompt.reshape(1, cands),
+        cand_ranks.reshape(1, cands),
         all_grads,
         parts,
     )
@@ -465,18 +555,21 @@
         + [cand_block] * 4
         + [parts_block(per_slab + 1)],
         out_specs=[cand_block] * 3,
-        out_shape=[like((cand_width, flat), bf16)] * 3,
+        out_shape=[pltpu.HBM((cand_width, flat), bf16)] * 3,
         name="cand",
-    )(cand_lengths, coef, cand_q, cand_k, cand_v, slope, states)
+    )(cand_lengths, coef, *hbm(*cand_in, slope_far), states)
+    rights, cand_dq, cand_dk, cand_dv = lax.optimization_barrier((rights, cand_dq, cand_dk, cand_dv))
 
     prompt_dk, prompt_dv = call(
         right_kernel,
-        grid=(heads,),
-        in_specs=[SMEM] + [whole] * 4 + [parts_block(PIECES)],
-        out_specs=[whole] * 2,
-        out_shape=[like((width, flat), bf16)] * 2,
+        in_specs=[SMEM, ANY, ANY] + [VMEM] * 3,
+        out_specs=[ANY] * 2,
+        out_shape=[pltpu.HBM((width, flat), bf16)] * 2,
+        scratch_shapes=[pltpu.VMEM((width, flat), f32)] * 2
+        + [pltpu.VMEM((width, flat), bf16)] * 2
+        + [pltpu.SemaphoreType.DMA((heads, 4))],
         name="right",
-    )(prompt_ends, dk_part, dv_part, prompt_k, prompt_v, rights)
+    )(prompt_ends, *hbm(dk_part, dv_part), *near(prompt_k, prompt_v), rights)
     return (
         prompt_dq,
         prompt_dk,

time: 120 us -> 90.4 us (0.75)
  blocking collectives: 33.5 us -> 0 us
  local copies, waits for them, and re-layouts: 19 us -> 0.68 us
  waiting for transfers between devices: 15.2 us -> 23.9 us
  starting transfers between devices: 11.7 us -> 20.2 us
  Pallas kernels: 37.1 us -> 44 us
  other arithmetic: 1.68 us -> 0 us
    all_to_all x2 -> x0, blocking collectives: 33.5 us -> none  [the longest x1 21.7 us: exchange(): return lax.all_to_all(a, 'seq', 0, 0, tiled=True)]
    unnamed x66 -> x18, local copies, waits for them, and re-layouts: 19 us -> 0.68 us
    all_to_all x3 -> x4, starting transfers between devices: 11.7 us -> 18.4 us  [exchange(): return lax.all_to_all(a, 'seq', 0, 0, tiled=True)]
    all_to_all x3 -> x4, waiting for transfers between devices: 15.2 us -> 21.1 us  [exchange(): return lax.all_to_all(a, 'seq', 0, 0, tiled=True)]
    pallas_call x3 -> x4, Pallas kernels: 11.1 us -> 15.4 us  [the longest x1 6.8 us: per_device(): call(right_kernel, in_specs=[SMEM, ANY, ANY] + [VMEM] * 3, out_specs=[ANY...]
    ppermute x0 -> x3, waiting for transfers between devices: none -> 2.87 us  [per_device(): lax.ppermute(raw, 'head', [(i, (i + step) % groups) for i in range(groups)])]
    ppermute x0 -> x3, starting transfers between devices: none -> 1.82 us  [per_device(): lax.ppermute(raw, 'head', [(i, (i + step) % groups) for i in range(groups)])]
    reshape x2 -> x0, other arithmetic: 1.68 us -> none  [the longest x1 1.17 us: per_device(): cand_ranks.astype(f32).reshape(1, cands)]
  transfers between devices with their start and end apart: 3 -> 7, of which waited for: 2 -> 6; matrix products, arithmetic and copies ran while one was open for 1% -> 0% of each run, Pallas kernels for 19% -> 28%
where the time goes in v3:
time: 90.4 us; the launch traced here: 89.7 us
  Pallas kernels  44 us (49%)
  waiting for transfers between devices  23.9 us (26%)
  starting transfers between devices  20.2 us (22%)
    all_to_all x4, waiting for transfers between devices, exchange(): return lax.all_to_all(a, 'seq', 0, 0, tiled=True)  21.1 us
    all_to_all x4, starting transfers between devices, exchange(): return lax.all_to_all(a, 'seq', 0, 0, tiled=True)  18.4 us
    pallas_call x1, Pallas kernels, per_device(): call(prompt_kernel, grid=(heads,), in_specs=[SMEM] + [whole] * 4, out_spe...  11.3 us
    pallas_call x1, Pallas kernels, per_device(): call(right_kernel, in_specs=[SMEM, ANY, ANY] + [VMEM] * 3, out_specs=[ANY...  6.8 us
    pallas_call x1, Pallas kernels, per_device(): call(lambda *refs: cand_kernel(*refs, scaling=scaling), grid=(heads,), in...  5.94 us
    pallas_call x1, Pallas kernels, per_device(): call(sums_kernel, in_specs=[SMEM] + [ANY] * 4, out_specs=VMEM, out_shape=...  4.41 us
    pallas_call x1, Pallas kernels, per_device(): call(query_kernel, grid=(heads,), in_specs=[SMEM, whole, whole, parts_blo...  4.22 us
    pallas_call x1, Pallas kernels, per_device(): call(inside_kernel, grid=(heads,), in_specs=[SMEM] + [cand_block] * 3, ou...  3.85 us
  transfers between devices with their start and end apart: 7, of which 6 were waited for; matrix products, arithmetic and copies ran while one was open for 0% of the time, Pallas kernels for 28%

profile of v3, /device:TPU:0, one launch (start us, length us, event | category | flops | bytes accessed | tf_op | source)
XLA Modules:
  0.0 89.7 jit_solution(8891697969810472016)
XLA Ops:
  0.6 0.0 copy-start.3
  0.6 0.6 copy-done.3
  1.3 0.0 copy-start.4
  1.3 4.4 %sums.1 = bf16[8,4,64,128]{3,2,1,0:T(8,128)(2,1)} custom-call(s32[8]{0:T(128)S(1)} %copy-done.3, bf16[1024,512]{1,0:T(8,128)(2,1)} %q, bf16[1024,512]{1,0:T(8,128)(2,1)} %k.3, bf16[1024,512]{1,0:T(8,128)(2,1)} %v.3, bf16[1024,512]{1,0:T(8,128)(2,1)} %g.1), custom_call_target="tpu_custom_call" | custom-call | tf_op jit(solution)/shard_map/sums/pallas_call | solution.py:449
  5.7 7.3 %all-to-all-start = ((bf16[8,4,64,128]{3,2,1,0:T(8,128)(2,1)}), bf16[8,4,64,128]{3,2,1,0:T(8,128)(2,1)S(1)}, u32[]{:S(2)}, u32[]{:S(2)}) async-start(bf16[8,4,64,128]{3,2,1,0:T(8,128)(2,1)} %sums.1), calls=%async_computation | async-start | bytes 1048576 | tf_op jit(solution)/shard_map/all_to_all | solution.py:407
  13.0 0.0 copy-done.4
  13.0 0.0 copy-start.6
  13.0 0.0 copy-start.5
  13.0 11.3 %prompt.1 = (f32[1024,512]{1,0:T(8,128)}, f32[1024,512]{1,0:T(8,128)}, f32[1024,512]{1,0:T(8,128)}) custom-call(s32[8]{0:T(128)S(1)} %copy-done.4, bf16[1024,512]{1,0:T(8,128)(2,1)} %q, bf16[1024,512]{1,0:T(8,128)(2,1)} %k.3, bf16[1024,512]{1,0:T(8,128)(2,1)} %v.3, bf16[1024,512]{1,0:T(8,128)(2,1)} %g.1), custom_call_target="tpu_custom_call" | custom-call | tf_op jit(solution)/shard_map/prompt/pallas_call | solution.py:460
  24.3 3.1 %all-to-all-done.refs_2_.refs_5_ = bf16[8,4,64,128]{3,2,1,0:T(8,128)(2,1)S(1)} async-done(((bf16[8,4,64,128]{3,2,1,0:T(8,128)(2,1)}), bf16[8,4,64,128]{3,2,1,0:T(8,128)(2,1)S(1)}, u32[]{:S(2)}, u32[]{:S(2)}) %all-to-all-start) | async-done | bytes 524320 | tf_op jit(solution)/shard_map/all_to_all | solution.py:407
  27.5 0.0 copy-done.6
  27.5 0.0 copy-start.2
  27.5 0.0 copy-start.7
  27.5 1.5 %chain.1 = bf16[8,3,64,128]{3,2,1,0:T(8,128)(2,1)} custom-call(s32[8]{0:T(128)S(1)} %copy-done.4, s32[16]{0:T(128)S(1)} %copy-done.6, bf16[8,4,64,128]{3,2,1,0:T(8,128)(2,1)S(1)} %all-to-all-done.refs_2_.refs_5_), custom_call_target="tpu_custom_call" | custom-call | tf_op jit(solution)/shard_map/chain/pallas_call | solution.py:470
  29.0 3.6 %all-to-all-start.1 = ((bf16[8,3,64,128]{3,2,1,0:T(8,128)(2,1)}), bf16[8,3,64,128]{3,2,1,0:T(8,128)(2,1)S(1)}, u32[]{:S(2)}, u32[]{:S(2)}) async-start(bf16[8,3,64,128]{3,2,1,0:T(8,128)(2,1)} %chain.1), calls=%async_computation.1 | async-start | bytes 786432 | tf_op jit(solution)/shard_map/all_to_all | solution.py:407
  32.6 0.0 copy-done.5
  32.6 3.9 %inside.1.refs_2_ = f32[512,512]{1,0:T(8,128)S(1)} custom-call(s32[1,2]{1,0:T(1,128)S(1)} %copy-done.5, bf16[512,512]{1,0:T(8,128)(2,1)} %refs_2_, bf16[512,512]{1,0:T(8,128)(2,1)} %refs_3_, bf16[512,512]{1,0:T(8,128)(2,1)} %refs_4_), custom_call_target="tpu_custom_call" | custom-call | tf_op jit(solution)/shard_map/inside/pallas_call | solution.py:481
  36.5 8.0 %all-to-all-done.1.refs_4_.states.refs_6_ = bf16[8,3,64,128]{3,2,1,0:T(8,128)(2,1)S(1)} async-done(((bf16[8,3,64,128]{3,2,1,0:T(8,128)(2,1)}), bf16[8,3,64,128]{3,2,1,0:T(8,128)(2,1)S(1)}, u32[]{:S(2)}, u32[]{:S(2)}) %all-to-all-start.1) | async-done | bytes 393248 | tf_op jit(solution)/shard_map/all_to_all | solution.py:407
  44.5 0.0 copy-done.2
  44.5 0.0 copy-done.7
  44.5 2.3 %scores.1 = (f32[512,512]{1,0:T(8,128)S(1)}, f32[8,128]{1,0:T(8,128)S(1)}, f32[512,512]{1,0:T(8,128)}) custom-call(s32[1,2]{1,0:T(1,128)S(1)} %copy-done.5, bf16[512,512]{1,0:T(8,128)(2,1)S(1)} %copy-done.2, f32[512,512]{1,0:T(8,128)S(1)} %inside.1.refs_2_, f32[1,512]{1,0:T(1,128)S(1)} %bitcast.6, ...), custom_call_target="tpu_custom_call" | custom-call | tf_op jit(solution)/shard_map/scores/pallas_call | solution.py:491
  46.8 0.1 collective-permute-start.2
  46.9 1.6 %collective-permute-start.1 = (f32[8,128]{1,0:T(8,128)S(1)}, f32[8,128]{1,0:T(8,128)S(1)}, u32[]{:S(2)}, u32[]{:S(2)}) collective-permute-start(f32[8,128]{1,0:T(8,128)S(1)} %get-tuple-element.51.refs_3_), channel_id=1, source_target_pairs={{0,2},{1,3},{2,0},{3,1},{4,6},{5,7},{6,4},{7,5},{8,10},{9,11},{10,... | collective-permute-start | bytes 12296 | tf_op jit(solution)/shard_map/ppermute | solution.py:505
  48.5 0.2 collective-permute-start
  48.6 0.0 collective-permute-done.2.refs_6_
  48.6 1.9 %collective-permute-done.1.refs_5_ = f32[8,128]{1,0:T(8,128)S(1)} collective-permute-done((f32[8,128]{1,0:T(8,128)S(1)}, f32[8,128]{1,0:T(8,128)S(1)}, u32[]{:S(2)}, u32[]{:S(2)}) %collective-permute-start.1) | collective-permute-done | bytes 4128 | tf_op jit(solution)/shard_map/ppermute | solution.py:505
  50.5 1.0 %collective-permute-done.refs_4_ = f32[8,128]{1,0:T(8,128)S(1)} collective-permute-done((f32[8,128]{1,0:T(8,128)S(1)}, f32[8,128]{1,0:T(8,128)S(1)}, u32[]{:S(2)}, u32[]{:S(2)}) %collective-permute-start) | collective-permute-done | bytes 4128 | tf_op jit(solution)/shard_map/ppermute | solution.py:505
  51.5 1.9 %grads.1 = bf16[8,144,128]{2,1,0:T(8,128)(2,1)} custom-call(s32[1,2]{1,0:T(1,128)S(1)} %copy-done.5, bf16[512,512]{1,0:T(8,128)(2,1)S(1)} %copy-done.2, f32[512,512]{1,0:T(8,128)S(1)} %get-tuple-element.50.refs_2_, f32[8,128]{1,0:T(8,128)S(1)} %get-tuple-element.51.refs_3_, f32[8,128]{1,0:T(8,128)S(1)} %collective-permute-done.refs_4_, ...), custom_call_target="tpu_custom_call" | custom-call | tf_op jit(solution)/shard_map/grads/pallas_call | solution.py:506
  53.4 3.7 %all-to-all-start.2 = ((bf16[8,144,128]{2,1,0:T(8,128)(2,1)}), bf16[8,144,128]{2,1,0:T(8,128)(2,1)S(1)}, u32[]{:S(2)}, u32[]{:S(2)}) async-start(bf16[8,144,128]{2,1,0:T(8,128)(2,1)} %grads.1), calls=%async_computation.2 | async-start | bytes 589824 | tf_op jit(solution)/shard_map/all_to_all | solution.py:407
  57.1 0.0 copy-start.8
  57.1 4.2 %query.1 = bf16[1024,512]{1,0:T(8,128)(2,1)} custom-call(s32[8]{0:T(128)S(1)} %copy-done.4, f32[1024,512]{1,0:T(8,128)} %get-tuple-element.52.part, bf16[1024,512]{1,0:T(8,128)(2,1)} %g.1, bf16[8,3,64,128]{3,2,1,0:T(8,128)(2,1)S(1)} %all-to-all-done.1.refs_4_.states.refs_6_), custom_call_target="tpu_custom_call" | custom-call | tf_op jit(solution)/shard_map/query/pallas_call | solution.py:516
  61.3 4.8 %all-to-all-done.2.refs_4_ = bf16[8,144,128]{2,1,0:T(8,128)(2,1)S(1)} async-done(((bf16[8,144,128]{2,1,0:T(8,128)(2,1)}), bf16[8,144,128]{2,1,0:T(8,128)(2,1)S(1)}, u32[]{:S(2)}, u32[]{:S(2)}) %all-to-all-start.2) | async-done | bytes 294944 | tf_op jit(solution)/shard_map/all_to_all | solution.py:407
  66.1 0.0 copy-done.8
  66.1 1.7 %listwise.1 = (bf16[8,3,64,128]{3,2,1,0:T(8,128)(2,1)}, f32[8,128]{1,0:T(8,128)S(1)}, f32[1,128]{1,0:T(1,128)}) custom-call(s32[8]{0:T(128)S(1)} %copy-done.4, s32[16]{0:T(128)S(1)} %copy-done.6, s32[1,16]{1,0:T(1,128)S(1)} %bitcast.5, s32[1,16]{1,0:T(1,128)S(1)} %bitcast.7, bf16[8,144,128]{2,1,0:T(8,128)(2,1)S(1)} %all-to-all-done.2.refs_4_, ...), custom_call_target="tpu_custom_call" | custom-call | tf_op jit(solution)/shard_map/listwise/pallas_call | solution.py:526
  67.8 0.0 copy-start
  67.8 0.0 copy-start.1
  67.8 3.8 %all-to-all-start.3 = ((bf16[8,3,64,128]{3,2,1,0:T(8,128)(2,1)}), bf16[8,3,64,128]{3,2,1,0:T(8,128)(2,1)S(1)}, u32[]{:S(2)}, u32[]{:S(2)}) async-start(bf16[8,3,64,128]{3,2,1,0:T(8,128)(2,1)} %get-tuple-element.58), calls=%async_computation.3 | async-start | bytes 786432 | tf_op jit(solution)/shard_map/all_to_all | solution.py:407
  71.6 5.9 %cand.1 = (bf16[512,512]{1,0:T(8,128)(2,1)}, bf16[512,512]{1,0:T(8,128)(2,1)}, bf16[512,512]{1,0:T(8,128)(2,1)}) custom-call(s32[1,2]{1,0:T(1,128)S(1)} %copy-done.5, f32[8,128]{1,0:T(8,128)S(1)} %get-tuple-element.59.refs_1_, bf16[512,512]{1,0:T(8,128)(2,1)} %refs_2_, bf16[512,512]{1,0:T(8,128)(2,1)} %refs_3_, bf16[512,512]{1,0:T(8,128)(2,1)} %refs_4_, ...), custom_call_target="tpu_custom_call" | custom-call | tf_op jit(solution)/shard_map/cand/pallas_call | solution.py:551
  77.6 5.2 %all-to-all-done.3.states = bf16[8,3,64,128]{3,2,1,0:T(8,128)(2,1)S(1)} async-done(((bf16[8,3,64,128]{3,2,1,0:T(8,128)(2,1)}), bf16[8,3,64,128]{3,2,1,0:T(8,128)(2,1)S(1)}, u32[]{:S(2)}, u32[]{:S(2)}) %all-to-all-start.3) | async-done | bytes 393248 | tf_op jit(solution)/shard_map/all_to_all | solution.py:407
  82.7 0.0 copy-done
  82.7 0.0 copy-done.1
  82.7 6.8 %right.1 = (bf16[1024,512]{1,0:T(8,128)(2,1)}, bf16[1024,512]{1,0:T(8,128)(2,1)}) custom-call(s32[8]{0:T(128)S(1)} %copy-done.4, f32[1024,512]{1,0:T(8,128)} %get-tuple-element.55.dk_in, f32[1024,512]{1,0:T(8,128)} %get-tuple-element.56.dv_in, bf16[1024,512]{1,0:T(8,128)(2,1)S(1)} %copy-done, bf16[1024,512]{1,0:T(8,128)(2,1)S(1)} %copy-done.1, ...), custom_call_target="tpu_custom_call" | custom-call | tf_op jit(solution)/shard_map/right/pallas_call | solution.py:563
Async XLA Ops:
  0.6 0.7 copy-start.3
  1.3 11.7 %copy-start.4 = (s32[8]{0:T(128)S(1)}, s32[8]{0:T(128)}, u32[]{:S(2)}) copy-start(s32[8]{0:T(128)} %ends.7) | copy-start | bytes 100
  5.7 21.7 %all-to-all-start = ((bf16[8,4,64,128]{3,2,1,0:T(8,128)(2,1)}), bf16[8,4,64,128]{3,2,1,0:T(8,128)(2,1)S(1)}, u32[]{:S(2)}, u32[]{:S(2)}) async-start(bf16[8,4,64,128]{3,2,1,0:T(8,128)(2,1)} %sums.1), calls=%async_computation | async-start | bytes 1048576 | tf_op jit(solution)/shard_map/all_to_all | solution.py:407
  13.0 14.5 %copy-start.6 = (s32[16]{0:T(128)S(1)}, s32[16]{0:T(128)}, u32[]{:S(2)}) copy-start(s32[16]{0:T(128)} %refs_1_.5) | copy-start | bytes 196
  13.0 19.6 %copy-start.5 = (s32[1,2]{1,0:T(1,128)S(1)}, s32[1,2]{1,0:T(1,128)}, u32[]{:S(2)}) copy-start(s32[1,2]{1,0:T(1,128)} %refs_0_.9) | copy-start | bytes 28
  27.5 17.0 %copy-start.2 = (bf16[512,512]{1,0:T(8,128)(2,1)S(1)}, bf16[512,512]{1,0:T(8,128)(2,1)}, u32[]{:S(2)}) copy-start(bf16[512,512]{1,0:T(8,128)(2,1)} %refs_2_) | copy-start | bytes 1572868
  27.5 17.0 %copy-start.7 = (f32[512]{0:T(512)S(1)}, f32[512]{0:T(512)}, u32[]{:S(2)}) copy-start(f32[512]{0:T(512)} %param.19) | copy-start | bytes 6148
  29.0 15.5 %all-to-all-start.1 = ((bf16[8,3,64,128]{3,2,1,0:T(8,128)(2,1)}), bf16[8,3,64,128]{3,2,1,0:T(8,128)(2,1)S(1)}, u32[]{:S(2)}, u32[]{:S(2)}) async-start(bf16[8,3,64,128]{3,2,1,0:T(8,128)(2,1)} %chain.1), calls=%async_computation.1 | async-start | bytes 786432 | tf_op jit(solution)/shard_map/all_to_all | solution.py:407
  46.8 1.8 %collective-permute-start.2 = (f32[8,128]{1,0:T(8,128)S(1)}, f32[8,128]{1,0:T(8,128)S(1)}, u32[]{:S(2)}, u32[]{:S(2)}) collective-permute-start(f32[8,128]{1,0:T(8,128)S(1)} %get-tuple-element.51.refs_3_), channel_id=1, source_target_pairs={{0,3},{1,0},{2,1},{3,2},{4,7},{5,4},{6,5},{7,6},{8,11},{9,8},{10,9... | collective-permute-start | bytes 12296 | tf_op jit(solution)/shard_map/ppermute | solution.py:505
  46.9 3.7 %collective-permute-start.1 = (f32[8,128]{1,0:T(8,128)S(1)}, f32[8,128]{1,0:T(8,128)S(1)}, u32[]{:S(2)}, u32[]{:S(2)}) collective-permute-start(f32[8,128]{1,0:T(8,128)S(1)} %get-tuple-element.51.refs_3_), channel_id=1, source_target_pairs={{0,2},{1,3},{2,0},{3,1},{4,6},{5,7},{6,4},{7,5},{8,10},{9,11},{10,... | collective-permute-start | bytes 12296 | tf_op jit(solution)/shard_map/ppermute | solution.py:505
  48.5 3.0 %collective-permute-start = (f32[8,128]{1,0:T(8,128)S(1)}, f32[8,128]{1,0:T(8,128)S(1)}, u32[]{:S(2)}, u32[]{:S(2)}) collective-permute-start(f32[8,128]{1,0:T(8,128)S(1)} %get-tuple-element.51.refs_3_), channel_id=1, source_target_pairs={{0,1},{1,2},{2,3},{3,0},{4,5},{5,6},{6,7},{7,4},{8,9},{9,10},{10,1... | collective-permute-start | bytes 12296 | tf_op jit(solution)/shard_map/ppermute | solution.py:505
  53.4 12.7 %all-to-all-start.2 = ((bf16[8,144,128]{2,1,0:T(8,128)(2,1)}), bf16[8,144,128]{2,1,0:T(8,128)(2,1)S(1)}, u32[]{:S(2)}, u32[]{:S(2)}) async-start(bf16[8,144,128]{2,1,0:T(8,128)(2,1)} %grads.1), calls=%async_computation.2 | async-start | bytes 589824 | tf_op jit(solution)/shard_map/all_to_all | solution.py:407
  57.1 9.0 %copy-start.8 = (s32[16]{0:T(128)S(1)}, s32[16]{0:T(128)}, u32[]{:S(2)}) copy-start(s32[16]{0:T(128)} %param.23) | copy-start | bytes 196
  67.8 14.9 %copy-start = (bf16[1024,512]{1,0:T(8,128)(2,1)S(1)}, bf16[1024,512]{1,0:T(8,128)(2,1)}, u32[]{:S(2)}) copy-start(bf16[1024,512]{1,0:T(8,128)(2,1)} %k.3) | copy-start | bytes 3145732
  67.8 14.9 %copy-start.1 = (bf16[1024,512]{1,0:T(8,128)(2,1)S(1)}, bf16[1024,512]{1,0:T(8,128)(2,1)}, u32[]{:S(2)}) copy-start(bf16[1024,512]{1,0:T(8,128)(2,1)} %v.3) | copy-start | bytes 3145732
  67.8 14.9 %all-to-all-start.3 = ((bf16[8,3,64,128]{3,2,1,0:T(8,128)(2,1)}), bf16[8,3,64,128]{3,2,1,0:T(8,128)(2,1)S(1)}, u32[]{:S(2)}, u32[]{:S(2)}) async-start(bf16[8,3,64,128]{3,2,1,0:T(8,128)(2,1)} %get-tuple-element.58), calls=%async_computation.3 | async-start | bytes 786432 | tf_op jit(solution)/shard_map/all_to_all | solution.py:407

commit v4 on v3

--- a/solution.py
+++ b/solution.py
@@ -81,7 +81,7 @@
     return jnp.concatenate([ref[h * share + o, place] for o in range(share)], axis=0)
 
 
-def sums_kernel(ends, q_in, k_in, v_in, g_in, out, q, k, v, g, sems):
+def sums_kernel(ends, q_in, k_in, v_in, g_in, out, both_out, q, k, v, g, sems):
     width, flat = q.shape
     heads = flat // E
     share = out.shape[0] // heads
@@ -116,7 +116,12 @@
         for m in range(PIECES):
             store_parts(mine, m, sums[:, m * E : (m + 1) * E])
         first = jnp.where(rows < bounds[0], g[:, at].astype(f32), zero).astype(bf16)
-        store_parts(mine, PIECES, scaling * dot(q[:, at], first, 0, 0))
+        both_out[1, h] = (scaling * dot(q[:, at], first, 0, 0)).astype(bf16)
+        cuts = [sums[:, m * E : (m + 1) * E] for m in range(PIECES)]
+        final = cuts[0]
+        for b, piece in zip(bounds, cuts[1:]):
+            final = jnp.where(b < width, piece, final)
+        both_out[0, h] = final.astype(bf16)
 
 
 def chain_kernel(ends, cand_prompt, parts, out, held, *, width):
@@ -131,7 +136,6 @@
         if e > 0:
             begins = jnp.logical_and(first > 0, begins)
         incoming = jnp.where(begins, 0.0, running)
-        out[e, per_slab] = incoming.astype(bf16)
         firsts = parts[e, 0].astype(f32) + incoming
         second = parts[e, 1].astype(f32)
         third = parts[e, 2].astype(f32)
@@ -251,7 +255,6 @@
     prompt_row,
     rank_row,
     grads,
-    parts,
     out,
     coef_out,
     loss_out,
@@ -262,7 +265,7 @@
     width,
 ):
     count = grads.shape[0]
-    size = parts.shape[2]
+    size = held.shape[1]
     per_slab = prompts.shape[0] // count
     cands = count * per_slab
     prompt_count = ends.shape[0]
@@ -300,23 +303,19 @@
     for c in range(cands):
         j = c % per_slab
         held[prompts[c]] += grads[c // per_slab, j * size : (j + 1) * size].astype(f32) * coef[c : c + 1]
-    running = jnp.zeros(parts.shape[2:], f32)
-    for e in reversed(range(count)):
+    nothing = jnp.zeros((size, E), f32)
+    for e in range(count):
         start = e * width
         far = start + width
         first = count_ends(ends, start)
         last = count_ends(ends, far - 1)
-        goes_on = ends[last] != far
-        from_right = jnp.where(goes_on, running, 0.0)
-        from_right_bf = from_right.astype(bf16)
+        open_grad = jnp.where(ends[last] != far, held[last], nothing).astype(bf16)
         for m in range(ENDS):
             pid = first + m
             ended = end_of(ends, pid, far + 1) <= far
-            here = held[jnp.minimum(pid, prompt_count - 1)]
-            out[e, m] = jnp.where(ended, here, from_right).astype(bf16)
-            if m == 0:
-                running = parts[e, PIECES].astype(f32) + jnp.where(ended, here, running)
-        out[e, ENDS] = from_right_bf
+            here = held[jnp.minimum(pid, prompt_count - 1)].astype(bf16)
+            out[e, m] = jnp.where(ended, here, open_grad)
+        out[e, ENDS] = open_grad
 
 
 def cand_kernel(lengths, coef, q, k, v, slope, states, dq, dk, dv, *, scaling):
@@ -363,22 +362,30 @@
             dq[lo:] += part
 
 
-def query_kernel(ends, part, g, states, dq):
+def query_kernel(ends, part, g, tails, firsts, dq, later):
     width = g.shape[0]
     scaling = 1.0 / math.sqrt(E * width)
-    bounds = slab_bounds(ends, lax.axis_index("seq"), width)
-    carry = load_matrix(states, states.shape[1] - 1)
-    crossed = dot(g[...], carry, 1, 1)
+    me = lax.axis_index("seq")
+    bounds = slab_bounds(ends, me, width)
+    first = count_ends(ends, me * width)
+    last = count_ends(ends, me * width + width - 1)
+    carry = jnp.zeros((E, E), f32)
+    ahead = jnp.zeros((E, E), f32)
+    for e in range(tails.shape[0]):
+        before = jnp.logical_and(e < me, count_ends(ends, e * width + width - 1) == first)
+        carry += jnp.where(before, tails[e, 0, 0].astype(f32), 0.0)
+        after = jnp.logical_and(e > me, count_ends(ends, e * width) == last)
+        ahead += jnp.where(after, firsts[e, 0, 0].astype(f32), 0.0)
+    later[0] = ahead
+    crossed = dot(g[...], carry.astype(bf16), 1, 1)
     rows = rows_of((width, E))
     dq[...] = (scaling * (part[...] + jnp.where(rows < bounds[0], crossed, 0.0))).astype(bf16)
 
 
-def right_kernel(ends, dk_in, dv_in, k, v, states, dk_out, dv_out, dk_part, dv_part, dk, dv, sems):
+def right_kernel(ends, dk_in, dv_in, k, v, later, states, dk_out, dv_out, dk_part, dv_part, dk, dv, mats, total, sems):
     width, flat = k.shape
     heads = flat // E
     bounds = slab_bounds(ends, lax.axis_index("seq"), width)
-    rows = rows_of((width, E))
-    cut = lambda a: [a[:, m * E : (m + 1) * E] for m in range(PIECES)]
     copies = []
     fetches = []
     for h in range(heads):
@@ -386,15 +393,64 @@
         for i, (a, b) in enumerate(((dk_in, dk_part), (dv_in, dv_part))):
             fetches.append(pltpu.make_async_copy(a.at[:, columns], b.at[:, columns], sems.at[h, 2 + i]))
             fetches[-1].start()
+    zero = jnp.zeros((E, E), bf16)
+    strips = []
+    for lo in range(0, width, STRIP):
+        low = jnp.int32(0)
+        high = jnp.int32(0)
+        for b in bounds:
+            low += (b <= lo).astype(jnp.int32)
+            high += (b < lo + STRIP).astype(jnp.int32)
+        strips.append((lo, low, high))
+    start = lax.axis_index("seq") * width
+    first = count_ends(ends, start)
+    still_open = [end_of(ends, first + m, start + width + 1) > start + width for m in range(PIECES)]
+    starts = [jnp.int32(0)] + bounds
+    stops = bounds + [jnp.int32(width)]
+
+    def chosen(table, m):
+        out = table[-1]
+        for i in reversed(range(PIECES - 1)):
+            out = jnp.where(m == i, table[i], out)
+        return out
+
     for h in range(heads):
         at = slice(h * E, (h + 1) * E)
-        mats = [load_matrix(states, m, h, states.shape[0] // heads) for m in range(PIECES)]
-        by_v = dot(v[:, at], jnp.concatenate(mats, axis=0), 1, 1)
+        for m in range(PIECES):
+            mat = load_matrix(states, m, h, states.shape[0] // heads).astype(f32)
+            mat = (mat + jnp.where(still_open[m], later[h], 0.0)).astype(bf16)
+            mats[h, m, :E, :E] = mat.T
+            mats[h, m, :E, E:] = zero
+            mats[h, m, E:, :E] = zero
+            mats[h, m, E:, E:] = mat
         fetches[2 * h].wait()
-        dk[:, at] = (dk_part[:, at] + pick_rows(rows, bounds, cut(by_v))).astype(bf16)
-        by_k = dot(k[:, at], jnp.concatenate(mats, axis=1), 1, 0)
         fetches[2 * h + 1].wait()
-        dv[:, at] = (dv_part[:, at] + pick_rows(rows, bounds, cut(by_k))).astype(bf16)
+        for lo, low, high in strips:
+            hi = lo + STRIP
+            both = jnp.concatenate([v[lo:hi, at], k[lo:hi, at]], axis=1)
+            rows = rows_of((STRIP, 2 * E), lo)
+
+            def part(m):
+                keep = jnp.logical_and(rows >= chosen(starts, m), rows < chosen(stops, m))
+                return dot(jnp.where(keep, both.astype(f32), 0.0).astype(bf16), mats[h, m], 1, 0)
+
+            @pl.when(low == high)
+            def _():
+                whole = dot(both, mats[h, low], 1, 0)
+                dk[lo:hi, at] = (dk_part[lo:hi, at] + whole[:, :E]).astype(bf16)
+                dv[lo:hi, at] = (dv_part[lo:hi, at] + whole[:, E:]).astype(bf16)
+
+            @pl.when(low != high)
+            def _():
+                total[...] = part(low) + part(low + 1)
+
+                @pl.when(high > low + 1)
+                def _():
+                    total[...] += part(low + 2)
+
+                dk[lo:hi, at] = (dk_part[lo:hi, at] + total[:, :E]).astype(bf16)
+                dv[lo:hi, at] = (dv_part[lo:hi, at] + total[:, E:]).astype(bf16)
+
         columns = pl.ds(h * E, E)
         for i, (a, b) in enumerate(((dk, dk_out), (dv, dv_out))):
             copies.append(pltpu.make_async_copy(a.at[:, columns], b.at[:, columns], sems.at[h, i]))
@@ -446,15 +502,16 @@
         return [pltpu.with_memory_space_constraint(a, pltpu.VMEM) for a in arrays]
 
     prompt_in = (prompt_q, prompt_k, prompt_v, prompt_grad)
-    pieces = call(
+    pieces, open_sums = call(
         sums_kernel,
         in_specs=[SMEM] + [ANY] * 4,
-        out_specs=VMEM,
-        out_shape=like((count, PIECES + 1, rows, E), bf16),
+        out_specs=[VMEM] * 2,
+        out_shape=[like((count, PIECES, rows, E), bf16), like((2, heads, E, E), bf16)],
         scratch_shapes=[pltpu.VMEM((width, flat), bf16)] * 4 + [pltpu.SemaphoreType.DMA((heads, 4))],
         name="sums",
     )(prompt_ends, *hbm(*prompt_in))
     parts = exchange(pieces)
+    open_sums = lax.all_gather(open_sums, "seq")
 
     pieces, late_in = lax.optimization_barrier((pieces, prompt_in))
     dq_part, dk_part, dv_part = call(
@@ -471,7 +528,7 @@
         lambda *refs: chain_kernel(*refs, width=width),
         in_specs=[SMEM, SMEM, VMEM],
         out_specs=VMEM,
-        out_shape=like((count, per_slab + 1, rows, E), bf16),
+        out_shape=like((count, per_slab, rows, E), bf16),
         scratch_shapes=[pltpu.VMEM((prompt_ends.shape[0] + 1, rows, E), f32)],
         name="chain",
     )(prompt_ends, cand_prompt, parts)
@@ -512,20 +569,9 @@
     )(cand_lengths, near_q, *near(slope), *raws)
     all_grads = exchange(grads)
 
-    grads, late_grad = lax.optimization_barrier((grads, prompt_grad))
-    prompt_dq = call(
-        query_kernel,
-        grid=(heads,),
-        in_specs=[SMEM, whole, whole, parts_block(per_slab + 1)],
-        out_specs=whole,
-        out_shape=pltpu.HBM((width, flat), bf16),
-        name="query",
-    )(prompt_ends, *hbm(dq_part, late_grad), states)
-    all_grads, prompt_dq = lax.optimization_barrier((all_grads, prompt_dq))
-
     right, coef, loss = call(
         lambda *refs: listwise_kernel(*refs, width=width),
-        in_specs=[SMEM, SMEM] + [VMEM] * 4,
+        in_specs=[SMEM, SMEM] + [VMEM] * 3,
         out_specs=[VMEM] * 3,
         out_shape=[
             like((count, PIECES, rows, E), bf16),
@@ -544,7 +590,6 @@
         cand_prompt.reshape(1, cands),
         cand_ranks.reshape(1, cands),
         all_grads,
-        parts,
     )
     rights = exchange(right)
 
@@ -553,23 +598,40 @@
         grid=(heads,),
         in_specs=[SMEM, pl.BlockSpec((8, E), lambda h: (0, 0))]
         + [cand_block] * 4
-        + [parts_block(per_slab + 1)],
+        + [parts_block(per_slab)],
         out_specs=[cand_block] * 3,
         out_shape=[pltpu.HBM((cand_width, flat), bf16)] * 3,
         name="cand",
     )(cand_lengths, coef, *hbm(*cand_in, slope_far), states)
-    rights, cand_dq, cand_dk, cand_dv = lax.optimization_barrier((rights, cand_dq, cand_dk, cand_dv))
+    gathered = [
+        pl.BlockSpec((count, 1, 1, E, E), lambda h: (0, 0, h, 0, 0)),
+        pl.BlockSpec((count, 1, 1, E, E), lambda h: (0, 1, h, 0, 0)),
+    ]
+    cand_dq, late_grad, open_sums = lax.optimization_barrier((cand_dq, prompt_grad, open_sums))
+    prompt_dq, later = call(
+        query_kernel,
+        grid=(heads,),
+        in_specs=[SMEM, whole, whole] + gathered,
+        out_specs=[whole, pl.BlockSpec((1, E, E), lambda h: (h, 0, 0))],
+        out_shape=[pltpu.HBM((width, flat), bf16), like((heads, E, E), f32)],
+        name="query",
+    )(prompt_ends, *hbm(dq_part, late_grad, open_sums, open_sums))
+    rights, cand_dk, prompt_dq = lax.optimization_barrier((rights, cand_dk, prompt_dq))
 
     prompt_dk, prompt_dv = call(
         right_kernel,
-        in_specs=[SMEM, ANY, ANY] + [VMEM] * 3,
+        in_specs=[SMEM, ANY, ANY] + [VMEM] * 4,
         out_specs=[ANY] * 2,
         out_shape=[pltpu.HBM((width, flat), bf16)] * 2,
         scratch_shapes=[pltpu.VMEM((width, flat), f32)] * 2
         + [pltpu.VMEM((width, flat), bf16)] * 2
-        + [pltpu.SemaphoreType.DMA((heads, 4))],
+        + [
+            pltpu.VMEM((heads, PIECES, 2 * E, 2 * E), bf16),
+            pltpu.VMEM((STRIP, 2 * E), f32),
+            pltpu.SemaphoreType.DMA((heads, 4)),
+        ],
         name="right",
-    )(prompt_ends, *hbm(dk_part, dv_part), *near(prompt_k, prompt_v), rights)
+    )(prompt_ends, *hbm(dk_part, dv_part), *near(prompt_k, prompt_v), later, rights)
     return (
         prompt_dq,
         prompt_dk,

time: 90.4 us -> 108 us (1.19)
  blocking collectives: 0 us -> 17.4 us
  between operations: 0.88 us -> 14.2 us
  waiting for transfers between devices: 23.9 us -> 12.6 us
  starting transfers between devices: 20.2 us -> 17.7 us
    all_to_all x0 -> x1, blocking collectives: none -> 17.4 us  [exchange(): return lax.all_to_all(a, 'seq', 0, 0, tiled=True)]
    all_to_all x4 -> x3, waiting for transfers between devices: 21.1 us -> 11.3 us  [exchange(): return lax.all_to_all(a, 'seq', 0, 0, tiled=True)]
    all_to_all x4 -> x3, starting transfers between devices: 18.4 us -> 14.1 us  [exchange(): return lax.all_to_all(a, 'seq', 0, 0, tiled=True)]
    ppermute x3, starting transfers between devices: 1.82 us -> 3.54 us  [per_device(): lax.ppermute(raw, 'head', [(i, (i + step) % groups) for i in range(groups)])]
    ppermute x3, waiting for transfers between devices: 2.87 us -> 1.33 us  [per_device(): lax.ppermute(raw, 'head', [(i, (i + step) % groups) for i in range(groups)])]
  transfers between devices with their start and end apart: 7 -> 7, of which waited for: 6 -> 5; matrix products, arithmetic and copies ran while one was open for 0% -> 0% of each run, Pallas kernels for 28% -> 31%
where the time goes in v4:
time: 108 us; the launch traced here: 107 us
  Pallas kernels  44.3 us (41%)
  starting transfers between devices  17.7 us (16%)
  blocking collectives  17.4 us (16%)
  between operations  14.2 us (13%)
  waiting for transfers between devices  12.6 us (12%)
    all_to_all x1, blocking collectives, exchange(): return lax.all_to_all(a, 'seq', 0, 0, tiled=True)  17.4 us
    all_to_all x3, starting transfers between devices, exchange(): return lax.all_to_all(a, 'seq', 0, 0, tiled=True)  14.1 us
    pallas_call x1, Pallas kernels, per_device(): call(prompt_kernel, grid=(heads,), in_specs=[SMEM] + [whole] * 4, out_spe...  11.4 us
    all_to_all x3, waiting for transfers between devices, exchange(): return lax.all_to_all(a, 'seq', 0, 0, tiled=True)  11.3 us
    pallas_call x1, Pallas kernels, per_device(): call(right_kernel, in_specs=[SMEM, ANY, ANY] + [VMEM] * 4, out_specs=[ANY...  6.98 us
    pallas_call x1, Pallas kernels, per_device(): call(lambda *refs: cand_kernel(*refs, scaling=scaling), grid=(heads,), in...  5.93 us
    pallas_call x1, Pallas kernels, per_device(): call(query_kernel, grid=(heads,), in_specs=[SMEM, whole, whole] + gathere...  5.09 us
    pallas_call x1, Pallas kernels, per_device(): call(sums_kernel, in_specs=[SMEM] + [ANY] * 4, out_specs=[VMEM] * 2, out_...  4.37 us
  transfers between devices with their start and end apart: 7, of which 5 were waited for; matrix products, arithmetic and copies ran while one was open for 0% of the time, Pallas kernels for 31%

profile of v4, /device:TPU:0, one launch (start us, length us, event | category | flops | bytes accessed | tf_op | source)
XLA Modules:
  0.0 107.0 jit_solution(15352116396546466081)
XLA Ops:
  7.2 0.0 all-gather.3.cloned.1.call-start
  7.2 0.0 copy-start.3
  7.2 0.6 copy-done.3
  7.9 0.0 copy-start.4
  7.9 4.4 %sums.1 = (bf16[8,3,64,128]{3,2,1,0:T(8,128)(2,1)}, bf16[2,4,128,128]{3,2,1,0:T(8,128)(2,1)}) custom-call(s32[8]{0:T(128)S(1)} %copy-done.3, bf16[1024,512]{1,0:T(8,128)(2,1)} %q, bf16[1024,512]{1,0:T(8,128)(2,1)} %k.3, bf16[1024,512]{1,0:T(8,128)(2,1)} %v.3, bf16[1024,512]{1,0:T(8,128)(2,1)} %g.1), custom_call_target="tpu_custom_call" | custom-call | tf_op jit(solution)/shard_map/sums/pallas_call | solution.py:505
  12.2 0.0 all-gather.3.cloned.1.call-update
  12.3 7.3 %all-to-all-start = ((bf16[8,3,64,128]{3,2,1,0:T(8,128)(2,1)}), bf16[8,3,64,128]{3,2,1,0:T(8,128)(2,1)S(1)}, u32[]{:S(2)}, u32[]{:S(2)}) async-start(bf16[8,3,64,128]{3,2,1,0:T(8,128)(2,1)} %get-tuple-element.42), calls=%async_computation | async-start | bytes 786432 | tf_op jit(solution)/shard_map/all_to_all | solution.py:463
  19.5 0.0 copy-done.4
  19.6 0.0 copy-start.6
  19.6 0.0 copy-start.5
  19.6 11.4 %prompt.1 = (f32[1024,512]{1,0:T(8,128)}, f32[1024,512]{1,0:T(8,128)}, f32[1024,512]{1,0:T(8,128)}) custom-call(s32[8]{0:T(128)S(1)} %copy-done.4, bf16[1024,512]{1,0:T(8,128)(2,1)} %q, bf16[1024,512]{1,0:T(8,128)(2,1)} %k.3, bf16[1024,512]{1,0:T(8,128)(2,1)} %v.3, bf16[1024,512]{1,0:T(8,128)(2,1)} %g.1), custom_call_target="tpu_custom_call" | custom-call | tf_op jit(solution)/shard_map/prompt/pallas_call | solution.py:517
  31.0 0.0 copy-start.2
  31.0 0.0 copy-start.7
  31.0 6.6 %all-to-all-done.refs_2_ = bf16[8,3,64,128]{3,2,1,0:T(8,128)(2,1)S(1)} async-done(((bf16[8,3,64,128]{3,2,1,0:T(8,128)(2,1)}), bf16[8,3,64,128]{3,2,1,0:T(8,128)(2,1)S(1)}, u32[]{:S(2)}, u32[]{:S(2)}) %all-to-all-start) | async-done | bytes 393248 | tf_op jit(solution)/shard_map/all_to_all | solution.py:463
  37.6 0.0 copy-done.6
  37.6 1.5 %chain.1 = bf16[8,2,64,128]{3,2,1,0:T(8,128)(2,1)} custom-call(s32[8]{0:T(128)S(1)} %copy-done.4, s32[16]{0:T(128)S(1)} %copy-done.6, bf16[8,3,64,128]{3,2,1,0:T(8,128)(2,1)S(1)} %all-to-all-done.refs_2_), custom_call_target="tpu_custom_call" | custom-call | tf_op jit(solution)/shard_map/chain/pallas_call | solution.py:527
  39.1 3.4 %all-to-all-start.1 = ((bf16[8,2,64,128]{3,2,1,0:T(8,128)(2,1)}), bf16[8,2,64,128]{3,2,1,0:T(8,128)(2,1)S(1)}, u32[]{:S(2)}, u32[]{:S(2)}) async-start(bf16[8,2,64,128]{3,2,1,0:T(8,128)(2,1)} %chain.1), calls=%async_computation.1 | async-start | bytes 524288 | tf_op jit(solution)/shard_map/all_to_all | solution.py:463
  42.5 0.0 copy-done.5
  42.5 3.9 %inside.1.refs_2_ = f32[512,512]{1,0:T(8,128)S(1)} custom-call(s32[1,2]{1,0:T(1,128)S(1)} %copy-done.5, bf16[512,512]{1,0:T(8,128)(2,1)} %refs_2_, bf16[512,512]{1,0:T(8,128)(2,1)} %refs_3_, bf16[512,512]{1,0:T(8,128)(2,1)} %refs_4_), custom_call_target="tpu_custom_call" | custom-call | tf_op jit(solution)/shard_map/inside/pallas_call | solution.py:538
  46.4 4.5 %all-to-all-done.1.refs_4_.refs_6_ = bf16[8,2,64,128]{3,2,1,0:T(8,128)(2,1)S(1)} async-done(((bf16[8,2,64,128]{3,2,1,0:T(8,128)(2,1)}), bf16[8,2,64,128]{3,2,1,0:T(8,128)(2,1)S(1)}, u32[]{:S(2)}, u32[]{:S(2)}) %all-to-all-start.1) | async-done | bytes 262176 | tf_op jit(solution)/shard_map/all_to_all | solution.py:463
  50.9 0.0 copy-done.2
  50.9 0.0 copy-done.7
  50.9 0.0 copy-start.8
  50.9 2.3 %scores.1 = (f32[512,512]{1,0:T(8,128)S(1)}, f32[8,128]{1,0:T(8,128)S(1)}, f32[512,512]{1,0:T(8,128)}) custom-call(s32[1,2]{1,0:T(1,128)S(1)} %copy-done.5, bf16[512,512]{1,0:T(8,128)(2,1)S(1)} %copy-done.2, f32[512,512]{1,0:T(8,128)S(1)} %inside.1.refs_2_, f32[1,512]{1,0:T(1,128)S(1)} %bitcast.7, bf16[8,2,64,128]{3,2,1,0:T(8,128)(2,1)S(1)} %all-to-all-done.1.refs_4_.refs_6_), custom_call_target="tpu_custom_call" | custom-call | tf_op jit(solution)/shard_map/scores/pallas_call | solution.py:548
  53.2 0.1 collective-permute-start
  53.2 2.1 %collective-permute-start.1 = (f32[8,128]{1,0:T(8,128)S(1)}, f32[8,128]{1,0:T(8,128)S(1)}, u32[]{:S(2)}, u32[]{:S(2)}) collective-permute-start(f32[8,128]{1,0:T(8,128)S(1)} %get-tuple-element.55.refs_3_), channel_id=1, source_target_pairs={{0,2},{1,3},{2,0},{3,1},{4,6},{5,7},{6,4},{7,5},{8,10},{9,11},{10,... | collective-permute-start | bytes 12296 | tf_op jit(solution)/shard_map/ppermute | solution.py:562
  55.3 1.4 %collective-permute-start.2 = (f32[8,128]{1,0:T(8,128)S(1)}, f32[8,128]{1,0:T(8,128)S(1)}, u32[]{:S(2)}, u32[]{:S(2)}) collective-permute-start(f32[8,128]{1,0:T(8,128)S(1)} %get-tuple-element.55.refs_3_), channel_id=1, source_target_pairs={{0,3},{1,0},{2,1},{3,2},{4,7},{5,4},{6,5},{7,6},{8,11},{9,8},{10,9... | collective-permute-start | bytes 12296 | tf_op jit(solution)/shard_map/ppermute | solution.py:562
  56.7 0.0 collective-permute-done.refs_4_
  56.7 0.2 collective-permute-done.1.refs_5_
  56.9 1.1 %collective-permute-done.2.refs_6_ = f32[8,128]{1,0:T(8,128)S(1)} collective-permute-done((f32[8,128]{1,0:T(8,128)S(1)}, f32[8,128]{1,0:T(8,128)S(1)}, u32[]{:S(2)}, u32[]{:S(2)}) %collective-permute-start.2) | collective-permute-done | bytes 4128 | tf_op jit(solution)/shard_map/ppermute | solution.py:562
  58.1 1.2 %grads.1 = bf16[8,144,128]{2,1,0:T(8,128)(2,1)S(1)} custom-call(s32[1,2]{1,0:T(1,128)S(1)} %copy-done.5, bf16[512,512]{1,0:T(8,128)(2,1)S(1)} %copy-done.2, f32[512,512]{1,0:T(8,128)S(1)} %get-tuple-element.54.refs_2_, f32[8,128]{1,0:T(8,128)S(1)} %get-tuple-element.55.refs_3_, f32[8,128]{1,0:T(8,128)S(1)} %collective-permute-done.refs_4_, ...), custom_call_target="tpu_custom_call" | custom-call | tf_op jit(solution)/shard_map/grads/pallas_call | solution.py:563
  59.3 17.4 %all_to_all.20.refs_4_ = bf16[8,144,128]{2,1,0:T(8,128)(2,1)S(1)} all-to-all(bf16[8,144,128]{2,1,0:T(8,128)(2,1)S(1)} %grads.1), channel_id=1, replica_groups=mesh['seq'=8,'head'=4] {'seq'}, dimensions={0} | all-to-all | bytes 589824 | tf_op jit(solution)/shard_map/all_to_all | solution.py:463
  76.7 0.0 copy-done.8
  76.7 1.7 %listwise.1 = (bf16[8,3,64,128]{3,2,1,0:T(8,128)(2,1)}, f32[8,128]{1,0:T(8,128)S(1)}, f32[1,128]{1,0:T(1,128)}) custom-call(s32[8]{0:T(128)S(1)} %copy-done.4, s32[16]{0:T(128)S(1)} %copy-done.6, s32[1,16]{1,0:T(1,128)S(1)} %bitcast.6, s32[1,16]{1,0:T(1,128)S(1)} %bitcast.8, bf16[8,144,128]{2,1,0:T(8,128)(2,1)S(1)} %all_to_all.20.refs_4_), custom_call_target="tpu_custom_call" | custom-call | tf_op jit(solution)/shard_map/listwise/pallas_call | solution.py:572
  78.4 3.5 %all-to-all-start.3 = ((bf16[8,3,64,128]{3,2,1,0:T(8,128)(2,1)}), bf16[8,3,64,128]{3,2,1,0:T(8,128)(2,1)S(1)}, u32[]{:S(2)}, u32[]{:S(2)}) async-start(bf16[8,3,64,128]{3,2,1,0:T(8,128)(2,1)} %get-tuple-element.56), calls=%async_computation.3 | async-start | bytes 786432 | tf_op jit(solution)/shard_map/all_to_all | solution.py:463
  81.9 5.9 %cand.1 = (bf16[512,512]{1,0:T(8,128)(2,1)}, bf16[512,512]{1,0:T(8,128)(2,1)}, bf16[512,512]{1,0:T(8,128)(2,1)}) custom-call(s32[1,2]{1,0:T(1,128)S(1)} %copy-done.5, f32[8,128]{1,0:T(8,128)S(1)} %get-tuple-element.57.refs_1_, bf16[512,512]{1,0:T(8,128)(2,1)} %refs_2_, bf16[512,512]{1,0:T(8,128)(2,1)} %refs_3_, bf16[512,512]{1,0:T(8,128)(2,1)} %refs_4_, ...), custom_call_target="tpu_custom_call" | custom-call | tf_op jit(solution)/shard_map/cand/pallas_call | solution.py:596
  87.8 0.0 all-gather.3.cloned.1.call-done
  87.8 0.0 copy-start
  87.9 0.0 copy-start.1
  87.9 5.1 %query.1 = (bf16[1024,512]{1,0:T(8,128)(2,1)}, f32[4,128,128]{2,1,0:T(8,128)S(1)}) custom-call(s32[8]{0:T(128)S(1)} %copy-done.4, f32[1024,512]{1,0:T(8,128)} %get-tuple-element.60.part, bf16[1024,512]{1,0:T(8,128)(2,1)} %g.1, bf16[8,2,4,128,128]{4,3,2,1,0:T(8,128)(2,1)} %bitcast.9, bf16[8,2,4,128,128]{4,3,2,1,0:T(8,128)(2,1)} %bitcast.10), custom_call_target="tpu_custom_call" | custom-call | tf_op jit(solution)/shard_map/query/pallas_call | solution.py:611
  93.0 0.2 all-to-all-done.3.states
  93.1 0.0 copy-done
  93.1 0.0 copy-done.1
  93.1 7.0 %right.1 = (bf16[1024,512]{1,0:T(8,128)(2,1)}, bf16[1024,512]{1,0:T(8,128)(2,1)}) custom-call(s32[8]{0:T(128)S(1)} %copy-done.4, f32[1024,512]{1,0:T(8,128)} %get-tuple-element.67.dk_in, f32[1024,512]{1,0:T(8,128)} %get-tuple-element.68.dv_in, bf16[1024,512]{1,0:T(8,128)(2,1)S(1)} %copy-done, bf16[1024,512]{1,0:T(8,128)(2,1)S(1)} %copy-done.1, ...), custom_call_target="tpu_custom_call" | custom-call | tf_op jit(solution)/shard_map/right/pallas_call | solution.py:621
Async XLA Ops:
  7.2 80.7 %all-gather.3.cloned.1.call-start = ((), (), s32[]{:S(2)}) async-start(), calls=%async_computation.4 | async-start | bytes 2359296 | tf_op jit(solution)/shard_map/all_gather | solution.py:514
  7.2 0.7 copy-start.3
  7.9 11.7 %copy-start.4 = (s32[8]{0:T(128)S(1)}, s32[8]{0:T(128)}, u32[]{:S(2)}) copy-start(s32[8]{0:T(128)} %ends.7) | copy-start | bytes 100
  12.3 25.3 %all-to-all-start = ((bf16[8,3,64,128]{3,2,1,0:T(8,128)(2,1)}), bf16[8,3,64,128]{3,2,1,0:T(8,128)(2,1)S(1)}, u32[]{:S(2)}, u32[]{:S(2)}) async-start(bf16[8,3,64,128]{3,2,1,0:T(8,128)(2,1)} %get-tuple-element.42), calls=%async_computation | async-start | bytes 786432 | tf_op jit(solution)/shard_map/all_to_all | solution.py:463
  19.6 18.0 %copy-start.6 = (s32[16]{0:T(128)S(1)}, s32[16]{0:T(128)}, u32[]{:S(2)}) copy-start(s32[16]{0:T(128)} %refs_1_.5) | copy-start | bytes 196
  19.6 22.9 %copy-start.5 = (s32[1,2]{1,0:T(1,128)S(1)}, s32[1,2]{1,0:T(1,128)}, u32[]{:S(2)}) copy-start(s32[1,2]{1,0:T(1,128)} %refs_0_.9) | copy-start | bytes 28
  31.0 19.9 %copy-start.2 = (bf16[512,512]{1,0:T(8,128)(2,1)S(1)}, bf16[512,512]{1,0:T(8,128)(2,1)}, u32[]{:S(2)}) copy-start(bf16[512,512]{1,0:T(8,128)(2,1)} %refs_2_) | copy-start | bytes 1572868
  31.0 19.9 %copy-start.7 = (f32[512]{0:T(512)S(1)}, f32[512]{0:T(512)}, u32[]{:S(2)}) copy-start(f32[512]{0:T(512)} %param.19) | copy-start | bytes 6148
  39.1 11.8 %all-to-all-start.1 = ((bf16[8,2,64,128]{3,2,1,0:T(8,128)(2,1)}), bf16[8,2,64,128]{3,2,1,0:T(8,128)(2,1)S(1)}, u32[]{:S(2)}, u32[]{:S(2)}) async-start(bf16[8,2,64,128]{3,2,1,0:T(8,128)(2,1)} %chain.1), calls=%async_computation.1 | async-start | bytes 524288 | tf_op jit(solution)/shard_map/all_to_all | solution.py:463
  50.9 25.8 %copy-start.8 = (s32[16]{0:T(128)S(1)}, s32[16]{0:T(128)}, u32[]{:S(2)}) copy-start(s32[16]{0:T(128)} %param.23) | copy-start | bytes 196
  53.2 3.5 %collective-permute-start = (f32[8,128]{1,0:T(8,128)S(1)}, f32[8,128]{1,0:T(8,128)S(1)}, u32[]{:S(2)}, u32[]{:S(2)}) collective-permute-start(f32[8,128]{1,0:T(8,128)S(1)} %get-tuple-element.55.refs_3_), channel_id=1, source_target_pairs={{0,1},{1,2},{2,3},{3,0},{4,5},{5,6},{6,7},{7,4},{8,9},{9,10},{10,1... | collective-permute-start | bytes 12296 | tf_op jit(solution)/shard_map/ppermute | solution.py:562
  53.2 3.7 %collective-permute-start.1 = (f32[8,128]{1,0:T(8,128)S(1)}, f32[8,128]{1,0:T(8,128)S(1)}, u32[]{:S(2)}, u32[]{:S(2)}) collective-permute-start(f32[8,128]{1,0:T(8,128)S(1)} %get-tuple-element.55.refs_3_), channel_id=1, source_target_pairs={{0,2},{1,3},{2,0},{3,1},{4,6},{5,7},{6,4},{7,5},{8,10},{9,11},{10,... | collective-permute-start | bytes 12296 | tf_op jit(solution)/shard_map/ppermute | solution.py:562
  55.3 2.7 %collective-permute-start.2 = (f32[8,128]{1,0:T(8,128)S(1)}, f32[8,128]{1,0:T(8,128)S(1)}, u32[]{:S(2)}, u32[]{:S(2)}) collective-permute-start(f32[8,128]{1,0:T(8,128)S(1)} %get-tuple-element.55.refs_3_), channel_id=1, source_target_pairs={{0,3},{1,0},{2,1},{3,2},{4,7},{5,4},{6,5},{7,6},{8,11},{9,8},{10,9... | collective-permute-start | bytes 12296 | tf_op jit(solution)/shard_map/ppermute | solution.py:562
  78.4 14.7 %all-to-all-start.3 = ((bf16[8,3,64,128]{3,2,1,0:T(8,128)(2,1)}), bf16[8,3,64,128]{3,2,1,0:T(8,128)(2,1)S(1)}, u32[]{:S(2)}, u32[]{:S(2)}) async-start(bf16[8,3,64,128]{3,2,1,0:T(8,128)(2,1)} %get-tuple-element.56), calls=%async_computation.3 | async-start | bytes 786432 | tf_op jit(solution)/shard_map/all_to_all | solution.py:463
  87.8 5.3 %copy-start = (bf16[1024,512]{1,0:T(8,128)(2,1)S(1)}, bf16[1024,512]{1,0:T(8,128)(2,1)}, u32[]{:S(2)}) copy-start(bf16[1024,512]{1,0:T(8,128)(2,1)} %k.3) | copy-start | bytes 3145732
  87.9 5.3 %copy-start.1 = (bf16[1024,512]{1,0:T(8,128)(2,1)S(1)}, bf16[1024,512]{1,0:T(8,128)(2,1)}, u32[]{:S(2)}) copy-start(bf16[1024,512]{1,0:T(8,128)(2,1)} %v.3) | copy-start | bytes 3145732
Sparse Core Ops, SparseCore 0:
  12.4 57.4 all-gather.2

commit v5 on v3

--- a/solution.py
+++ b/solution.py
@@ -81,23 +81,25 @@
     return jnp.concatenate([ref[h * share + o, place] for o in range(share)], axis=0)
 
 
-def sums_kernel(ends, q_in, k_in, v_in, g_in, out, q, k, v, g, sems):
-    width, flat = q.shape
+def sums_kernel(ends_in, k_in, v_in, out, ends, k, v, sems):
+    width, flat = k.shape
     heads = flat // E
     share = out.shape[0] // heads
     columns = [pl.ds(h * E, E) for h in range(heads)]
+    fetch_ends = pltpu.make_async_copy(ends_in, ends, sems.at[heads, 0])
+    fetch_ends.start()
     copies = [
         [
             pltpu.make_async_copy(a.at[:, columns[h]], b.at[:, columns[h]], sems.at[h, i])
-            for i, (a, b) in enumerate(((k_in, k), (v_in, v), (q_in, q), (g_in, g)))
+            for i, (a, b) in enumerate(((k_in, k), (v_in, v)))
         ]
         for h in range(heads)
     ]
     for group in copies:
         for c in group:
             c.start()
+    fetch_ends.wait()
     bounds = slab_bounds(ends, lax.axis_index("seq"), width)
-    scaling = 1.0 / math.sqrt(E * width)
     rows = rows_of((width, E))
     zero = jnp.zeros((width, E), f32)
     for h in range(heads):
@@ -115,8 +117,6 @@
         mine = out.at[pl.ds(h * share, share)]
         for m in range(PIECES):
             store_parts(mine, m, sums[:, m * E : (m + 1) * E])
-        first = jnp.where(rows < bounds[0], g[:, at].astype(f32), zero).astype(bf16)
-        store_parts(mine, PIECES, scaling * dot(q[:, at], first, 0, 0))
 
 
 def chain_kernel(ends, cand_prompt, parts, out, held, *, width):
@@ -201,8 +201,7 @@
         c.wait()
 
 
-def grads_kernel(lengths, q, slope, *refs, scaling):
-    raws, out = refs[:-1], refs[-1]
+def grads_kernel(lengths, q, slope, head, out, *, scaling):
     width, flat = q.shape
     heads = flat // E
     count = out.shape[0]
@@ -229,6 +228,12 @@
             grad = (scaling * grad).astype(bf16)
             for o in range(share):
                 out[h * share + o, j * size : (j + 1) * size] = grad[o * size : (o + 1) * size]
+    for o in range(count):
+        out[o, per_slab * size : (per_slab + 1) * size] = head[o, 0]
+
+
+def append_kernel(payload, *refs, per_slab):
+    raws, out, tile, sems = refs[:-3], refs[-3], refs[-2], refs[-1]
     total = raws[0][...]
     for r in raws[1:]:
         total += r[...]
@@ -240,9 +245,13 @@
             lines.append(line)
             left = left - line
     lines.append(jnp.zeros((SCORE_ROWS - len(lines), E), f32))
-    tile = jnp.concatenate(lines, axis=0).astype(bf16)
-    for o in range(count):
-        out[o, per_slab * size :] = tile
+    tile[...] = jnp.concatenate(lines, axis=0).astype(bf16)
+    place = pl.ds(out.shape[1] - SCORE_ROWS, SCORE_ROWS)
+    copies = [pltpu.make_async_copy(tile, out.at[o, place], sems.at[o]) for o in range(out.shape[0])]
+    for c in copies:
+        c.start()
+    for c in copies:
+        c.wait()
 
 
 def listwise_kernel(
@@ -251,7 +260,6 @@
     prompt_row,
     rank_row,
     grads,
-    parts,
     out,
     coef_out,
     loss_out,
@@ -262,12 +270,12 @@
     width,
 ):
     count = grads.shape[0]
-    size = parts.shape[2]
+    size = held.shape[1]
     per_slab = prompts.shape[0] // count
     cands = count * per_slab
     prompt_count = ends.shape[0]
     for e in range(count):
-        tile = grads[e, per_slab * size :].astype(f32)
+        tile = grads[e, (per_slab + 1) * size :].astype(f32)
         for j in range(per_slab):
             total = tile[SCORE_PARTS * j : SCORE_PARTS * j + 1]
             for i in range(1, SCORE_PARTS):
@@ -300,7 +308,7 @@
     for c in range(cands):
         j = c % per_slab
         held[prompts[c]] += grads[c // per_slab, j * size : (j + 1) * size].astype(f32) * coef[c : c + 1]
-    running = jnp.zeros(parts.shape[2:], f32)
+    running = jnp.zeros((size, E), f32)
     for e in reversed(range(count)):
         start = e * width
         far = start + width
@@ -315,7 +323,7 @@
             here = held[jnp.minimum(pid, prompt_count - 1)]
             out[e, m] = jnp.where(ended, here, from_right).astype(bf16)
             if m == 0:
-                running = parts[e, PIECES].astype(f32) + jnp.where(ended, here, running)
+                running = grads[e, per_slab * size : (per_slab + 1) * size].astype(f32) + jnp.where(ended, here, running)
         out[e, ENDS] = from_right_bf
 
 
@@ -344,7 +352,7 @@
         dq[lo:hi] = (scaling * block).astype(bf16)
 
 
-def prompt_kernel(ends, q, k, v, g, dq, dk, dv):
+def prompt_kernel(ends, q, k, v, g, dq, dk, dv, head):
     width = q.shape[0]
     scaling = 1.0 / math.sqrt(E * width)
     bounds = slab_bounds(ends, lax.axis_index("seq"), width)
@@ -358,6 +366,8 @@
         dv[lo:hi] = scaling * dot(attn, g[lo:], 1, 0)
         part = dot(gw, keys, 0, 0)
         if lo == 0:
+            first = jnp.where(rows_of((width, E)) < bounds[0], g[...].astype(f32), 0.0).astype(bf16)
+            store_parts(head, 0, scaling * dot(q[...], first, 0, 0))
             dq[...] = part
         else:
             dq[lo:] += part
@@ -373,31 +383,54 @@
     dq[...] = (scaling * (part[...] + jnp.where(rows < bounds[0], crossed, 0.0))).astype(bf16)
 
 
-def right_kernel(ends, dk_in, dv_in, k, v, states, dk_out, dv_out, dk_part, dv_part, dk, dv, sems):
-    width, flat = k.shape
+def fetch(pairs, columns, sems, first):
+    copies = []
+    for i, (a, b) in enumerate(pairs):
+        copies.append(pltpu.make_async_copy(a.at[:, columns], b, sems.at[first + i]))
+        copies[-1].start()
+    return copies
+
+
+def stage_kernel(dk_part, dv_part, k, v, partial, both, sems):
+    ahead = partial.shape[2] // E
+    copies = []
+    for h in range(ahead):
+        at = pl.ds(h * E, E)
+        pairs = [(dk_part, partial.at[0]), (dv_part, partial.at[1]), (k, both.at[0]), (v, both.at[1])]
+        copies += fetch([(a, b.at[:, at]) for a, b in pairs], at, sems, h * 4)
+    for c in copies:
+        c.wait()
+
+
+def right_kernel(
+    ends, partial, both, states, dk_in, dv_in, k_in, v_in, dk_out, dv_out, rest, rest_both, dk, dv, sems
+):
+    width, flat = dk_out.shape
     heads = flat // E
+    ahead = partial.shape[2] // E
+    waits = [[]] * ahead
+    for h in range(ahead, heads):
+        at = pl.ds((h - ahead) * E, E)
+        pairs = [(k_in, rest_both.at[0]), (v_in, rest_both.at[1]), (dk_in, rest.at[0]), (dv_in, rest.at[1])]
+        waits.append(fetch([(a, b.at[:, at]) for a, b in pairs], pl.ds(h * E, E), sems, h * 4))
     bounds = slab_bounds(ends, lax.axis_index("seq"), width)
     rows = rows_of((width, E))
     cut = lambda a: [a[:, m * E : (m + 1) * E] for m in range(PIECES)]
     copies = []
-    fetches = []
     for h in range(heads):
-        columns = pl.ds(h * E, E)
-        for i, (a, b) in enumerate(((dk_in, dk_part), (dv_in, dv_part))):
-            fetches.append(pltpu.make_async_copy(a.at[:, columns], b.at[:, columns], sems.at[h, 2 + i]))
-            fetches[-1].start()
-    for h in range(heads):
-        at = slice(h * E, (h + 1) * E)
+        near, kv, place = (partial, both, h) if h < ahead else (rest, rest_both, h - ahead)
+        at = slice(place * E, (place + 1) * E)
+        mine = slice(h * E, (h + 1) * E)
+        for c in waits[h]:
+            c.wait()
         mats = [load_matrix(states, m, h, states.shape[0] // heads) for m in range(PIECES)]
-        by_v = dot(v[:, at], jnp.concatenate(mats, axis=0), 1, 1)
-        fetches[2 * h].wait()
-        dk[:, at] = (dk_part[:, at] + pick_rows(rows, bounds, cut(by_v))).astype(bf16)
-        by_k = dot(k[:, at], jnp.concatenate(mats, axis=1), 1, 0)
-        fetches[2 * h + 1].wait()
-        dv[:, at] = (dv_part[:, at] + pick_rows(rows, bounds, cut(by_k))).astype(bf16)
+        by_v = dot(kv[1, :, at], jnp.concatenate(mats, axis=0), 1, 1)
+        dk[:, mine] = (near[0, :, at] + pick_rows(rows, bounds, cut(by_v))).astype(bf16)
+        by_k = dot(kv[0, :, at], jnp.concatenate(mats, axis=1), 1, 0)
+        dv[:, mine] = (near[1, :, at] + pick_rows(rows, bounds, cut(by_k))).astype(bf16)
         columns = pl.ds(h * E, E)
         for i, (a, b) in enumerate(((dk, dk_out), (dv, dv_out))):
-            copies.append(pltpu.make_async_copy(a.at[:, columns], b.at[:, columns], sems.at[h, i]))
+            copies.append(pltpu.make_async_copy(a.at[:, columns], b.at[:, columns], sems.at[(heads + h) * 4 + i]))
             copies[-1].start()
     for c in copies:
         c.wait()
@@ -448,21 +481,23 @@
     prompt_in = (prompt_q, prompt_k, prompt_v, prompt_grad)
     pieces = call(
         sums_kernel,
-        in_specs=[SMEM] + [ANY] * 4,
+        in_specs=[ANY] * 3,
         out_specs=VMEM,
-        out_shape=like((count, PIECES + 1, rows, E), bf16),
-        scratch_shapes=[pltpu.VMEM((width, flat), bf16)] * 4 + [pltpu.SemaphoreType.DMA((heads, 4))],
+        out_shape=like((count, PIECES, rows, E), bf16),
+        scratch_shapes=[pltpu.SMEM(prompt_ends.shape, jnp.int32)]
+        + [pltpu.VMEM((width, flat), bf16)] * 2
+        + [pltpu.SemaphoreType.DMA((heads + 1, 2))],
         name="sums",
-    )(prompt_ends, *hbm(*prompt_in))
+    )(*hbm(prompt_ends, prompt_k, prompt_v))
     parts = exchange(pieces)
 
     pieces, late_in = lax.optimization_barrier((pieces, prompt_in))
-    dq_part, dk_part, dv_part = call(
+    dq_part, dk_part, dv_part, head_part = call(
         prompt_kernel,
         grid=(heads,),
         in_specs=[SMEM] + [whole] * 4,
-        out_specs=[whole] * 3,
-        out_shape=[pltpu.HBM((width, flat), f32)] * 3,
+        out_specs=[whole] * 3 + [parts_block(1)],
+        out_shape=[pltpu.HBM((width, flat), f32)] * 3 + [like((count, 1, rows, E), bf16)],
         name="prompt",
     )(prompt_ends, *hbm(*late_in))
     parts, dq_part, dk_part, dv_part = lax.optimization_barrier((parts, dq_part, dk_part, dv_part))
@@ -503,13 +538,23 @@
     raws = [raw]
     for step in range(1, groups):
         raws.append(lax.ppermute(raw, "head", [(i, (i + step) % groups) for i in range(groups)]))
+    payload_shape = (count, (per_slab + 1) * rows + SCORE_ROWS, E)
     grads = call(
         lambda *refs: grads_kernel(*refs, scaling=scaling),
-        in_specs=[SMEM] + [VMEM] * (2 + groups),
+        in_specs=[SMEM] + [VMEM] * 3,
         out_specs=VMEM,
-        out_shape=like((count, per_slab * rows + SCORE_ROWS, E), bf16),
+        out_shape=pltpu.HBM(payload_shape, bf16),
         name="grads",
-    )(cand_lengths, near_q, *near(slope), *raws)
+    )(cand_lengths, near_q, *near(slope), head_part)
+    grads = call(
+        lambda *refs: append_kernel(*refs, per_slab=per_slab),
+        in_specs=[ANY] + [VMEM] * groups,
+        out_specs=ANY,
+        out_shape=pltpu.HBM(payload_shape, bf16),
+        input_output_aliases={0: 0},
+        scratch_shapes=[pltpu.VMEM((SCORE_ROWS, E), bf16), pltpu.SemaphoreType.DMA((count,))],
+        name="append",
+    )(*hbm(grads), *raws)
     all_grads = exchange(grads)
 
     grads, late_grad = lax.optimization_barrier((grads, prompt_grad))
@@ -525,7 +570,7 @@
 
     right, coef, loss = call(
         lambda *refs: listwise_kernel(*refs, width=width),
-        in_specs=[SMEM, SMEM] + [VMEM] * 4,
+        in_specs=[SMEM, SMEM] + [VMEM] * 3,
         out_specs=[VMEM] * 3,
         out_shape=[
             like((count, PIECES, rows, E), bf16),
@@ -544,7 +589,6 @@
         cand_prompt.reshape(1, cands),
         cand_ranks.reshape(1, cands),
         all_grads,
-        parts,
     )
     rights = exchange(right)
 
@@ -558,18 +602,32 @@
         out_shape=[pltpu.HBM((cand_width, flat), bf16)] * 3,
         name="cand",
     )(cand_lengths, coef, *hbm(*cand_in, slope_far), states)
-    rights, cand_dq, cand_dk, cand_dv = lax.optimization_barrier((rights, cand_dq, cand_dk, cand_dv))
+    cand_dq, late = lax.optimization_barrier((cand_dq, (dk_part, dv_part, prompt_k, prompt_v)))
+    ahead = flat // 2
+    staged = call(
+        stage_kernel,
+        in_specs=[ANY] * 4,
+        out_specs=[VMEM] * 2,
+        out_shape=[pltpu.VMEM((2, width, ahead), f32), pltpu.VMEM((2, width, ahead), bf16)],
+        scratch_shapes=[pltpu.SemaphoreType.DMA((heads * 4,))],
+        name="stage",
+    )(*hbm(*late))
+    rights, staged = lax.optimization_barrier((rights, staged))
 
     prompt_dk, prompt_dv = call(
         right_kernel,
-        in_specs=[SMEM, ANY, ANY] + [VMEM] * 3,
+        in_specs=[SMEM] + [VMEM] * 3 + [ANY] * 4,
         out_specs=[ANY] * 2,
         out_shape=[pltpu.HBM((width, flat), bf16)] * 2,
-        scratch_shapes=[pltpu.VMEM((width, flat), f32)] * 2
-        + [pltpu.VMEM((width, flat), bf16)] * 2
-        + [pltpu.SemaphoreType.DMA((heads, 4))],
+        scratch_shapes=[
+            pltpu.VMEM((2, width, flat - ahead), f32),
+            pltpu.VMEM((2, width, flat - ahead), bf16),
+            pltpu.VMEM((width, flat), bf16),
+            pltpu.VMEM((width, flat), bf16),
+            pltpu.SemaphoreType.DMA((8 * heads,)),
+        ],
         name="right",
-    )(prompt_ends, *hbm(dk_part, dv_part), *near(prompt_k, prompt_v), rights)
+    )(prompt_ends, *near(*staged), rights, *hbm(*late))
     return (
         prompt_dq,
         prompt_dk,

time: 90.4 us -> 87.6 us (0.969)
  waiting for transfers between devices: 23.9 us -> 20.2 us
  starting transfers between devices: 20.2 us -> 22.4 us
    all_to_all x4, starting transfers between devices: 18.4 us -> 20.6 us  [exchange(): return lax.all_to_all(a, 'seq', 0, 0, tiled=True)]
    ppermute x3, waiting for transfers between devices: 2.87 us -> 0.9 us  [per_device(): lax.ppermute(raw, 'head', [(i, (i + step) % groups) for i in range(groups)])]
    all_to_all x4, waiting for transfers between devices: 21.1 us -> 19.3 us  [exchange(): return lax.all_to_all(a, 'seq', 0, 0, tiled=True)]
    pallas_call x2 -> x4, Pallas kernels: 11.2 us -> 10.4 us  [the longest x1 4.39 us: per_device(): call(right_kernel, in_specs=[SMEM] + [VMEM] * 3 + [ANY] * 4, out_specs=[A...]
  transfers between devices with their start and end apart: 7 -> 7, of which waited for: 6 -> 4; matrix products, arithmetic and copies ran while one was open for 0% -> 0% of each run, Pallas kernels for 28% -> 34%
where the time goes in v5:
time: 87.6 us; the launch traced here: 86.8 us
  Pallas kernels  43.5 us (50%)
  starting transfers between devices  22.4 us (26%)
  waiting for transfers between devices  20.2 us (23%)
    all_to_all x4, starting transfers between devices, exchange(): return lax.all_to_all(a, 'seq', 0, 0, tiled=True)  20.6 us
    all_to_all x4, waiting for transfers between devices, exchange(): return lax.all_to_all(a, 'seq', 0, 0, tiled=True)  19.3 us
    pallas_call x1, Pallas kernels, per_device(): call(prompt_kernel, grid=(heads,), in_specs=[SMEM] + [whole] * 4, out_spe...  11.6 us
    pallas_call x1, Pallas kernels, per_device(): call(lambda *refs: cand_kernel(*refs, scaling=scaling), grid=(heads,), in...  5.92 us
    pallas_call x1, Pallas kernels, per_device(): call(right_kernel, in_specs=[SMEM] + [VMEM] * 3 + [ANY] * 4, out_specs=[A...  4.39 us
    pallas_call x1, Pallas kernels, per_device(): call(query_kernel, grid=(heads,), in_specs=[SMEM, whole, whole, parts_blo...  4.22 us
    pallas_call x1, Pallas kernels, per_device(): call(inside_kernel, grid=(heads,), in_specs=[SMEM] + [cand_block] * 3, ou...  3.85 us
    pallas_call x1, Pallas kernels, per_device(): call(sums_kernel, in_specs=[ANY] * 3, out_specs=VMEM, out_shape=like((cou...  3.28 us
  transfers between devices with their start and end apart: 7, of which 4 were waited for; matrix products, arithmetic and copies ran while one was open for 0% of the time, Pallas kernels for 34%

profile of v5, /device:TPU:0, one launch (start us, length us, event | category | flops | bytes accessed | tf_op | source)
XLA Modules:
  0.0 86.8 jit_solution(13440060264063628747)
XLA Ops:
  0.6 0.0 copy-start.1
  0.6 3.3 %sums.1 = bf16[8,3,64,128]{3,2,1,0:T(8,128)(2,1)} custom-call(s32[8]{0:T(128)} %ends.5, bf16[1024,512]{1,0:T(8,128)(2,1)} %k_in.2, bf16[1024,512]{1,0:T(8,128)(2,1)} %v_in.2), custom_call_target="tpu_custom_call" | custom-call | tf_op jit(solution)/shard_map/sums/pallas_call | solution.py:482
  3.9 7.3 %all-to-all-start = ((bf16[8,3,64,128]{3,2,1,0:T(8,128)(2,1)}), bf16[8,3,64,128]{3,2,1,0:T(8,128)(2,1)S(1)}, u32[]{:S(2)}, u32[]{:S(2)}) async-start(bf16[8,3,64,128]{3,2,1,0:T(8,128)(2,1)} %sums.1), calls=%async_computation | async-start | bytes 786432 | tf_op jit(solution)/shard_map/all_to_all | solution.py:440
  11.2 0.0 copy-done.1
  11.2 0.0 copy-start.3
  11.2 0.0 copy-start.2
  11.2 11.6 %prompt.1 = (f32[1024,512]{1,0:T(8,128)}, f32[1024,512]{1,0:T(8,128)}, f32[1024,512]{1,0:T(8,128)}, bf16[8,1,64,128]{3,2,1,0:T(8,128)(2,1)S(1)}) custom-call(s32[8]{0:T(128)S(1)} %copy-done.1, bf16[1024,512]{1,0:T(8,128)(2,1)} %q, bf16[1024,512]{1,0:T(8,128)(2,1)} %k_in.2, bf16[1024,512]{1,0:T(8,128)(2,1)} %v_in.2, bf16[1024,512]{1,0:T(8,128)(2,1)} %g.1), custom_call_target="tpu_custom_call" | custom-call | tf_op jit(solution)/shard_map/prompt/pallas_call | solution.py:495
  22.8 0.0 all-to-all-done.refs_2_
  22.9 0.0 copy-done.3
  22.9 0.0 copy-start
  22.9 0.0 copy-start.4
  22.9 1.5 %chain.1 = bf16[8,3,64,128]{3,2,1,0:T(8,128)(2,1)} custom-call(s32[8]{0:T(128)S(1)} %copy-done.1, s32[16]{0:T(128)S(1)} %copy-done.3, bf16[8,3,64,128]{3,2,1,0:T(8,128)(2,1)S(1)} %all-to-all-done.refs_2_), custom_call_target="tpu_custom_call" | custom-call | tf_op jit(solution)/shard_map/chain/pallas_call | solution.py:505
  24.4 6.0 %all-to-all-start.1 = ((bf16[8,3,64,128]{3,2,1,0:T(8,128)(2,1)}), bf16[8,3,64,128]{3,2,1,0:T(8,128)(2,1)S(1)}, u32[]{:S(2)}, u32[]{:S(2)}) async-start(bf16[8,3,64,128]{3,2,1,0:T(8,128)(2,1)} %chain.1), calls=%async_computation.1 | async-start | bytes 786432 | tf_op jit(solution)/shard_map/all_to_all | solution.py:440
  30.4 0.0 copy-done.2
  30.4 3.9 %inside.1.refs_2_ = f32[512,512]{1,0:T(8,128)S(1)} custom-call(s32[1,2]{1,0:T(1,128)S(1)} %copy-done.2, bf16[512,512]{1,0:T(8,128)(2,1)} %refs_2_, bf16[512,512]{1,0:T(8,128)(2,1)} %refs_3_, bf16[512,512]{1,0:T(8,128)(2,1)} %refs_4_), custom_call_target="tpu_custom_call" | custom-call | tf_op jit(solution)/shard_map/inside/pallas_call | solution.py:516
  34.3 7.3 %all-to-all-done.1.refs_4_.states.refs_6_ = bf16[8,3,64,128]{3,2,1,0:T(8,128)(2,1)S(1)} async-done(((bf16[8,3,64,128]{3,2,1,0:T(8,128)(2,1)}), bf16[8,3,64,128]{3,2,1,0:T(8,128)(2,1)S(1)}, u32[]{:S(2)}, u32[]{:S(2)}) %all-to-all-start.1) | async-done | bytes 393248 | tf_op jit(solution)/shard_map/all_to_all | solution.py:440
  41.5 0.0 copy-done
  41.5 0.0 copy-done.4
  41.5 2.3 %scores.1 = (f32[512,512]{1,0:T(8,128)S(1)}, f32[8,128]{1,0:T(8,128)S(1)}, f32[512,512]{1,0:T(8,128)}) custom-call(s32[1,2]{1,0:T(1,128)S(1)} %copy-done.2, bf16[512,512]{1,0:T(8,128)(2,1)S(1)} %copy-done, f32[512,512]{1,0:T(8,128)S(1)} %inside.1.refs_2_, f32[1,512]{1,0:T(1,128)S(1)} %bitcast.6, bf16[8,3,64,128]{3,2,1,0:T(8,128)(2,1)S(1)} %all-to-all-done.1.refs_4_.states.refs_6_), custom_call_target="tpu_custom_call" | custom-call | tf_op jit(solution)/shard_map/scores/pallas_call | solution.py:526
  43.8 0.1 collective-permute-start.2
  43.9 1.6 %collective-permute-start.1 = (f32[8,128]{1,0:T(8,128)S(1)}, f32[8,128]{1,0:T(8,128)S(1)}, u32[]{:S(2)}, u32[]{:S(2)}) collective-permute-start(f32[8,128]{1,0:T(8,128)S(1)} %get-tuple-element.59.refs_1_), channel_id=1, source_target_pairs={{0,2},{1,3},{2,0},{3,1},{4,6},{5,7},{6,4},{7,5},{8,10},{9,11},{10,... | collective-permute-start | bytes 12296 | tf_op jit(solution)/shard_map/ppermute | solution.py:540
  45.5 0.2 collective-permute-start
  45.7 2.0 %grads.1.refs_0_ = bf16[8,208,128]{2,1,0:T(8,128)(2,1)} custom-call(s32[1,2]{1,0:T(1,128)S(1)} %copy-done.2, bf16[512,512]{1,0:T(8,128)(2,1)S(1)} %copy-done, f32[512,512]{1,0:T(8,128)S(1)} %get-tuple-element.57.refs_2_, bf16[8,1,64,128]{3,2,1,0:T(8,128)(2,1)S(1)} %get-tuple-element.58.refs_3_), custom_call_target="tpu_custom_call" | custom-call | tf_op jit(solution)/shard_map/grads/pallas_call | solution.py:542
  47.6 0.0 collective-permute-done.2.refs_4_
  47.6 0.0 collective-permute-done.1.refs_3_
  47.6 0.9 %collective-permute-done.refs_2_ = f32[8,128]{1,0:T(8,128)S(1)} collective-permute-done((f32[8,128]{1,0:T(8,128)S(1)}, f32[8,128]{1,0:T(8,128)S(1)}, u32[]{:S(2)}, u32[]{:S(2)}) %collective-permute-start) | collective-permute-done | bytes 4128 | tf_op jit(solution)/shard_map/ppermute | solution.py:540
  48.5 0.7 append.1
  49.2 3.7 %all-to-all-start.2 = ((bf16[8,208,128]{2,1,0:T(8,128)(2,1)}), bf16[8,208,128]{2,1,0:T(8,128)(2,1)S(1)}, u32[]{:S(2)}, u32[]{:S(2)}) async-start(bf16[8,208,128]{2,1,0:T(8,128)(2,1)} %append.1), calls=%async_computation.2 | async-start | bytes 851968 | tf_op jit(solution)/shard_map/all_to_all | solution.py:440
  52.9 0.0 copy-start.5
  52.9 4.2 %query.1 = bf16[1024,512]{1,0:T(8,128)(2,1)} custom-call(s32[8]{0:T(128)S(1)} %copy-done.1, f32[1024,512]{1,0:T(8,128)} %get-tuple-element.60.part, bf16[1024,512]{1,0:T(8,128)(2,1)} %g.1, bf16[8,3,64,128]{3,2,1,0:T(8,128)(2,1)S(1)} %all-to-all-done.1.refs_4_.states.refs_6_), custom_call_target="tpu_custom_call" | custom-call | tf_op jit(solution)/shard_map/query/pallas_call | solution.py:561
  57.2 8.2 %all-to-all-done.2.refs_4_ = bf16[8,208,128]{2,1,0:T(8,128)(2,1)S(1)} async-done(((bf16[8,208,128]{2,1,0:T(8,128)(2,1)}), bf16[8,208,128]{2,1,0:T(8,128)(2,1)S(1)}, u32[]{:S(2)}, u32[]{:S(2)}) %all-to-all-start.2) | async-done | bytes 426016 | tf_op jit(solution)/shard_map/all_to_all | solution.py:440
  65.4 0.0 copy-done.5
  65.4 1.7 %listwise.1 = (bf16[8,3,64,128]{3,2,1,0:T(8,128)(2,1)}, f32[8,128]{1,0:T(8,128)S(1)}, f32[1,128]{1,0:T(1,128)}) custom-call(s32[8]{0:T(128)S(1)} %copy-done.1, s32[16]{0:T(128)S(1)} %copy-done.3, s32[1,16]{1,0:T(1,128)S(1)} %bitcast.5, s32[1,16]{1,0:T(1,128)S(1)} %bitcast.7, bf16[8,208,128]{2,1,0:T(8,128)(2,1)S(1)} %all-to-all-done.2.refs_4_), custom_call_target="tpu_custom_call" | custom-call | tf_op jit(solution)/shard_map/listwise/pallas_call | solution.py:571
  67.1 3.6 %all-to-all-start.3 = ((bf16[8,3,64,128]{3,2,1,0:T(8,128)(2,1)}), bf16[8,3,64,128]{3,2,1,0:T(8,128)(2,1)S(1)}, u32[]{:S(2)}, u32[]{:S(2)}) async-start(bf16[8,3,64,128]{3,2,1,0:T(8,128)(2,1)} %get-tuple-element.64), calls=%async_computation.3 | async-start | bytes 786432 | tf_op jit(solution)/shard_map/all_to_all | solution.py:440
  70.7 5.9 %cand.1 = (bf16[512,512]{1,0:T(8,128)(2,1)}, bf16[512,512]{1,0:T(8,128)(2,1)}, bf16[512,512]{1,0:T(8,128)(2,1)}) custom-call(s32[1,2]{1,0:T(1,128)S(1)} %copy-done.2, f32[8,128]{1,0:T(8,128)S(1)} %get-tuple-element.65.refs_1_, bf16[512,512]{1,0:T(8,128)(2,1)} %refs_2_, bf16[512,512]{1,0:T(8,128)(2,1)} %refs_3_, bf16[512,512]{1,0:T(8,128)(2,1)} %refs_4_, ...), custom_call_target="tpu_custom_call" | custom-call | tf_op jit(solution)/shard_map/cand/pallas_call | solution.py:595
  76.6 2.0 %stage.1 = (f32[2,1024,256]{2,1,0:T(8,128)S(1)}, bf16[2,1024,256]{2,1,0:T(8,128)(2,1)S(1)}) custom-call(f32[1024,512]{1,0:T(8,128)} %get-tuple-element.70.dk_part.dk_in, f32[1024,512]{1,0:T(8,128)} %get-tuple-element.71.dv_part.dv_in, bf16[1024,512]{1,0:T(8,128)(2,1)} %k_in.2, bf16[1024,512]{1,0:T(8,128)(2,1)} %v_in.2), custom_call_target="tpu_custom_call" | custom-call | tf_op jit(solution)/shard_map/stage/pallas_call | solution.py:607
  78.7 3.8 %all-to-all-done.3.states = bf16[8,3,64,128]{3,2,1,0:T(8,128)(2,1)S(1)} async-done(((bf16[8,3,64,128]{3,2,1,0:T(8,128)(2,1)}), bf16[8,3,64,128]{3,2,1,0:T(8,128)(2,1)S(1)}, u32[]{:S(2)}, u32[]{:S(2)}) %all-to-all-start.3) | async-done | bytes 393248 | tf_op jit(solution)/shard_map/all_to_all | solution.py:440
  82.4 4.4 %right.1 = (bf16[1024,512]{1,0:T(8,128)(2,1)}, bf16[1024,512]{1,0:T(8,128)(2,1)}) custom-call(s32[8]{0:T(128)S(1)} %copy-done.1, f32[2,1024,256]{2,1,0:T(8,128)S(1)} %get-tuple-element.76.partial, bf16[2,1024,256]{2,1,0:T(8,128)(2,1)S(1)} %get-tuple-element.77.both, bf16[8,3,64,128]{3,2,1,0:T(8,128)(2,1)S(1)} %all-to-all-done.3.states, ...), custom_call_target="tpu_custom_call" | custom-call | tf_op jit(solution)/shard_map/right/pallas_call | solution.py:617
Async XLA Ops:
  0.6 10.6 %copy-start.1 = (s32[8]{0:T(128)S(1)}, s32[8]{0:T(128)}, u32[]{:S(2)}) copy-start(s32[8]{0:T(128)} %ends.5) | copy-start | bytes 100
  3.9 19.0 %all-to-all-start = ((bf16[8,3,64,128]{3,2,1,0:T(8,128)(2,1)}), bf16[8,3,64,128]{3,2,1,0:T(8,128)(2,1)S(1)}, u32[]{:S(2)}, u32[]{:S(2)}) async-start(bf16[8,3,64,128]{3,2,1,0:T(8,128)(2,1)} %sums.1), calls=%async_computation | async-start | bytes 786432 | tf_op jit(solution)/shard_map/all_to_all | solution.py:440
  11.2 11.7 %copy-start.3 = (s32[16]{0:T(128)S(1)}, s32[16]{0:T(128)}, u32[]{:S(2)}) copy-start(s32[16]{0:T(128)} %refs_1_.5) | copy-start | bytes 196
  11.2 19.2 %copy-start.2 = (s32[1,2]{1,0:T(1,128)S(1)}, s32[1,2]{1,0:T(1,128)}, u32[]{:S(2)}) copy-start(s32[1,2]{1,0:T(1,128)} %refs_0_.9) | copy-start | bytes 28
  22.9 18.6 %copy-start = (bf16[512,512]{1,0:T(8,128)(2,1)S(1)}, bf16[512,512]{1,0:T(8,128)(2,1)}, u32[]{:S(2)}) copy-start(bf16[512,512]{1,0:T(8,128)(2,1)} %refs_2_) | copy-start | bytes 1572868
  22.9 18.6 %copy-start.4 = (f32[512]{0:T(512)S(1)}, f32[512]{0:T(512)}, u32[]{:S(2)}) copy-start(f32[512]{0:T(512)} %param.19) | copy-start | bytes 6148
  24.4 17.1 %all-to-all-start.1 = ((bf16[8,3,64,128]{3,2,1,0:T(8,128)(2,1)}), bf16[8,3,64,128]{3,2,1,0:T(8,128)(2,1)S(1)}, u32[]{:S(2)}, u32[]{:S(2)}) async-start(bf16[8,3,64,128]{3,2,1,0:T(8,128)(2,1)} %chain.1), calls=%async_computation.1 | async-start | bytes 786432 | tf_op jit(solution)/shard_map/all_to_all | solution.py:440
  43.8 3.8 %collective-permute-start.2 = (f32[8,128]{1,0:T(8,128)S(1)}, f32[8,128]{1,0:T(8,128)S(1)}, u32[]{:S(2)}, u32[]{:S(2)}) collective-permute-start(f32[8,128]{1,0:T(8,128)S(1)} %get-tuple-element.59.refs_1_), channel_id=1, source_target_pairs={{0,3},{1,0},{2,1},{3,2},{4,7},{5,4},{6,5},{7,6},{8,11},{9,8},{10,9... | collective-permute-start | bytes 12296 | tf_op jit(solution)/shard_map/ppermute | solution.py:540
  43.9 3.7 %collective-permute-start.1 = (f32[8,128]{1,0:T(8,128)S(1)}, f32[8,128]{1,0:T(8,128)S(1)}, u32[]{:S(2)}, u32[]{:S(2)}) collective-permute-start(f32[8,128]{1,0:T(8,128)S(1)} %get-tuple-element.59.refs_1_), channel_id=1, source_target_pairs={{0,2},{1,3},{2,0},{3,1},{4,6},{5,7},{6,4},{7,5},{8,10},{9,11},{10,... | collective-permute-start | bytes 12296 | tf_op jit(solution)/shard_map/ppermute | solution.py:540
  45.5 3.0 %collective-permute-start = (f32[8,128]{1,0:T(8,128)S(1)}, f32[8,128]{1,0:T(8,128)S(1)}, u32[]{:S(2)}, u32[]{:S(2)}) collective-permute-start(f32[8,128]{1,0:T(8,128)S(1)} %get-tuple-element.59.refs_1_), channel_id=1, source_target_pairs={{0,1},{1,2},{2,3},{3,0},{4,5},{5,6},{6,7},{7,4},{8,9},{9,10},{10,1... | collective-permute-start | bytes 12296 | tf_op jit(solution)/shard_map/ppermute | solution.py:540
  49.2 16.1 %all-to-all-start.2 = ((bf16[8,208,128]{2,1,0:T(8,128)(2,1)}), bf16[8,208,128]{2,1,0:T(8,128)(2,1)S(1)}, u32[]{:S(2)}, u32[]{:S(2)}) async-start(bf16[8,208,128]{2,1,0:T(8,128)(2,1)} %append.1), calls=%async_computation.2 | async-start | bytes 851968 | tf_op jit(solution)/shard_map/all_to_all | solution.py:440
  52.9 12.4 %copy-start.5 = (s32[16]{0:T(128)S(1)}, s32[16]{0:T(128)}, u32[]{:S(2)}) copy-start(s32[16]{0:T(128)} %param.23) | copy-start | bytes 196
  67.1 15.4 %all-to-all-start.3 = ((bf16[8,3,64,128]{3,2,1,0:T(8,128)(2,1)}), bf16[8,3,64,128]{3,2,1,0:T(8,128)(2,1)S(1)}, u32[]{:S(2)}, u32[]{:S(2)}) async-start(bf16[8,3,64,128]{3,2,1,0:T(8,128)(2,1)} %get-tuple-element.64), calls=%async_computation.3 | async-start | bytes 786432 | tf_op jit(solution)/shard_map/all_to_all | solution.py:440

commit v6 on v5

--- a/solution.py
+++ b/solution.py
@@ -50,6 +50,17 @@
     first = count_ends(ends, start)
     far = start + width
     return [jnp.minimum(end_of(ends, first + m, far) - start, width) for m in range(ENDS)]
+
+
+def slot_use(ends, slab, width):
+    start = slab * width
+    first = count_ends(ends, start)
+    segments = count_ends(ends, start + width - 1) - first + 1
+    begins = jnp.logical_or(start == 0, jnp.logical_and(first > 0, ends[jnp.maximum(first - 1, 0)] == start))
+    closed = end_of(ends, first + 1, start) == start + width
+    longer = 2 * (end_of(ends, first, start) - start) > width
+    of_first = jnp.logical_and(jnp.logical_not(begins), jnp.logical_or(closed, longer))
+    return segments, jnp.logical_or(segments == 1, of_first)
 
 
 def pick_rows(rows, bounds, options):
@@ -99,7 +110,9 @@
         for c in group:
             c.start()
     fetch_ends.wait()
-    bounds = slab_bounds(ends, lax.axis_index("seq"), width)
+    me = lax.axis_index("seq")
+    bounds = slab_bounds(ends, me, width)
+    segments, of_first = slot_use(ends, me, width)
     rows = rows_of((width, E))
     zero = jnp.zeros((width, E), f32)
     for h in range(heads):
@@ -115,8 +128,12 @@
             low = b
         sums = dot(k[:, at], jnp.concatenate(pieces, axis=1), 0, 0)
         mine = out.at[pl.ds(h * share, share)]
-        for m in range(PIECES):
-            store_parts(mine, m, sums[:, m * E : (m + 1) * E])
+        cuts = [sums[:, m * E : (m + 1) * E] for m in range(PIECES)]
+        source = jnp.where(of_first, cuts[0], cuts[1])
+        spare = source - source.astype(bf16).astype(f32)
+        store_parts(mine, 0, cuts[0])
+        store_parts(mine, 1, jnp.where(segments == 1, spare, cuts[1]))
+        store_parts(mine, 2, jnp.where(segments == PIECES, cuts[2], spare))
 
 
 def chain_kernel(ends, cand_prompt, parts, out, held, *, width):
@@ -132,13 +149,16 @@
             begins = jnp.logical_and(first > 0, begins)
         incoming = jnp.where(begins, 0.0, running)
         out[e, per_slab] = incoming.astype(bf16)
-        firsts = parts[e, 0].astype(f32) + incoming
+        segments, of_first = slot_use(ends, jnp.int32(e), width)
         second = parts[e, 1].astype(f32)
         third = parts[e, 2].astype(f32)
-        spare = ends.shape[0]
+        spare = jnp.where(segments == 1, second, jnp.where(segments == PIECES, 0.0, third))
+        firsts = incoming + (parts[e, 0].astype(f32) + jnp.where(of_first, spare, 0.0))
+        second = second + jnp.where(of_first, 0.0, spare)
+        nowhere = ends.shape[0]
         for m, piece in enumerate((firsts, second)):
             ended = end_of(ends, first + m, start + width + 1) <= start + width
-            held[jnp.where(ended, first + m, spare)] = piece
+            held[jnp.where(ended, first + m, nowhere)] = piece
         running = jnp.where(last == first, firsts, jnp.where(last == first + 1, second, third))
     for c in range(cand_prompt.shape[0]):
         out[c // per_slab, c % per_slab] = held[cand_prompt[c]].astype(bf16)
@@ -166,7 +186,7 @@
     return bounds
 
 
-def scores_kernel(lengths, q, inside, readout, states, slope_out, raw_out, slope_far, sems, *, scaling):
+def scores_kernel(lengths, q, inside, readout, states, slope_out, raw_out, *, scaling):
     width, flat = q.shape
     heads = flat // E
     per_slab = lengths.shape[1]
@@ -175,7 +195,6 @@
     zero = jnp.zeros((width, E), f32)
     inverse = [1.0 / jnp.full((1, E), lengths[0, j], jnp.int32).astype(f32) for j in range(per_slab)]
     totals = [jnp.zeros((1, E), f32) for j in range(per_slab)]
-    copies = []
     for h in range(heads):
         at = slice(h * E, (h + 1) * E)
         wide = [load_matrix(states, j, h, states.shape[0] // heads) for j in range(per_slab)]
@@ -185,9 +204,6 @@
         weight = pick_rows(rows, bounds, inverse) * readout[:, at]
         sigma = jax.nn.sigmoid(out)
         slope_out[:, at] = weight * sigma * (1.0 + out * (1.0 - sigma))
-        columns = pl.ds(h * E, E)
-        copies.append(pltpu.make_async_copy(slope_out.at[:, columns], slope_far.at[:, columns], sems.at[h]))
-        copies[-1].start()
         silu = out * sigma * weight
         low = 0
         for j, b in enumerate(bounds + [width]):
@@ -197,17 +213,27 @@
     raw_out[...] = jnp.zeros_like(raw_out)
     for j in range(per_slab):
         raw_out[j : j + 1] = jnp.broadcast_to(jnp.sum(totals[j], axis=1, keepdims=True), (1, E))
+
+
+def save_kernel(near, far, sems):
+    size = near.shape[0] // sems.shape[0]
+    some = [pl.ds(i * size, size) for i in range(sems.shape[0])]
+    copies = [pltpu.make_async_copy(near.at[a], far.at[a], sems.at[i]) for i, a in enumerate(some)]
+    for c in copies:
+        c.start()
     for c in copies:
         c.wait()
 
 
-def grads_kernel(lengths, q, slope, head, out, *, scaling):
+def grads_kernel(lengths, q, slope, head, out, sem, *, scaling):
     width, flat = q.shape
     heads = flat // E
     count = out.shape[0]
     share = count // heads
     size = flat // count
     per_slab = lengths.shape[1]
+    bring = pltpu.make_async_copy(head.at[:, 0], out.at[:, pl.ds(per_slab * size, size)], sem)
+    bring.start()
     bounds = cand_bounds(lengths)
     rows = rows_of((width, E))
     zero = jnp.zeros((width, E), f32)
@@ -228,8 +254,7 @@
             grad = (scaling * grad).astype(bf16)
             for o in range(share):
                 out[h * share + o, j * size : (j + 1) * size] = grad[o * size : (o + 1) * size]
-    for o in range(count):
-        out[o, per_slab * size : (per_slab + 1) * size] = head[o, 0]
+    bring.wait()
 
 
 def append_kernel(payload, *refs, per_slab):
@@ -352,7 +377,8 @@
         dq[lo:hi] = (scaling * block).astype(bf16)
 
 
-def prompt_kernel(ends, q, k, v, g, dq, dk, dv, head):
+def prompt_kernel(ends, q, k, v, g, *refs):
+    dq, dk, dv, head = refs[-4:]
     width = q.shape[0]
     scaling = 1.0 / math.sqrt(E * width)
     bounds = slab_bounds(ends, lax.axis_index("seq"), width)
@@ -492,15 +518,24 @@
     parts = exchange(pieces)
 
     pieces, late_in = lax.optimization_barrier((pieces, prompt_in))
-    dq_part, dk_part, dv_part, head_part = call(
-        prompt_kernel,
-        grid=(heads,),
-        in_specs=[SMEM] + [whole] * 4,
-        out_specs=[whole] * 3 + [parts_block(1)],
-        out_shape=[pltpu.HBM((width, flat), f32)] * 3 + [like((count, 1, rows, E), bf16)],
-        name="prompt",
-    )(prompt_ends, *hbm(*late_in))
-    parts, dq_part, dk_part, dv_part = lax.optimization_barrier((parts, dq_part, dk_part, dv_part))
+    late = max(1, heads // 4)
+    partial_shapes = [pltpu.HBM((width, flat), f32)] * 3 + [pltpu.HBM((count, 1, rows, E), bf16)]
+
+    def some_heads(from_head, how_many, arrays, held):
+        columns = pl.BlockSpec((width, E), lambda h: (0, h + from_head))
+        return call(
+            prompt_kernel,
+            grid=(how_many,),
+            in_specs=[SMEM] + [columns] * 4 + [ANY] * len(held),
+            out_specs=[columns] * 3
+            + [pl.BlockSpec((share, 1, rows, E), lambda h: (h + from_head, 0, 0, 0))],
+            out_shape=partial_shapes,
+            input_output_aliases={5 + i: i for i in range(len(held))},
+            name="prompt",
+        )(prompt_ends, *hbm(*arrays), *hbm(*held))
+
+    partials = some_heads(0, heads - late, late_in, [])
+    parts, partials = lax.optimization_barrier((parts, partials))
 
     chained = call(
         lambda *refs: chain_kernel(*refs, width=width),
@@ -522,17 +557,15 @@
         name="inside",
     )(cand_lengths, *hbm(*cand_in))
 
+    inside, partials, late_in = lax.optimization_barrier((inside, partials, late_in))
+    dq_part, dk_part, dv_part, head_part = some_heads(heads - late, late, late_in, partials)
+    states, head_part = lax.optimization_barrier((states, head_part))
     near_q = near(cand_in[0])[0]
-    slope, raw, slope_far = call(
+    slope, raw = call(
         lambda *refs: scores_kernel(*refs, scaling=scaling),
         in_specs=[SMEM] + [VMEM] * 4,
-        out_specs=[VMEM, VMEM, ANY],
-        out_shape=[
-            pltpu.VMEM((cand_width, flat), f32),
-            like((8, E), f32),
-            pltpu.HBM((cand_width, flat), f32),
-        ],
-        scratch_shapes=[pltpu.SemaphoreType.DMA((heads,))],
+        out_specs=[VMEM, VMEM],
+        out_shape=[pltpu.VMEM((cand_width, flat), f32), like((8, E), f32)],
         name="scores",
     )(cand_lengths, near_q, inside, readout.reshape(1, flat), states)
     raws = [raw]
@@ -541,11 +574,12 @@
     payload_shape = (count, (per_slab + 1) * rows + SCORE_ROWS, E)
     grads = call(
         lambda *refs: grads_kernel(*refs, scaling=scaling),
-        in_specs=[SMEM] + [VMEM] * 3,
+        in_specs=[SMEM, VMEM, VMEM, ANY],
         out_specs=VMEM,
         out_shape=pltpu.HBM(payload_shape, bf16),
+        scratch_shapes=[pltpu.SemaphoreType.DMA],
         name="grads",
-    )(cand_lengths, near_q, *near(slope), head_part)
+    )(cand_lengths, near_q, *near(slope), *hbm(head_part))
     grads = call(
         lambda *refs: append_kernel(*refs, per_slab=per_slab),
         in_specs=[ANY] + [VMEM] * groups,
@@ -557,7 +591,15 @@
     )(*hbm(grads), *raws)
     all_grads = exchange(grads)
 
-    grads, late_grad = lax.optimization_barrier((grads, prompt_grad))
+    grads, late_grad, slope = lax.optimization_barrier((grads, prompt_grad, slope))
+    slope_far = call(
+        save_kernel,
+        in_specs=[VMEM],
+        out_specs=ANY,
+        out_shape=pltpu.HBM((cand_width, flat), f32),
+        scratch_shapes=[pltpu.SemaphoreType.DMA((4,))],
+        name="save",
+    )(*near(slope))
     prompt_dq = call(
         query_kernel,
         grid=(heads,),
@@ -566,7 +608,7 @@
         out_shape=pltpu.HBM((width, flat), bf16),
         name="query",
     )(prompt_ends, *hbm(dq_part, late_grad), states)
-    all_grads, prompt_dq = lax.optimization_barrier((all_grads, prompt_dq))
+    all_grads, prompt_dq, slope_far = lax.optimization_barrier((all_grads, prompt_dq, slope_far))
 
     right, coef, loss = call(
         lambda *refs: listwise_kernel(*refs, width=width),

time: 87.6 us -> 85.5 us (0.976)
  Pallas kernels: 43.5 us -> 46.5 us
  waiting for transfers between devices: 20.2 us -> 17.3 us
  starting transfers between devices: 22.4 us -> 19.9 us
    pallas_call x2 -> x4, Pallas kernels: 13.6 us -> 17.2 us  [the longest x2 14 us: some_heads(): call(prompt_kernel, grid=(how_many,), in_specs=[SMEM] + [columns] * 4 + [...]
    all_to_all x4, waiting for transfers between devices: 19.3 us -> 16.7 us  [exchange(): return lax.all_to_all(a, 'seq', 0, 0, tiled=True)]
    all_to_all x4, starting transfers between devices: 20.6 us -> 18.2 us  [exchange(): return lax.all_to_all(a, 'seq', 0, 0, tiled=True)]
  transfers between devices with their start and end apart: 7 -> 7, of which waited for: 4 -> 5; matrix products, arithmetic and copies ran while one was open for 0% -> 0% of each run, Pallas kernels for 34% -> 39%
where the time goes in v6:
time: 85.5 us; the launch traced here: 84.7 us
  Pallas kernels  46.5 us (54%)
  starting transfers between devices  19.9 us (23%)
  waiting for transfers between devices  17.3 us (20%)
  between operations  0.93 us (1%)
    all_to_all x4, starting transfers between devices, exchange(): return lax.all_to_all(a, 'seq', 0, 0, tiled=True)  18.2 us
    all_to_all x4, waiting for transfers between devices, exchange(): return lax.all_to_all(a, 'seq', 0, 0, tiled=True)  16.7 us
    pallas_call x2, Pallas kernels, some_heads(): call(prompt_kernel, grid=(how_many,), in_specs=[SMEM] + [columns] * 4 + [...  14 us
    pallas_call x1, Pallas kernels, per_device(): call(lambda *refs: cand_kernel(*refs, scaling=scaling), grid=(heads,), in...  5.94 us
    pallas_call x1, Pallas kernels, per_device(): call(right_kernel, in_specs=[SMEM] + [VMEM] * 3 + [ANY] * 4, out_specs=[A...  4.39 us
    pallas_call x1, Pallas kernels, per_device(): call(query_kernel, grid=(heads,), in_specs=[SMEM, whole, whole, parts_blo...  4.22 us
    pallas_call x1, Pallas kernels, per_device(): call(inside_kernel, grid=(heads,), in_specs=[SMEM] + [cand_block] * 3, ou...  3.85 us
    pallas_call x1, Pallas kernels, per_device(): call(sums_kernel, in_specs=[ANY] * 3, out_specs=VMEM, out_shape=like((cou...  3.3 us
  transfers between devices with their start and end apart: 7, of which 5 were waited for; matrix products, arithmetic and copies ran while one was open for 0% of the time, Pallas kernels for 39%

profile of v6, /device:TPU:0, one launch (start us, length us, event | category | flops | bytes accessed | tf_op | source)
XLA Modules:
  0.0 84.7 jit_solution(12204151356276128640)
XLA Ops:
  0.6 0.0 copy-start.1
  0.6 3.3 %sums.1 = bf16[8,3,64,128]{3,2,1,0:T(8,128)(2,1)} custom-call(s32[8]{0:T(128)} %ends.7, bf16[1024,512]{1,0:T(8,128)(2,1)} %k_in.2, bf16[1024,512]{1,0:T(8,128)(2,1)} %v_in.2), custom_call_target="tpu_custom_call" | custom-call | tf_op jit(solution)/shard_map/sums/pallas_call | solution.py:508
  4.0 7.3 %all-to-all-start = ((bf16[8,3,64,128]{3,2,1,0:T(8,128)(2,1)}), bf16[8,3,64,128]{3,2,1,0:T(8,128)(2,1)S(1)}, u32[]{:S(2)}, u32[]{:S(2)}) async-start(bf16[8,3,64,128]{3,2,1,0:T(8,128)(2,1)} %sums.1), calls=%async_computation | async-start | bytes 786432 | tf_op jit(solution)/shard_map/all_to_all | solution.py:466
  11.2 0.0 copy-done.1
  11.2 0.0 copy-start.3
  11.2 0.0 copy-start.2
  11.2 9.3 %prompt.2 = (f32[1024,512]{1,0:T(8,128)}, f32[1024,512]{1,0:T(8,128)}, f32[1024,512]{1,0:T(8,128)}, bf16[8,1,64,128]{3,2,1,0:T(8,128)(2,1)}) custom-call(s32[8]{0:T(128)S(1)} %copy-done.1, bf16[1024,512]{1,0:T(8,128)(2,1)} %q.2, bf16[1024,512]{1,0:T(8,128)(2,1)} %k_in.2, bf16[1024,512]{1,0:T(8,128)(2,1)} %v_in.2, bf16[1024,512]{1,0:T(8,128)(2,1)} %g.2), custom_call_target="tpu_custom_call" | custom-call | tf_op jit(solution)/shard_map/prompt/pallas_call | solution.py:526
  20.5 2.4 %all-to-all-done.refs_2_ = bf16[8,3,64,128]{3,2,1,0:T(8,128)(2,1)S(1)} async-done(((bf16[8,3,64,128]{3,2,1,0:T(8,128)(2,1)}), bf16[8,3,64,128]{3,2,1,0:T(8,128)(2,1)S(1)}, u32[]{:S(2)}, u32[]{:S(2)}) %all-to-all-start) | async-done | bytes 393248 | tf_op jit(solution)/shard_map/all_to_all | solution.py:466
  22.9 0.0 copy-done.3
  22.9 1.6 %chain.1 = bf16[8,3,64,128]{3,2,1,0:T(8,128)(2,1)} custom-call(s32[8]{0:T(128)S(1)} %copy-done.1, s32[16]{0:T(128)S(1)} %copy-done.3, bf16[8,3,64,128]{3,2,1,0:T(8,128)(2,1)S(1)} %all-to-all-done.refs_2_), custom_call_target="tpu_custom_call" | custom-call | tf_op jit(solution)/shard_map/chain/pallas_call | solution.py:540
  24.5 3.6 %all-to-all-start.1 = ((bf16[8,3,64,128]{3,2,1,0:T(8,128)(2,1)}), bf16[8,3,64,128]{3,2,1,0:T(8,128)(2,1)S(1)}, u32[]{:S(2)}, u32[]{:S(2)}) async-start(bf16[8,3,64,128]{3,2,1,0:T(8,128)(2,1)} %chain.1), calls=%async_computation.1 | async-start | bytes 786432 | tf_op jit(solution)/shard_map/all_to_all | solution.py:466
  28.1 0.0 copy-done.2
  28.1 3.9 %inside.1.refs_2_ = f32[512,512]{1,0:T(8,128)S(1)} custom-call(s32[1,2]{1,0:T(1,128)S(1)} %copy-done.2, bf16[512,512]{1,0:T(8,128)(2,1)} %refs_2_, bf16[512,512]{1,0:T(8,128)(2,1)} %refs_3_, bf16[512,512]{1,0:T(8,128)(2,1)} %refs_4_), custom_call_target="tpu_custom_call" | custom-call | tf_op jit(solution)/shard_map/inside/pallas_call | solution.py:551
  32.0 0.0 copy-start
  32.0 0.0 copy-start.4
  32.0 4.7 %prompt.3 = (f32[1024,512]{1,0:T(8,128)}, f32[1024,512]{1,0:T(8,128)}, f32[1024,512]{1,0:T(8,128)}, bf16[8,1,64,128]{3,2,1,0:T(8,128)(2,1)}) custom-call(s32[8]{0:T(128)S(1)} %copy-done.1, bf16[1024,512]{1,0:T(8,128)(2,1)} %q.2, bf16[1024,512]{1,0:T(8,128)(2,1)} %k_in.2, ...), custom_call_target="tpu_custom_call", output_to_operand_aliasing={{0}: (5, {}), {1}: (6, {}), {2}: (7, {}), {3}: (8, {})} | custom-call | tf_op jit(solution)/shard_map/prompt/pallas_call | solution.py:526
  36.8 2.9 %all-to-all-done.1.refs_4_.states.refs_6_ = bf16[8,3,64,128]{3,2,1,0:T(8,128)(2,1)S(1)} async-done(((bf16[8,3,64,128]{3,2,1,0:T(8,128)(2,1)}), bf16[8,3,64,128]{3,2,1,0:T(8,128)(2,1)S(1)}, u32[]{:S(2)}, u32[]{:S(2)}) %all-to-all-start.1) | async-done | bytes 393248 | tf_op jit(solution)/shard_map/all_to_all | solution.py:466
  39.7 0.0 copy-done
  39.7 0.0 copy-done.4
  39.7 1.5 %scores.1 = (f32[512,512]{1,0:T(8,128)S(1)}, f32[8,128]{1,0:T(8,128)S(1)}) custom-call(s32[1,2]{1,0:T(1,128)S(1)} %copy-done.2, bf16[512,512]{1,0:T(8,128)(2,1)S(1)} %copy-done, f32[512,512]{1,0:T(8,128)S(1)} %inside.1.refs_2_, f32[1,512]{1,0:T(1,128)S(1)} %bitcast.6, bf16[8,3,64,128]{3,2,1,0:T(8,128)(2,1)S(1)} %all-to-all-done.1.refs_4_.states.refs_6_), custom_call_target="tpu_custom_call" | custom-call | tf_op jit(solution)/shard_map/scores/pallas_call | solution.py:564
  41.2 0.0 collective-permute-start.2
  41.2 1.6 %collective-permute-start.1 = (f32[8,128]{1,0:T(8,128)S(1)}, f32[8,128]{1,0:T(8,128)S(1)}, u32[]{:S(2)}, u32[]{:S(2)}) collective-permute-start(f32[8,128]{1,0:T(8,128)S(1)} %get-tuple-element.92.refs_1_), channel_id=1, source_target_pairs={{0,2},{1,3},{2,0},{3,1},{4,6},{5,7},{6,4},{7,5},{8,10},{9,11},{10,... | collective-permute-start | bytes 12296 | tf_op jit(solution)/shard_map/ppermute | solution.py:573
  42.8 0.2 collective-permute-start
  43.0 2.2 %grads.1.refs_0_ = bf16[8,208,128]{2,1,0:T(8,128)(2,1)} custom-call(s32[1,2]{1,0:T(1,128)S(1)} %copy-done.2, bf16[512,512]{1,0:T(8,128)(2,1)S(1)} %copy-done, f32[512,512]{1,0:T(8,128)S(1)} %get-tuple-element.95.refs_2_.near, bf16[8,1,64,128]{3,2,1,0:T(8,128)(2,1)} %get-tuple-element.91.refs_3_), custom_call_target="tpu_custom_call" | custom-call | tf_op jit(solution)/shard_map/grads/pallas_call | solution.py:575
  45.2 0.0 collective-permute-done.2.refs_4_
  45.2 0.0 collective-permute-done.1.refs_3_
  45.2 0.6 collective-permute-done.refs_2_
  45.8 0.7 append.1
  46.6 3.6 %all-to-all-start.2 = ((bf16[8,208,128]{2,1,0:T(8,128)(2,1)}), bf16[8,208,128]{2,1,0:T(8,128)(2,1)S(1)}, u32[]{:S(2)}, u32[]{:S(2)}) async-start(bf16[8,208,128]{2,1,0:T(8,128)(2,1)} %append.1), calls=%async_computation.2 | async-start | bytes 851968 | tf_op jit(solution)/shard_map/all_to_all | solution.py:466
  50.2 1.0 %save.1.refs_5_ = f32[512,512]{1,0:T(8,128)} custom-call(f32[512,512]{1,0:T(8,128)S(1)} %get-tuple-element.95.refs_2_.near), custom_call_target="tpu_custom_call" | custom-call | tf_op jit(solution)/shard_map/save/pallas_call | solution.py:595
  51.2 0.0 copy-start.5
  51.2 4.2 %query.1 = bf16[1024,512]{1,0:T(8,128)(2,1)} custom-call(s32[8]{0:T(128)S(1)} %copy-done.1, f32[1024,512]{1,0:T(8,128)} %get-tuple-element.93.part, bf16[1024,512]{1,0:T(8,128)(2,1)} %g.2, bf16[8,3,64,128]{3,2,1,0:T(8,128)(2,1)S(1)} %all-to-all-done.1.refs_4_.states.refs_6_), custom_call_target="tpu_custom_call" | custom-call | tf_op jit(solution)/shard_map/query/pallas_call | solution.py:603
  55.4 7.5 %all-to-all-done.2.refs_4_ = bf16[8,208,128]{2,1,0:T(8,128)(2,1)S(1)} async-done(((bf16[8,208,128]{2,1,0:T(8,128)(2,1)}), bf16[8,208,128]{2,1,0:T(8,128)(2,1)S(1)}, u32[]{:S(2)}, u32[]{:S(2)}) %all-to-all-start.2) | async-done | bytes 426016 | tf_op jit(solution)/shard_map/all_to_all | solution.py:466
  62.9 0.0 copy-done.5
  62.9 1.7 %listwise.1 = (bf16[8,3,64,128]{3,2,1,0:T(8,128)(2,1)}, f32[8,128]{1,0:T(8,128)S(1)}, f32[1,128]{1,0:T(1,128)}) custom-call(s32[8]{0:T(128)S(1)} %copy-done.1, s32[16]{0:T(128)S(1)} %copy-done.3, s32[1,16]{1,0:T(1,128)S(1)} %bitcast.5, s32[1,16]{1,0:T(1,128)S(1)} %bitcast.7, bf16[8,208,128]{2,1,0:T(8,128)(2,1)S(1)} %all-to-all-done.2.refs_4_), custom_call_target="tpu_custom_call" | custom-call | tf_op jit(solution)/shard_map/listwise/pallas_call | solution.py:613
  64.7 3.6 %all-to-all-start.3 = ((bf16[8,3,64,128]{3,2,1,0:T(8,128)(2,1)}), bf16[8,3,64,128]{3,2,1,0:T(8,128)(2,1)S(1)}, u32[]{:S(2)}, u32[]{:S(2)}) async-start(bf16[8,3,64,128]{3,2,1,0:T(8,128)(2,1)} %get-tuple-element.98), calls=%async_computation.3 | async-start | bytes 786432 | tf_op jit(solution)/shard_map/all_to_all | solution.py:466
  68.3 5.9 %cand.1 = (bf16[512,512]{1,0:T(8,128)(2,1)}, bf16[512,512]{1,0:T(8,128)(2,1)}, bf16[512,512]{1,0:T(8,128)(2,1)}) custom-call(s32[1,2]{1,0:T(1,128)S(1)} %copy-done.2, f32[8,128]{1,0:T(8,128)S(1)} %get-tuple-element.99.refs_1_, bf16[512,512]{1,0:T(8,128)(2,1)} %refs_2_, bf16[512,512]{1,0:T(8,128)(2,1)} %refs_3_, bf16[512,512]{1,0:T(8,128)(2,1)} %refs_4_, ...), custom_call_target="tpu_custom_call" | custom-call | tf_op jit(solution)/shard_map/cand/pallas_call | solution.py:637
  74.2 2.0 %stage.1 = (f32[2,1024,256]{2,1,0:T(8,128)S(1)}, bf16[2,1024,256]{2,1,0:T(8,128)(2,1)S(1)}) custom-call(f32[1024,512]{1,0:T(8,128)} %get-tuple-element.104.dk_part.dk_in, f32[1024,512]{1,0:T(8,128)} %get-tuple-element.105.dv_part.dv_in, bf16[1024,512]{1,0:T(8,128)(2,1)} %k_in.2, bf16[1024,512]{1,0:T(8,128)(2,1)} %v_in.2), custom_call_target="tpu_custom_call" | custom-call | tf_op jit(solution)/shard_map/stage/pallas_call | solution.py:649
  76.3 3.9 %all-to-all-done.3.states = bf16[8,3,64,128]{3,2,1,0:T(8,128)(2,1)S(1)} async-done(((bf16[8,3,64,128]{3,2,1,0:T(8,128)(2,1)}), bf16[8,3,64,128]{3,2,1,0:T(8,128)(2,1)S(1)}, u32[]{:S(2)}, u32[]{:S(2)}) %all-to-all-start.3) | async-done | bytes 393248 | tf_op jit(solution)/shard_map/all_to_all | solution.py:466
  80.2 4.4 %right.1 = (bf16[1024,512]{1,0:T(8,128)(2,1)}, bf16[1024,512]{1,0:T(8,128)(2,1)}) custom-call(s32[8]{0:T(128)S(1)} %copy-done.1, f32[2,1024,256]{2,1,0:T(8,128)S(1)} %get-tuple-element.110.partial, bf16[2,1024,256]{2,1,0:T(8,128)(2,1)S(1)} %get-tuple-element.111.both, bf16[8,3,64,128]{3,2,1,0:T(8,128)(2,1)S(1)} %all-to-all-done.3.states, ...), custom_call_target="tpu_custom_call" | custom-call | tf_op jit(solution)/shard_map/right/pallas_call | solution.py:659
Async XLA Ops:
  0.6 10.6 %copy-start.1 = (s32[8]{0:T(128)S(1)}, s32[8]{0:T(128)}, u32[]{:S(2)}) copy-start(s32[8]{0:T(128)} %ends.7) | copy-start | bytes 100
  4.0 18.9 %all-to-all-start = ((bf16[8,3,64,128]{3,2,1,0:T(8,128)(2,1)}), bf16[8,3,64,128]{3,2,1,0:T(8,128)(2,1)S(1)}, u32[]{:S(2)}, u32[]{:S(2)}) async-start(bf16[8,3,64,128]{3,2,1,0:T(8,128)(2,1)} %sums.1), calls=%async_computation | async-start | bytes 786432 | tf_op jit(solution)/shard_map/all_to_all | solution.py:466
  11.2 11.7 %copy-start.3 = (s32[16]{0:T(128)S(1)}, s32[16]{0:T(128)}, u32[]{:S(2)}) copy-start(s32[16]{0:T(128)} %refs_1_.5) | copy-start | bytes 196
  11.2 16.9 %copy-start.2 = (s32[1,2]{1,0:T(1,128)S(1)}, s32[1,2]{1,0:T(1,128)}, u32[]{:S(2)}) copy-start(s32[1,2]{1,0:T(1,128)} %refs_0_.9) | copy-start | bytes 28
  24.5 15.2 %all-to-all-start.1 = ((bf16[8,3,64,128]{3,2,1,0:T(8,128)(2,1)}), bf16[8,3,64,128]{3,2,1,0:T(8,128)(2,1)S(1)}, u32[]{:S(2)}, u32[]{:S(2)}) async-start(bf16[8,3,64,128]{3,2,1,0:T(8,128)(2,1)} %chain.1), calls=%async_computation.1 | async-start | bytes 786432 | tf_op jit(solution)/shard_map/all_to_all | solution.py:466
  32.0 7.7 %copy-start = (bf16[512,512]{1,0:T(8,128)(2,1)S(1)}, bf16[512,512]{1,0:T(8,128)(2,1)}, u32[]{:S(2)}) copy-start(bf16[512,512]{1,0:T(8,128)(2,1)} %refs_2_) | copy-start | bytes 1572868
  32.0 7.7 %copy-start.4 = (f32[512]{0:T(512)S(1)}, f32[512]{0:T(512)}, u32[]{:S(2)}) copy-start(f32[512]{0:T(512)} %param.19) | copy-start | bytes 6148
  41.2 4.0 %collective-permute-start.2 = (f32[8,128]{1,0:T(8,128)S(1)}, f32[8,128]{1,0:T(8,128)S(1)}, u32[]{:S(2)}, u32[]{:S(2)}) collective-permute-start(f32[8,128]{1,0:T(8,128)S(1)} %get-tuple-element.92.refs_1_), channel_id=1, source_target_pairs={{0,3},{1,0},{2,1},{3,2},{4,7},{5,4},{6,5},{7,6},{8,11},{9,8},{10,9... | collective-permute-start | bytes 12296 | tf_op jit(solution)/shard_map/ppermute | solution.py:573
  41.2 4.0 %collective-permute-start.1 = (f32[8,128]{1,0:T(8,128)S(1)}, f32[8,128]{1,0:T(8,128)S(1)}, u32[]{:S(2)}, u32[]{:S(2)}) collective-permute-start(f32[8,128]{1,0:T(8,128)S(1)} %get-tuple-element.92.refs_1_), channel_id=1, source_target_pairs={{0,2},{1,3},{2,0},{3,1},{4,6},{5,7},{6,4},{7,5},{8,10},{9,11},{10,... | collective-permute-start | bytes 12296 | tf_op jit(solution)/shard_map/ppermute | solution.py:573
  42.8 3.0 %collective-permute-start = (f32[8,128]{1,0:T(8,128)S(1)}, f32[8,128]{1,0:T(8,128)S(1)}, u32[]{:S(2)}, u32[]{:S(2)}) collective-permute-start(f32[8,128]{1,0:T(8,128)S(1)} %get-tuple-element.92.refs_1_), channel_id=1, source_target_pairs={{0,1},{1,2},{2,3},{3,0},{4,5},{5,6},{6,7},{7,4},{8,9},{9,10},{10,1... | collective-permute-start | bytes 12296 | tf_op jit(solution)/shard_map/ppermute | solution.py:573
  46.6 16.4 %all-to-all-start.2 = ((bf16[8,208,128]{2,1,0:T(8,128)(2,1)}), bf16[8,208,128]{2,1,0:T(8,128)(2,1)S(1)}, u32[]{:S(2)}, u32[]{:S(2)}) async-start(bf16[8,208,128]{2,1,0:T(8,128)(2,1)} %append.1), calls=%async_computation.2 | async-start | bytes 851968 | tf_op jit(solution)/shard_map/all_to_all | solution.py:466
  51.2 11.7 %copy-start.5 = (s32[16]{0:T(128)S(1)}, s32[16]{0:T(128)}, u32[]{:S(2)}) copy-start(s32[16]{0:T(128)} %param.23) | copy-start | bytes 196
  64.7 15.5 %all-to-all-start.3 = ((bf16[8,3,64,128]{3,2,1,0:T(8,128)(2,1)}), bf16[8,3,64,128]{3,2,1,0:T(8,128)(2,1)S(1)}, u32[]{:S(2)}, u32[]{:S(2)}) async-start(bf16[8,3,64,128]{3,2,1,0:T(8,128)(2,1)} %get-tuple-element.98), calls=%async_computation.3 | async-start | bytes 786432 | tf_op jit(solution)/shard_map/all_to_all | solution.py:466

commit v7 on v6

--- a/solution.py
+++ b/solution.py
@@ -225,36 +225,41 @@
         c.wait()
 
 
-def grads_kernel(lengths, q, slope, head, out, sem, *, scaling):
+def grads_kernel(lengths, q, slope, head, out, made, sems, *, scaling):
     width, flat = q.shape
     heads = flat // E
     count = out.shape[0]
     share = count // heads
     size = flat // count
     per_slab = lengths.shape[1]
-    bring = pltpu.make_async_copy(head.at[:, 0], out.at[:, pl.ds(per_slab * size, size)], sem)
-    bring.start()
+    copies = [pltpu.make_async_copy(head.at[:, 0], out.at[:, pl.ds(per_slab * size, size)], sems.at[heads])]
+    copies[0].start()
     bounds = cand_bounds(lengths)
     rows = rows_of((width, E))
-    zero = jnp.zeros((width, E), f32)
     for h in range(heads):
         at = slice(h * E, (h + 1) * E)
         mine = slope[:, at]
-        high, low_part = [], []
+        high = mine.astype(bf16)
+        low_part = (mine - high.astype(f32)).astype(bf16)
+        queries = q[:, at].astype(f32)
+        masked = []
         low = 0
         for b in bounds + [width]:
-            kept = jnp.where(jnp.logical_and(rows >= low, rows < b), mine, zero)
-            top = kept.astype(bf16)
-            high.append(top)
-            low_part.append((kept - top.astype(f32)).astype(bf16))
+            masked.append(jnp.where(jnp.logical_and(rows >= low, rows < b), queries, 0.0).astype(bf16))
             low = b
-        grads = dot(q[:, at], jnp.concatenate(high + low_part, axis=1), 0, 0)
+        grads = dot(jnp.concatenate(masked, axis=1), jnp.concatenate([high, low_part], axis=1), 0, 0)
+        grads = (scaling * (grads[:, :E] + grads[:, E:])).astype(bf16)
         for j in range(per_slab):
-            grad = grads[:, j * E : (j + 1) * E] + grads[:, (per_slab + j) * E : (per_slab + j + 1) * E]
-            grad = (scaling * grad).astype(bf16)
             for o in range(share):
-                out[h * share + o, j * size : (j + 1) * size] = grad[o * size : (o + 1) * size]
-    bring.wait()
+                start = j * E + o * size
+                made[h * share + o, j * size : (j + 1) * size] = grads[start : start + size]
+        some = pl.ds(h * share, share)
+        copies.append(
+            pltpu.make_async_copy(made.at[some], out.at[some, pl.ds(0, per_slab * size)], sems.at[h])
+        )
+        copies[-1].start()
+    for c in copies:
+        c.wait()
 
 
 def append_kernel(payload, *refs, per_slab):
@@ -291,6 +296,8 @@
     raw_held,
     coef_held,
     held,
+    made,
+    sems,
     *,
     width,
 ):
@@ -334,6 +341,7 @@
         j = c % per_slab
         held[prompts[c]] += grads[c // per_slab, j * size : (j + 1) * size].astype(f32) * coef[c : c + 1]
     running = jnp.zeros((size, E), f32)
+    copies = []
     for e in reversed(range(count)):
         start = e * width
         far = start + width
@@ -346,10 +354,14 @@
             pid = first + m
             ended = end_of(ends, pid, far + 1) <= far
             here = held[jnp.minimum(pid, prompt_count - 1)]
-            out[e, m] = jnp.where(ended, here, from_right).astype(bf16)
+            made[e, m] = jnp.where(ended, here, from_right).astype(bf16)
             if m == 0:
                 running = grads[e, per_slab * size : (per_slab + 1) * size].astype(f32) + jnp.where(ended, here, running)
-        out[e, ENDS] = from_right_bf
+        made[e, ENDS] = from_right_bf
+        copies.append(pltpu.make_async_copy(made.at[e], out.at[e], sems.at[e]))
+        copies[-1].start()
+    for c in copies:
+        c.wait()
 
 
 def cand_kernel(lengths, coef, q, k, v, slope, states, dq, dk, dv, *, scaling):
@@ -441,7 +453,6 @@
         waits.append(fetch([(a, b.at[:, at]) for a, b in pairs], pl.ds(h * E, E), sems, h * 4))
     bounds = slab_bounds(ends, lax.axis_index("seq"), width)
     rows = rows_of((width, E))
-    cut = lambda a: [a[:, m * E : (m + 1) * E] for m in range(PIECES)]
     copies = []
     for h in range(heads):
         near, kv, place = (partial, both, h) if h < ahead else (rest, rest_both, h - ahead)
@@ -449,11 +460,18 @@
         mine = slice(h * E, (h + 1) * E)
         for c in waits[h]:
             c.wait()
-        mats = [load_matrix(states, m, h, states.shape[0] // heads) for m in range(PIECES)]
-        by_v = dot(kv[1, :, at], jnp.concatenate(mats, axis=0), 1, 1)
-        dk[:, mine] = (near[0, :, at] + pick_rows(rows, bounds, cut(by_v))).astype(bf16)
-        by_k = dot(kv[0, :, at], jnp.concatenate(mats, axis=1), 1, 0)
-        dv[:, mine] = (near[1, :, at] + pick_rows(rows, bounds, cut(by_k))).astype(bf16)
+
+        def finish(pieces):
+            mats = [load_matrix(states, m, h, states.shape[0] // heads) for m in range(pieces)]
+            cut = lambda a: [a[:, m * E : (m + 1) * E] for m in range(pieces)]
+            some = bounds[: pieces - 1]
+            by_v = dot(kv[1, :, at], jnp.concatenate(mats, axis=0), 1, 1)
+            dk[:, mine] = (near[0, :, at] + pick_rows(rows, some, cut(by_v))).astype(bf16)
+            by_k = dot(kv[0, :, at], jnp.concatenate(mats, axis=1), 1, 0)
+            dv[:, mine] = (near[1, :, at] + pick_rows(rows, some, cut(by_k))).astype(bf16)
+
+        pl.when(bounds[-1] < width)(lambda: finish(PIECES))
+        pl.when(bounds[-1] >= width)(lambda: finish(PIECES - 1))
         columns = pl.ds(h * E, E)
         for i, (a, b) in enumerate(((dk, dk_out), (dv, dv_out))):
             copies.append(pltpu.make_async_copy(a.at[:, columns], b.at[:, columns], sems.at[(heads + h) * 4 + i]))
@@ -575,9 +593,12 @@
     grads = call(
         lambda *refs: grads_kernel(*refs, scaling=scaling),
         in_specs=[SMEM, VMEM, VMEM, ANY],
-        out_specs=VMEM,
+        out_specs=ANY,
         out_shape=pltpu.HBM(payload_shape, bf16),
-        scratch_shapes=[pltpu.SemaphoreType.DMA],
+        scratch_shapes=[
+            pltpu.VMEM((count, per_slab * rows, E), bf16),
+            pltpu.SemaphoreType.DMA((heads + 1,)),
+        ],
         name="grads",
     )(cand_lengths, near_q, *near(slope), *hbm(head_part))
     grads = call(
@@ -613,9 +634,9 @@
     right, coef, loss = call(
         lambda *refs: listwise_kernel(*refs, width=width),
         in_specs=[SMEM, SMEM] + [VMEM] * 3,
-        out_specs=[VMEM] * 3,
+        out_specs=[ANY, VMEM, VMEM],
         out_shape=[
-            like((count, PIECES, rows, E), bf16),
+            pltpu.HBM((count, PIECES, rows, E), bf16),
             like((8, E), f32),
             like((1, E), f32),
         ],
@@ -623,6 +644,8 @@
             pltpu.VMEM((cands, E), f32),
             pltpu.VMEM((cands, E), f32),
             pltpu.VMEM((prompt_ends.shape[0], rows, E), f32),
+            pltpu.VMEM((count, PIECES, rows, E), bf16),
+            pltpu.SemaphoreType.DMA((count,)),
         ],
         name="listwise",
     )(

time: 85.5 us -> 89.4 us (1.046)
  Pallas kernels: 46.5 us -> 50.3 us
    pallas_call x1, Pallas kernels: 2.22 us -> 5.66 us  [per_device(): call(lambda *refs: grads_kernel(*refs, scaling=scaling), in_specs=[SMEM,...]
  transfers between devices with their start and end apart: 7 -> 7, of which waited for: 5 -> 4; matrix products, arithmetic and copies ran while one was open for 0% -> 0% of each run, Pallas kernels for 39% -> 41%
where the time goes in v7:
time: 89.4 us; the launch traced here: 88.6 us
  Pallas kernels  50.3 us (56%)
  starting transfers between devices  20 us (22%)
  waiting for transfers between devices  17.4 us (19%)
  between operations  0.94 us (1%)
    all_to_all x4, starting transfers between devices, exchange(): return lax.all_to_all(a, 'seq', 0, 0, tiled=True)  18.2 us
    all_to_all x4, waiting for transfers between devices, exchange(): return lax.all_to_all(a, 'seq', 0, 0, tiled=True)  17.4 us
    pallas_call x2, Pallas kernels, some_heads(): call(prompt_kernel, grid=(how_many,), in_specs=[SMEM] + [columns] * 4 + [...  14 us
    pallas_call x1, Pallas kernels, per_device(): call(lambda *refs: cand_kernel(*refs, scaling=scaling), grid=(heads,), in...  5.92 us
    pallas_call x1, Pallas kernels, per_device(): call(lambda *refs: grads_kernel(*refs, scaling=scaling), in_specs=[SMEM,...  5.66 us
    pallas_call x1, Pallas kernels, per_device(): call(right_kernel, in_specs=[SMEM] + [VMEM] * 3 + [ANY] * 4, out_specs=[A...  4.31 us
    pallas_call x1, Pallas kernels, per_device(): call(query_kernel, grid=(heads,), in_specs=[SMEM, whole, whole, parts_blo...  4.22 us
    pallas_call x1, Pallas kernels, per_device(): call(inside_kernel, grid=(heads,), in_specs=[SMEM] + [cand_block] * 3, ou...  3.85 us
  transfers between devices with their start and end apart: 7, of which 4 were waited for; matrix products, arithmetic and copies ran while one was open for 0% of the time, Pallas kernels for 41%

profile of v7, /device:TPU:0, one launch (start us, length us, event | category | flops | bytes accessed | tf_op | source)
XLA Modules:
  0.0 88.6 jit_solution(7193758546290025937)
XLA Ops:
  0.6 0.0 copy-start.1
  0.6 3.3 %sums.1 = bf16[8,3,64,128]{3,2,1,0:T(8,128)(2,1)} custom-call(s32[8]{0:T(128)} %ends.7, bf16[1024,512]{1,0:T(8,128)(2,1)} %k_in.2, bf16[1024,512]{1,0:T(8,128)(2,1)} %v_in.2), custom_call_target="tpu_custom_call" | custom-call | tf_op jit(solution)/shard_map/sums/pallas_call | solution.py:526
  4.0 7.3 %all-to-all-start = ((bf16[8,3,64,128]{3,2,1,0:T(8,128)(2,1)}), bf16[8,3,64,128]{3,2,1,0:T(8,128)(2,1)S(1)}, u32[]{:S(2)}, u32[]{:S(2)}) async-start(bf16[8,3,64,128]{3,2,1,0:T(8,128)(2,1)} %sums.1), calls=%async_computation | async-start | bytes 786432 | tf_op jit(solution)/shard_map/all_to_all | solution.py:484
  11.2 0.0 copy-done.1
  11.2 0.0 copy-start.3
  11.2 0.0 copy-start.2
  11.2 9.3 %prompt.2 = (f32[1024,512]{1,0:T(8,128)}, f32[1024,512]{1,0:T(8,128)}, f32[1024,512]{1,0:T(8,128)}, bf16[8,1,64,128]{3,2,1,0:T(8,128)(2,1)}) custom-call(s32[8]{0:T(128)S(1)} %copy-done.1, bf16[1024,512]{1,0:T(8,128)(2,1)} %q.2, bf16[1024,512]{1,0:T(8,128)(2,1)} %k_in.2, bf16[1024,512]{1,0:T(8,128)(2,1)} %v_in.2, bf16[1024,512]{1,0:T(8,128)(2,1)} %g.2), custom_call_target="tpu_custom_call" | custom-call | tf_op jit(solution)/shard_map/prompt/pallas_call | solution.py:544
  20.5 2.4 %all-to-all-done.refs_2_ = bf16[8,3,64,128]{3,2,1,0:T(8,128)(2,1)S(1)} async-done(((bf16[8,3,64,128]{3,2,1,0:T(8,128)(2,1)}), bf16[8,3,64,128]{3,2,1,0:T(8,128)(2,1)S(1)}, u32[]{:S(2)}, u32[]{:S(2)}) %all-to-all-start) | async-done | bytes 393248 | tf_op jit(solution)/shard_map/all_to_all | solution.py:484
  22.9 0.0 copy-done.3
  22.9 1.6 %chain.1 = bf16[8,3,64,128]{3,2,1,0:T(8,128)(2,1)} custom-call(s32[8]{0:T(128)S(1)} %copy-done.1, s32[16]{0:T(128)S(1)} %copy-done.3, bf16[8,3,64,128]{3,2,1,0:T(8,128)(2,1)S(1)} %all-to-all-done.refs_2_), custom_call_target="tpu_custom_call" | custom-call | tf_op jit(solution)/shard_map/chain/pallas_call | solution.py:558
  24.5 3.6 %all-to-all-start.1 = ((bf16[8,3,64,128]{3,2,1,0:T(8,128)(2,1)}), bf16[8,3,64,128]{3,2,1,0:T(8,128)(2,1)S(1)}, u32[]{:S(2)}, u32[]{:S(2)}) async-start(bf16[8,3,64,128]{3,2,1,0:T(8,128)(2,1)} %chain.1), calls=%async_computation.1 | async-start | bytes 786432 | tf_op jit(solution)/shard_map/all_to_all | solution.py:484
  28.1 0.0 copy-done.2
  28.1 3.9 %inside.1.refs_2_ = f32[512,512]{1,0:T(8,128)S(1)} custom-call(s32[1,2]{1,0:T(1,128)S(1)} %copy-done.2, bf16[512,512]{1,0:T(8,128)(2,1)} %refs_2_, bf16[512,512]{1,0:T(8,128)(2,1)} %refs_3_, bf16[512,512]{1,0:T(8,128)(2,1)} %refs_4_), custom_call_target="tpu_custom_call" | custom-call | tf_op jit(solution)/shard_map/inside/pallas_call | solution.py:569
  32.0 0.0 copy-start
  32.0 0.0 copy-start.4
  32.0 4.7 %prompt.3 = (f32[1024,512]{1,0:T(8,128)}, f32[1024,512]{1,0:T(8,128)}, f32[1024,512]{1,0:T(8,128)}, bf16[8,1,64,128]{3,2,1,0:T(8,128)(2,1)}) custom-call(s32[8]{0:T(128)S(1)} %copy-done.1, bf16[1024,512]{1,0:T(8,128)(2,1)} %q.2, bf16[1024,512]{1,0:T(8,128)(2,1)} %k_in.2, ...), custom_call_target="tpu_custom_call", output_to_operand_aliasing={{0}: (5, {}), {1}: (6, {}), {2}: (7, {}), {3}: (8, {})} | custom-call | tf_op jit(solution)/shard_map/prompt/pallas_call | solution.py:544
  36.8 2.9 %all-to-all-done.1.refs_4_.states.refs_6_ = bf16[8,3,64,128]{3,2,1,0:T(8,128)(2,1)S(1)} async-done(((bf16[8,3,64,128]{3,2,1,0:T(8,128)(2,1)}), bf16[8,3,64,128]{3,2,1,0:T(8,128)(2,1)S(1)}, u32[]{:S(2)}, u32[]{:S(2)}) %all-to-all-start.1) | async-done | bytes 393248 | tf_op jit(solution)/shard_map/all_to_all | solution.py:484
  39.7 0.0 copy-done
  39.7 0.0 copy-done.4
  39.7 1.5 %scores.1 = (f32[512,512]{1,0:T(8,128)S(1)}, f32[8,128]{1,0:T(8,128)S(1)}) custom-call(s32[1,2]{1,0:T(1,128)S(1)} %copy-done.2, bf16[512,512]{1,0:T(8,128)(2,1)S(1)} %copy-done, f32[512,512]{1,0:T(8,128)S(1)} %inside.1.refs_2_, f32[1,512]{1,0:T(1,128)S(1)} %bitcast.6, bf16[8,3,64,128]{3,2,1,0:T(8,128)(2,1)S(1)} %all-to-all-done.1.refs_4_.states.refs_6_), custom_call_target="tpu_custom_call" | custom-call | tf_op jit(solution)/shard_map/scores/pallas_call | solution.py:582
  41.2 0.0 collective-permute-start.2
  41.2 1.6 %collective-permute-start.1 = (f32[8,128]{1,0:T(8,128)S(1)}, f32[8,128]{1,0:T(8,128)S(1)}, u32[]{:S(2)}, u32[]{:S(2)}) collective-permute-start(f32[8,128]{1,0:T(8,128)S(1)} %get-tuple-element.92.refs_1_), channel_id=1, source_target_pairs={{0,2},{1,3},{2,0},{3,1},{4,6},{5,7},{6,4},{7,5},{8,10},{9,11},{10,... | collective-permute-start | bytes 12296 | tf_op jit(solution)/shard_map/ppermute | solution.py:591
  42.8 0.2 collective-permute-start
  43.0 5.7 %grads.1.refs_0_ = bf16[8,208,128]{2,1,0:T(8,128)(2,1)} custom-call(s32[1,2]{1,0:T(1,128)S(1)} %copy-done.2, bf16[512,512]{1,0:T(8,128)(2,1)S(1)} %copy-done, f32[512,512]{1,0:T(8,128)S(1)} %get-tuple-element.95.refs_2_.near, bf16[8,1,64,128]{3,2,1,0:T(8,128)(2,1)} %get-tuple-element.91.refs_3_), custom_call_target="tpu_custom_call" | custom-call | tf_op jit(solution)/shard_map/grads/pallas_call | solution.py:593
  48.7 0.0 collective-permute-done.2.refs_4_
  48.7 0.0 collective-permute-done.1.refs_3_
  48.7 0.0 collective-permute-done.refs_2_
  48.7 0.7 append.1
  49.4 3.6 %all-to-all-start.2 = ((bf16[8,208,128]{2,1,0:T(8,128)(2,1)}), bf16[8,208,128]{2,1,0:T(8,128)(2,1)S(1)}, u32[]{:S(2)}, u32[]{:S(2)}) async-start(bf16[8,208,128]{2,1,0:T(8,128)(2,1)} %append.1), calls=%async_computation.2 | async-start | bytes 851968 | tf_op jit(solution)/shard_map/all_to_all | solution.py:484
  53.1 1.0 %save.1.refs_5_ = f32[512,512]{1,0:T(8,128)} custom-call(f32[512,512]{1,0:T(8,128)S(1)} %get-tuple-element.95.refs_2_.near), custom_call_target="tpu_custom_call" | custom-call | tf_op jit(solution)/shard_map/save/pallas_call | solution.py:616
  54.1 0.0 copy-start.5
  54.1 4.2 %query.1 = bf16[1024,512]{1,0:T(8,128)(2,1)} custom-call(s32[8]{0:T(128)S(1)} %copy-done.1, f32[1024,512]{1,0:T(8,128)} %get-tuple-element.93.part, bf16[1024,512]{1,0:T(8,128)(2,1)} %g.2, bf16[8,3,64,128]{3,2,1,0:T(8,128)(2,1)S(1)} %all-to-all-done.1.refs_4_.states.refs_6_), custom_call_target="tpu_custom_call" | custom-call | tf_op jit(solution)/shard_map/query/pallas_call | solution.py:624
  58.3 8.1 %all-to-all-done.2.refs_4_ = bf16[8,208,128]{2,1,0:T(8,128)(2,1)S(1)} async-done(((bf16[8,208,128]{2,1,0:T(8,128)(2,1)}), bf16[8,208,128]{2,1,0:T(8,128)(2,1)S(1)}, u32[]{:S(2)}, u32[]{:S(2)}) %all-to-all-start.2) | async-done | bytes 426016 | tf_op jit(solution)/shard_map/all_to_all | solution.py:484
  66.4 0.0 copy-done.5
  66.4 2.2 %listwise.1 = (bf16[8,3,64,128]{3,2,1,0:T(8,128)(2,1)}, f32[8,128]{1,0:T(8,128)S(1)}, f32[1,128]{1,0:T(1,128)}) custom-call(s32[8]{0:T(128)S(1)} %copy-done.1, s32[16]{0:T(128)S(1)} %copy-done.3, s32[1,16]{1,0:T(1,128)S(1)} %bitcast.5, s32[1,16]{1,0:T(1,128)S(1)} %bitcast.7, bf16[8,208,128]{2,1,0:T(8,128)(2,1)S(1)} %all-to-all-done.2.refs_4_), custom_call_target="tpu_custom_call" | custom-call | tf_op jit(solution)/shard_map/listwise/pallas_call | solution.py:634
  68.6 3.6 %all-to-all-start.3 = ((bf16[8,3,64,128]{3,2,1,0:T(8,128)(2,1)}), bf16[8,3,64,128]{3,2,1,0:T(8,128)(2,1)S(1)}, u32[]{:S(2)}, u32[]{:S(2)}) async-start(bf16[8,3,64,128]{3,2,1,0:T(8,128)(2,1)} %get-tuple-element.98), calls=%async_computation.3 | async-start | bytes 786432 | tf_op jit(solution)/shard_map/all_to_all | solution.py:484
  72.2 5.9 %cand.1 = (bf16[512,512]{1,0:T(8,128)(2,1)}, bf16[512,512]{1,0:T(8,128)(2,1)}, bf16[512,512]{1,0:T(8,128)(2,1)}) custom-call(s32[1,2]{1,0:T(1,128)S(1)} %copy-done.2, f32[8,128]{1,0:T(8,128)S(1)} %get-tuple-element.99.refs_1_, bf16[512,512]{1,0:T(8,128)(2,1)} %refs_2_, bf16[512,512]{1,0:T(8,128)(2,1)} %refs_3_, bf16[512,512]{1,0:T(8,128)(2,1)} %refs_4_, ...), custom_call_target="tpu_custom_call" | custom-call | tf_op jit(solution)/shard_map/cand/pallas_call | solution.py:660
  78.1 2.0 %stage.1 = (f32[2,1024,256]{2,1,0:T(8,128)S(1)}, bf16[2,1024,256]{2,1,0:T(8,128)(2,1)S(1)}) custom-call(f32[1024,512]{1,0:T(8,128)} %get-tuple-element.104.dk_part.dk_in, f32[1024,512]{1,0:T(8,128)} %get-tuple-element.105.dv_part.dv_in, bf16[1024,512]{1,0:T(8,128)(2,1)} %k_in.2, bf16[1024,512]{1,0:T(8,128)(2,1)} %v_in.2), custom_call_target="tpu_custom_call" | custom-call | tf_op jit(solution)/shard_map/stage/pallas_call | solution.py:672
  80.2 4.0 %all-to-all-done.3.states = bf16[8,3,64,128]{3,2,1,0:T(8,128)(2,1)S(1)} async-done(((bf16[8,3,64,128]{3,2,1,0:T(8,128)(2,1)}), bf16[8,3,64,128]{3,2,1,0:T(8,128)(2,1)S(1)}, u32[]{:S(2)}, u32[]{:S(2)}) %all-to-all-start.3) | async-done | bytes 393248 | tf_op jit(solution)/shard_map/all_to_all | solution.py:484
  84.1 4.3 %right.1 = (bf16[1024,512]{1,0:T(8,128)(2,1)}, bf16[1024,512]{1,0:T(8,128)(2,1)}) custom-call(s32[8]{0:T(128)S(1)} %copy-done.1, f32[2,1024,256]{2,1,0:T(8,128)S(1)} %get-tuple-element.110.partial, bf16[2,1024,256]{2,1,0:T(8,128)(2,1)S(1)} %get-tuple-element.111.both, bf16[8,3,64,128]{3,2,1,0:T(8,128)(2,1)S(1)} %all-to-all-done.3.states, ...), custom_call_target="tpu_custom_call" | custom-call | tf_op jit(solution)/shard_map/right/pallas_call | solution.py:682
Async XLA Ops:
  0.6 10.6 %copy-start.1 = (s32[8]{0:T(128)S(1)}, s32[8]{0:T(128)}, u32[]{:S(2)}) copy-start(s32[8]{0:T(128)} %ends.7) | copy-start | bytes 100
  4.0 18.9 %all-to-all-start = ((bf16[8,3,64,128]{3,2,1,0:T(8,128)(2,1)}), bf16[8,3,64,128]{3,2,1,0:T(8,128)(2,1)S(1)}, u32[]{:S(2)}, u32[]{:S(2)}) async-start(bf16[8,3,64,128]{3,2,1,0:T(8,128)(2,1)} %sums.1), calls=%async_computation | async-start | bytes 786432 | tf_op jit(solution)/shard_map/all_to_all | solution.py:484
  11.2 11.7 %copy-start.3 = (s32[16]{0:T(128)S(1)}, s32[16]{0:T(128)}, u32[]{:S(2)}) copy-start(s32[16]{0:T(128)} %refs_1_.5) | copy-start | bytes 196
  11.2 16.9 %copy-start.2 = (s32[1,2]{1,0:T(1,128)S(1)}, s32[1,2]{1,0:T(1,128)}, u32[]{:S(2)}) copy-start(s32[1,2]{1,0:T(1,128)} %refs_0_.9) | copy-start | bytes 28
  24.5 15.2 %all-to-all-start.1 = ((bf16[8,3,64,128]{3,2,1,0:T(8,128)(2,1)}), bf16[8,3,64,128]{3,2,1,0:T(8,128)(2,1)S(1)}, u32[]{:S(2)}, u32[]{:S(2)}) async-start(bf16[8,3,64,128]{3,2,1,0:T(8,128)(2,1)} %chain.1), calls=%async_computation.1 | async-start | bytes 786432 | tf_op jit(solution)/shard_map/all_to_all | solution.py:484
  32.0 7.7 %copy-start = (bf16[512,512]{1,0:T(8,128)(2,1)S(1)}, bf16[512,512]{1,0:T(8,128)(2,1)}, u32[]{:S(2)}) copy-start(bf16[512,512]{1,0:T(8,128)(2,1)} %refs_2_) | copy-start | bytes 1572868
  32.0 7.7 %copy-start.4 = (f32[512]{0:T(512)S(1)}, f32[512]{0:T(512)}, u32[]{:S(2)}) copy-start(f32[512]{0:T(512)} %param.19) | copy-start | bytes 6148
  41.2 7.5 %collective-permute-start.2 = (f32[8,128]{1,0:T(8,128)S(1)}, f32[8,128]{1,0:T(8,128)S(1)}, u32[]{:S(2)}, u32[]{:S(2)}) collective-permute-start(f32[8,128]{1,0:T(8,128)S(1)} %get-tuple-element.92.refs_1_), channel_id=1, source_target_pairs={{0,3},{1,0},{2,1},{3,2},{4,7},{5,4},{6,5},{7,6},{8,11},{9,8},{10,9... | collective-permute-start | bytes 12296 | tf_op jit(solution)/shard_map/ppermute | solution.py:591
  41.2 7.5 %collective-permute-start.1 = (f32[8,128]{1,0:T(8,128)S(1)}, f32[8,128]{1,0:T(8,128)S(1)}, u32[]{:S(2)}, u32[]{:S(2)}) collective-permute-start(f32[8,128]{1,0:T(8,128)S(1)} %get-tuple-element.92.refs_1_), channel_id=1, source_target_pairs={{0,2},{1,3},{2,0},{3,1},{4,6},{5,7},{6,4},{7,5},{8,10},{9,11},{10,... | collective-permute-start | bytes 12296 | tf_op jit(solution)/shard_map/ppermute | solution.py:591
  42.8 5.9 %collective-permute-start = (f32[8,128]{1,0:T(8,128)S(1)}, f32[8,128]{1,0:T(8,128)S(1)}, u32[]{:S(2)}, u32[]{:S(2)}) collective-permute-start(f32[8,128]{1,0:T(8,128)S(1)} %get-tuple-element.92.refs_1_), channel_id=1, source_target_pairs={{0,1},{1,2},{2,3},{3,0},{4,5},{5,6},{6,7},{7,4},{8,9},{9,10},{10,1... | collective-permute-start | bytes 12296 | tf_op jit(solution)/shard_map/ppermute | solution.py:591
  49.4 17.0 %all-to-all-start.2 = ((bf16[8,208,128]{2,1,0:T(8,128)(2,1)}), bf16[8,208,128]{2,1,0:T(8,128)(2,1)S(1)}, u32[]{:S(2)}, u32[]{:S(2)}) async-start(bf16[8,208,128]{2,1,0:T(8,128)(2,1)} %append.1), calls=%async_computation.2 | async-start | bytes 851968 | tf_op jit(solution)/shard_map/all_to_all | solution.py:484
  54.1 12.3 %copy-start.5 = (s32[16]{0:T(128)S(1)}, s32[16]{0:T(128)}, u32[]{:S(2)}) copy-start(s32[16]{0:T(128)} %param.23) | copy-start | bytes 196
  68.6 15.6 %all-to-all-start.3 = ((bf16[8,3,64,128]{3,2,1,0:T(8,128)(2,1)}), bf16[8,3,64,128]{3,2,1,0:T(8,128)(2,1)S(1)}, u32[]{:S(2)}, u32[]{:S(2)}) async-start(bf16[8,3,64,128]{3,2,1,0:T(8,128)(2,1)} %get-tuple-element.98), calls=%async_computation.3 | async-start | bytes 786432 | tf_op jit(solution)/shard_map/all_to_all | solution.py:484

commit v8 on v6

--- a/solution.py
+++ b/solution.py
@@ -236,24 +236,23 @@
     bring.start()
     bounds = cand_bounds(lengths)
     rows = rows_of((width, E))
-    zero = jnp.zeros((width, E), f32)
     for h in range(heads):
         at = slice(h * E, (h + 1) * E)
         mine = slope[:, at]
-        high, low_part = [], []
+        high = mine.astype(bf16)
+        low_part = (mine - high.astype(f32)).astype(bf16)
+        queries = q[:, at].astype(f32)
+        masked = []
         low = 0
         for b in bounds + [width]:
-            kept = jnp.where(jnp.logical_and(rows >= low, rows < b), mine, zero)
-            top = kept.astype(bf16)
-            high.append(top)
-            low_part.append((kept - top.astype(f32)).astype(bf16))
+            masked.append(jnp.where(jnp.logical_and(rows >= low, rows < b), queries, 0.0).astype(bf16))
             low = b
-        grads = dot(q[:, at], jnp.concatenate(high + low_part, axis=1), 0, 0)
+        grads = dot(jnp.concatenate(masked, axis=1), jnp.concatenate([high, low_part], axis=1), 0, 0)
+        grads = (scaling * (grads[:, :E] + grads[:, E:])).astype(bf16)
         for j in range(per_slab):
-            grad = grads[:, j * E : (j + 1) * E] + grads[:, (per_slab + j) * E : (per_slab + j + 1) * E]
-            grad = (scaling * grad).astype(bf16)
             for o in range(share):
-                out[h * share + o, j * size : (j + 1) * size] = grad[o * size : (o + 1) * size]
+                start = j * E + o * size
+                out[h * share + o, j * size : (j + 1) * size] = grads[start : start + size]
     bring.wait()
 
 
@@ -441,7 +440,6 @@
         waits.append(fetch([(a, b.at[:, at]) for a, b in pairs], pl.ds(h * E, E), sems, h * 4))
     bounds = slab_bounds(ends, lax.axis_index("seq"), width)
     rows = rows_of((width, E))
-    cut = lambda a: [a[:, m * E : (m + 1) * E] for m in range(PIECES)]
     copies = []
     for h in range(heads):
         near, kv, place = (partial, both, h) if h < ahead else (rest, rest_both, h - ahead)
@@ -449,11 +447,18 @@
         mine = slice(h * E, (h + 1) * E)
         for c in waits[h]:
             c.wait()
-        mats = [load_matrix(states, m, h, states.shape[0] // heads) for m in range(PIECES)]
-        by_v = dot(kv[1, :, at], jnp.concatenate(mats, axis=0), 1, 1)
-        dk[:, mine] = (near[0, :, at] + pick_rows(rows, bounds, cut(by_v))).astype(bf16)
-        by_k = dot(kv[0, :, at], jnp.concatenate(mats, axis=1), 1, 0)
-        dv[:, mine] = (near[1, :, at] + pick_rows(rows, bounds, cut(by_k))).astype(bf16)
+
+        def finish(pieces):
+            mats = [load_matrix(states, m, h, states.shape[0] // heads) for m in range(pieces)]
+            cut = lambda a: [a[:, m * E : (m + 1) * E] for m in range(pieces)]
+            some = bounds[: pieces - 1]
+            by_v = dot(kv[1, :, at], jnp.concatenate(mats, axis=0), 1, 1)
+            dk[:, mine] = (near[0, :, at] + pick_rows(rows, some, cut(by_v))).astype(bf16)
+            by_k = dot(kv[0, :, at], jnp.concatenate(mats, axis=1), 1, 0)
+            dv[:, mine] = (near[1, :, at] + pick_rows(rows, some, cut(by_k))).astype(bf16)
+
+        pl.when(bounds[-1] < width)(lambda: finish(PIECES))
+        pl.when(bounds[-1] >= width)(lambda: finish(PIECES - 1))
         columns = pl.ds(h * E, E)
         for i, (a, b) in enumerate(((dk, dk_out), (dv, dv_out))):
             copies.append(pltpu.make_async_copy(a.at[:, columns], b.at[:, columns], sems.at[(heads + h) * 4 + i]))

time: 85.5 us -> 85.2 us (level)
  no operation moved by 1% of the time
where the time goes in v8:
time: 85.2 us; the launch traced here: 84.4 us
  Pallas kernels  46.3 us (54%)
  starting transfers between devices  19.9 us (23%)
  waiting for transfers between devices  17.4 us (20%)
    all_to_all x4, starting transfers between devices, exchange(): return lax.all_to_all(a, 'seq', 0, 0, tiled=True)  18.2 us
    all_to_all x4, waiting for transfers between devices, exchange(): return lax.all_to_all(a, 'seq', 0, 0, tiled=True)  16.8 us
    pallas_call x2, Pallas kernels, some_heads(): call(prompt_kernel, grid=(how_many,), in_specs=[SMEM] + [columns] * 4 + [...  14 us
    pallas_call x1, Pallas kernels, per_device(): call(lambda *refs: cand_kernel(*refs, scaling=scaling), grid=(heads,), in...  5.92 us
    pallas_call x1, Pallas kernels, per_device(): call(right_kernel, in_specs=[SMEM] + [VMEM] * 3 + [ANY] * 4, out_specs=[A...  4.27 us
    pallas_call x1, Pallas kernels, per_device(): call(query_kernel, grid=(heads,), in_specs=[SMEM, whole, whole, parts_blo...  4.22 us
    pallas_call x1, Pallas kernels, per_device(): call(inside_kernel, grid=(heads,), in_specs=[SMEM] + [cand_block] * 3, ou...  3.85 us
    pallas_call x1, Pallas kernels, per_device(): call(sums_kernel, in_specs=[ANY] * 3, out_specs=VMEM, out_shape=like((cou...  3.3 us
  transfers between devices with their start and end apart: 7, of which 5 were waited for; matrix products, arithmetic and copies ran while one was open for 0% of the time, Pallas kernels for 39%

profile of v8, /device:TPU:0, one launch (start us, length us, event | category | flops | bytes accessed | tf_op | source)
XLA Modules:
  0.0 84.4 jit_solution(16984132210008796988)
XLA Ops:
  0.6 0.0 copy-start.1
  0.6 3.3 %sums.1 = bf16[8,3,64,128]{3,2,1,0:T(8,128)(2,1)} custom-call(s32[8]{0:T(128)} %ends.7, bf16[1024,512]{1,0:T(8,128)(2,1)} %k_in.2, bf16[1024,512]{1,0:T(8,128)(2,1)} %v_in.2), custom_call_target="tpu_custom_call" | custom-call | tf_op jit(solution)/shard_map/sums/pallas_call | solution.py:513
  4.0 7.3 %all-to-all-start = ((bf16[8,3,64,128]{3,2,1,0:T(8,128)(2,1)}), bf16[8,3,64,128]{3,2,1,0:T(8,128)(2,1)S(1)}, u32[]{:S(2)}, u32[]{:S(2)}) async-start(bf16[8,3,64,128]{3,2,1,0:T(8,128)(2,1)} %sums.1), calls=%async_computation | async-start | bytes 786432 | tf_op jit(solution)/shard_map/all_to_all | solution.py:471
  11.2 0.0 copy-done.1
  11.2 0.0 copy-start.3
  11.2 0.0 copy-start.2
  11.2 9.3 %prompt.2 = (f32[1024,512]{1,0:T(8,128)}, f32[1024,512]{1,0:T(8,128)}, f32[1024,512]{1,0:T(8,128)}, bf16[8,1,64,128]{3,2,1,0:T(8,128)(2,1)}) custom-call(s32[8]{0:T(128)S(1)} %copy-done.1, bf16[1024,512]{1,0:T(8,128)(2,1)} %q.2, bf16[1024,512]{1,0:T(8,128)(2,1)} %k_in.2, bf16[1024,512]{1,0:T(8,128)(2,1)} %v_in.2, bf16[1024,512]{1,0:T(8,128)(2,1)} %g.2), custom_call_target="tpu_custom_call" | custom-call | tf_op jit(solution)/shard_map/prompt/pallas_call | solution.py:531
  20.5 2.4 %all-to-all-done.refs_2_ = bf16[8,3,64,128]{3,2,1,0:T(8,128)(2,1)S(1)} async-done(((bf16[8,3,64,128]{3,2,1,0:T(8,128)(2,1)}), bf16[8,3,64,128]{3,2,1,0:T(8,128)(2,1)S(1)}, u32[]{:S(2)}, u32[]{:S(2)}) %all-to-all-start) | async-done | bytes 393248 | tf_op jit(solution)/shard_map/all_to_all | solution.py:471
  22.9 0.0 copy-done.3
  22.9 1.6 %chain.1 = bf16[8,3,64,128]{3,2,1,0:T(8,128)(2,1)} custom-call(s32[8]{0:T(128)S(1)} %copy-done.1, s32[16]{0:T(128)S(1)} %copy-done.3, bf16[8,3,64,128]{3,2,1,0:T(8,128)(2,1)S(1)} %all-to-all-done.refs_2_), custom_call_target="tpu_custom_call" | custom-call | tf_op jit(solution)/shard_map/chain/pallas_call | solution.py:545
  24.5 3.6 %all-to-all-start.1 = ((bf16[8,3,64,128]{3,2,1,0:T(8,128)(2,1)}), bf16[8,3,64,128]{3,2,1,0:T(8,128)(2,1)S(1)}, u32[]{:S(2)}, u32[]{:S(2)}) async-start(bf16[8,3,64,128]{3,2,1,0:T(8,128)(2,1)} %chain.1), calls=%async_computation.1 | async-start | bytes 786432 | tf_op jit(solution)/shard_map/all_to_all | solution.py:471
  28.1 0.0 copy-done.2
  28.1 3.9 %inside.1.refs_2_ = f32[512,512]{1,0:T(8,128)S(1)} custom-call(s32[1,2]{1,0:T(1,128)S(1)} %copy-done.2, bf16[512,512]{1,0:T(8,128)(2,1)} %refs_2_, bf16[512,512]{1,0:T(8,128)(2,1)} %refs_3_, bf16[512,512]{1,0:T(8,128)(2,1)} %refs_4_), custom_call_target="tpu_custom_call" | custom-call | tf_op jit(solution)/shard_map/inside/pallas_call | solution.py:556
  32.0 0.0 copy-start
  32.0 0.0 copy-start.4
  32.0 4.7 %prompt.3 = (f32[1024,512]{1,0:T(8,128)}, f32[1024,512]{1,0:T(8,128)}, f32[1024,512]{1,0:T(8,128)}, bf16[8,1,64,128]{3,2,1,0:T(8,128)(2,1)}) custom-call(s32[8]{0:T(128)S(1)} %copy-done.1, bf16[1024,512]{1,0:T(8,128)(2,1)} %q.2, bf16[1024,512]{1,0:T(8,128)(2,1)} %k_in.2, ...), custom_call_target="tpu_custom_call", output_to_operand_aliasing={{0}: (5, {}), {1}: (6, {}), {2}: (7, {}), {3}: (8, {})} | custom-call | tf_op jit(solution)/shard_map/prompt/pallas_call | solution.py:531
  36.8 3.0 %all-to-all-done.1.refs_4_.states.refs_6_ = bf16[8,3,64,128]{3,2,1,0:T(8,128)(2,1)S(1)} async-done(((bf16[8,3,64,128]{3,2,1,0:T(8,128)(2,1)}), bf16[8,3,64,128]{3,2,1,0:T(8,128)(2,1)S(1)}, u32[]{:S(2)}, u32[]{:S(2)}) %all-to-all-start.1) | async-done | bytes 393248 | tf_op jit(solution)/shard_map/all_to_all | solution.py:471
  39.7 0.0 copy-done
  39.7 0.0 copy-done.4
  39.7 1.5 %scores.1 = (f32[512,512]{1,0:T(8,128)S(1)}, f32[8,128]{1,0:T(8,128)S(1)}) custom-call(s32[1,2]{1,0:T(1,128)S(1)} %copy-done.2, bf16[512,512]{1,0:T(8,128)(2,1)S(1)} %copy-done, f32[512,512]{1,0:T(8,128)S(1)} %inside.1.refs_2_, f32[1,512]{1,0:T(1,128)S(1)} %bitcast.6, bf16[8,3,64,128]{3,2,1,0:T(8,128)(2,1)S(1)} %all-to-all-done.1.refs_4_.states.refs_6_), custom_call_target="tpu_custom_call" | custom-call | tf_op jit(solution)/shard_map/scores/pallas_call | solution.py:569
  41.2 0.0 collective-permute-start.2
  41.2 1.6 %collective-permute-start.1 = (f32[8,128]{1,0:T(8,128)S(1)}, f32[8,128]{1,0:T(8,128)S(1)}, u32[]{:S(2)}, u32[]{:S(2)}) collective-permute-start(f32[8,128]{1,0:T(8,128)S(1)} %get-tuple-element.92.refs_1_), channel_id=1, source_target_pairs={{0,2},{1,3},{2,0},{3,1},{4,6},{5,7},{6,4},{7,5},{8,10},{9,11},{10,... | collective-permute-start | bytes 12296 | tf_op jit(solution)/shard_map/ppermute | solution.py:578
  42.8 0.2 collective-permute-start
  43.0 2.2 %grads.1.refs_0_ = bf16[8,208,128]{2,1,0:T(8,128)(2,1)} custom-call(s32[1,2]{1,0:T(1,128)S(1)} %copy-done.2, bf16[512,512]{1,0:T(8,128)(2,1)S(1)} %copy-done, f32[512,512]{1,0:T(8,128)S(1)} %get-tuple-element.95.refs_2_.near, bf16[8,1,64,128]{3,2,1,0:T(8,128)(2,1)} %get-tuple-element.91.refs_3_), custom_call_target="tpu_custom_call" | custom-call | tf_op jit(solution)/shard_map/grads/pallas_call | solution.py:580
  45.2 0.0 collective-permute-done.2.refs_4_
  45.2 0.0 collective-permute-done.1.refs_3_
  45.2 0.6 collective-permute-done.refs_2_
  45.8 0.7 append.1
  46.5 3.6 %all-to-all-start.2 = ((bf16[8,208,128]{2,1,0:T(8,128)(2,1)}), bf16[8,208,128]{2,1,0:T(8,128)(2,1)S(1)}, u32[]{:S(2)}, u32[]{:S(2)}) async-start(bf16[8,208,128]{2,1,0:T(8,128)(2,1)} %append.1), calls=%async_computation.2 | async-start | bytes 851968 | tf_op jit(solution)/shard_map/all_to_all | solution.py:471
  50.2 1.0 %save.1.refs_5_ = f32[512,512]{1,0:T(8,128)} custom-call(f32[512,512]{1,0:T(8,128)S(1)} %get-tuple-element.95.refs_2_.near), custom_call_target="tpu_custom_call" | custom-call | tf_op jit(solution)/shard_map/save/pallas_call | solution.py:600
  51.2 0.0 copy-start.5
  51.2 4.2 %query.1 = bf16[1024,512]{1,0:T(8,128)(2,1)} custom-call(s32[8]{0:T(128)S(1)} %copy-done.1, f32[1024,512]{1,0:T(8,128)} %get-tuple-element.93.part, bf16[1024,512]{1,0:T(8,128)(2,1)} %g.2, bf16[8,3,64,128]{3,2,1,0:T(8,128)(2,1)S(1)} %all-to-all-done.1.refs_4_.states.refs_6_), custom_call_target="tpu_custom_call" | custom-call | tf_op jit(solution)/shard_map/query/pallas_call | solution.py:608
  55.4 7.5 %all-to-all-done.2.refs_4_ = bf16[8,208,128]{2,1,0:T(8,128)(2,1)S(1)} async-done(((bf16[8,208,128]{2,1,0:T(8,128)(2,1)}), bf16[8,208,128]{2,1,0:T(8,128)(2,1)S(1)}, u32[]{:S(2)}, u32[]{:S(2)}) %all-to-all-start.2) | async-done | bytes 426016 | tf_op jit(solution)/shard_map/all_to_all | solution.py:471
  62.9 0.0 copy-done.5
  62.9 1.7 %listwise.1 = (bf16[8,3,64,128]{3,2,1,0:T(8,128)(2,1)}, f32[8,128]{1,0:T(8,128)S(1)}, f32[1,128]{1,0:T(1,128)}) custom-call(s32[8]{0:T(128)S(1)} %copy-done.1, s32[16]{0:T(128)S(1)} %copy-done.3, s32[1,16]{1,0:T(1,128)S(1)} %bitcast.5, s32[1,16]{1,0:T(1,128)S(1)} %bitcast.7, bf16[8,208,128]{2,1,0:T(8,128)(2,1)S(1)} %all-to-all-done.2.refs_4_), custom_call_target="tpu_custom_call" | custom-call | tf_op jit(solution)/shard_map/listwise/pallas_call | solution.py:618
  64.6 3.6 %all-to-all-start.3 = ((bf16[8,3,64,128]{3,2,1,0:T(8,128)(2,1)}), bf16[8,3,64,128]{3,2,1,0:T(8,128)(2,1)S(1)}, u32[]{:S(2)}, u32[]{:S(2)}) async-start(bf16[8,3,64,128]{3,2,1,0:T(8,128)(2,1)} %get-tuple-element.98), calls=%async_computation.3 | async-start | bytes 786432 | tf_op jit(solution)/shard_map/all_to_all | solution.py:471
  68.3 5.9 %cand.1 = (bf16[512,512]{1,0:T(8,128)(2,1)}, bf16[512,512]{1,0:T(8,128)(2,1)}, bf16[512,512]{1,0:T(8,128)(2,1)}) custom-call(s32[1,2]{1,0:T(1,128)S(1)} %copy-done.2, f32[8,128]{1,0:T(8,128)S(1)} %get-tuple-element.99.refs_1_, bf16[512,512]{1,0:T(8,128)(2,1)} %refs_2_, bf16[512,512]{1,0:T(8,128)(2,1)} %refs_3_, bf16[512,512]{1,0:T(8,128)(2,1)} %refs_4_, ...), custom_call_target="tpu_custom_call" | custom-call | tf_op jit(solution)/shard_map/cand/pallas_call | solution.py:642
  74.2 2.0 %stage.1 = (f32[2,1024,256]{2,1,0:T(8,128)S(1)}, bf16[2,1024,256]{2,1,0:T(8,128)(2,1)S(1)}) custom-call(f32[1024,512]{1,0:T(8,128)} %get-tuple-element.104.dk_part.dk_in, f32[1024,512]{1,0:T(8,128)} %get-tuple-element.105.dv_part.dv_in, bf16[1024,512]{1,0:T(8,128)(2,1)} %k_in.2, bf16[1024,512]{1,0:T(8,128)(2,1)} %v_in.2), custom_call_target="tpu_custom_call" | custom-call | tf_op jit(solution)/shard_map/stage/pallas_call | solution.py:654
  76.2 3.9 %all-to-all-done.3.states = bf16[8,3,64,128]{3,2,1,0:T(8,128)(2,1)S(1)} async-done(((bf16[8,3,64,128]{3,2,1,0:T(8,128)(2,1)}), bf16[8,3,64,128]{3,2,1,0:T(8,128)(2,1)S(1)}, u32[]{:S(2)}, u32[]{:S(2)}) %all-to-all-start.3) | async-done | bytes 393248 | tf_op jit(solution)/shard_map/all_to_all | solution.py:471
  80.1 4.3 %right.1 = (bf16[1024,512]{1,0:T(8,128)(2,1)}, bf16[1024,512]{1,0:T(8,128)(2,1)}) custom-call(s32[8]{0:T(128)S(1)} %copy-done.1, f32[2,1024,256]{2,1,0:T(8,128)S(1)} %get-tuple-element.110.partial, bf16[2,1024,256]{2,1,0:T(8,128)(2,1)S(1)} %get-tuple-element.111.both, bf16[8,3,64,128]{3,2,1,0:T(8,128)(2,1)S(1)} %all-to-all-done.3.states, ...), custom_call_target="tpu_custom_call" | custom-call | tf_op jit(solution)/shard_map/right/pallas_call | solution.py:664
Async XLA Ops:
  0.6 10.6 %copy-start.1 = (s32[8]{0:T(128)S(1)}, s32[8]{0:T(128)}, u32[]{:S(2)}) copy-start(s32[8]{0:T(128)} %ends.7) | copy-start | bytes 100
  4.0 19.0 %all-to-all-start = ((bf16[8,3,64,128]{3,2,1,0:T(8,128)(2,1)}), bf16[8,3,64,128]{3,2,1,0:T(8,128)(2,1)S(1)}, u32[]{:S(2)}, u32[]{:S(2)}) async-start(bf16[8,3,64,128]{3,2,1,0:T(8,128)(2,1)} %sums.1), calls=%async_computation | async-start | bytes 786432 | tf_op jit(solution)/shard_map/all_to_all | solution.py:471
  11.2 11.7 %copy-start.3 = (s32[16]{0:T(128)S(1)}, s32[16]{0:T(128)}, u32[]{:S(2)}) copy-start(s32[16]{0:T(128)} %refs_1_.5) | copy-start | bytes 196
  11.2 16.9 %copy-start.2 = (s32[1,2]{1,0:T(1,128)S(1)}, s32[1,2]{1,0:T(1,128)}, u32[]{:S(2)}) copy-start(s32[1,2]{1,0:T(1,128)} %refs_0_.9) | copy-start | bytes 28
  24.5 15.2 %all-to-all-start.1 = ((bf16[8,3,64,128]{3,2,1,0:T(8,128)(2,1)}), bf16[8,3,64,128]{3,2,1,0:T(8,128)(2,1)S(1)}, u32[]{:S(2)}, u32[]{:S(2)}) async-start(bf16[8,3,64,128]{3,2,1,0:T(8,128)(2,1)} %chain.1), calls=%async_computation.1 | async-start | bytes 786432 | tf_op jit(solution)/shard_map/all_to_all | solution.py:471
  32.0 7.7 %copy-start = (bf16[512,512]{1,0:T(8,128)(2,1)S(1)}, bf16[512,512]{1,0:T(8,128)(2,1)}, u32[]{:S(2)}) copy-start(bf16[512,512]{1,0:T(8,128)(2,1)} %refs_2_) | copy-start | bytes 1572868
  32.0 7.7 %copy-start.4 = (f32[512]{0:T(512)S(1)}, f32[512]{0:T(512)}, u32[]{:S(2)}) copy-start(f32[512]{0:T(512)} %param.19) | copy-start | bytes 6148
  41.2 4.0 %collective-permute-start.2 = (f32[8,128]{1,0:T(8,128)S(1)}, f32[8,128]{1,0:T(8,128)S(1)}, u32[]{:S(2)}, u32[]{:S(2)}) collective-permute-start(f32[8,128]{1,0:T(8,128)S(1)} %get-tuple-element.92.refs_1_), channel_id=1, source_target_pairs={{0,3},{1,0},{2,1},{3,2},{4,7},{5,4},{6,5},{7,6},{8,11},{9,8},{10,9... | collective-permute-start | bytes 12296 | tf_op jit(solution)/shard_map/ppermute | solution.py:578
  41.2 4.0 %collective-permute-start.1 = (f32[8,128]{1,0:T(8,128)S(1)}, f32[8,128]{1,0:T(8,128)S(1)}, u32[]{:S(2)}, u32[]{:S(2)}) collective-permute-start(f32[8,128]{1,0:T(8,128)S(1)} %get-tuple-element.92.refs_1_), channel_id=1, source_target_pairs={{0,2},{1,3},{2,0},{3,1},{4,6},{5,7},{6,4},{7,5},{8,10},{9,11},{10,... | collective-permute-start | bytes 12296 | tf_op jit(solution)/shard_map/ppermute | solution.py:578
  42.8 3.0 %collective-permute-start = (f32[8,128]{1,0:T(8,128)S(1)}, f32[8,128]{1,0:T(8,128)S(1)}, u32[]{:S(2)}, u32[]{:S(2)}) collective-permute-start(f32[8,128]{1,0:T(8,128)S(1)} %get-tuple-element.92.refs_1_), channel_id=1, source_target_pairs={{0,1},{1,2},{2,3},{3,0},{4,5},{5,6},{6,7},{7,4},{8,9},{9,10},{10,1... | collective-permute-start | bytes 12296 | tf_op jit(solution)/shard_map/ppermute | solution.py:578
  46.5 16.4 %all-to-all-start.2 = ((bf16[8,208,128]{2,1,0:T(8,128)(2,1)}), bf16[8,208,128]{2,1,0:T(8,128)(2,1)S(1)}, u32[]{:S(2)}, u32[]{:S(2)}) async-start(bf16[8,208,128]{2,1,0:T(8,128)(2,1)} %append.1), calls=%async_computation.2 | async-start | bytes 851968 | tf_op jit(solution)/shard_map/all_to_all | solution.py:471
  51.2 11.7 %copy-start.5 = (s32[16]{0:T(128)S(1)}, s32[16]{0:T(128)}, u32[]{:S(2)}) copy-start(s32[16]{0:T(128)} %param.23) | copy-start | bytes 196
  64.6 15.5 %all-to-all-start.3 = ((bf16[8,3,64,128]{3,2,1,0:T(8,128)(2,1)}), bf16[8,3,64,128]{3,2,1,0:T(8,128)(2,1)S(1)}, u32[]{:S(2)}, u32[]{:S(2)}) async-start(bf16[8,3,64,128]{3,2,1,0:T(8,128)(2,1)} %get-tuple-element.98), calls=%async_computation.3 | async-start | bytes 786432 | tf_op jit(solution)/shard_map/all_to_all | solution.py:471

commit v9 on v8

--- a/solution.py
+++ b/solution.py
@@ -31,6 +31,22 @@
         compiler_params=pltpu.CompilerParams(vmem_limit_bytes=24 * 1024 * 1024),
         **kw,
     )
+
+
+def small_first(body, arrays):
+    n = len(arrays)
+
+    def wrapped(*refs):
+        held, sems = refs[-n - 1 : -1], refs[-1]
+        copies = [pltpu.make_async_copy(refs[i], held[i], sems.at[i]) for i in range(n)]
+        for c in copies:
+            c.start()
+        for c in copies:
+            c.wait()
+        body(*held, *refs[n : -n - 1])
+
+    scratch = [pltpu.SMEM(a.shape, a.dtype) for a in arrays] + [pltpu.SemaphoreType.DMA((n,))]
+    return wrapped, scratch
 
 
 def count_ends(ends, limit):
@@ -428,16 +444,19 @@
 
 
 def right_kernel(
-    ends, partial, both, states, dk_in, dv_in, k_in, v_in, dk_out, dv_out, rest, rest_both, dk, dv, sems
+    ends_in, partial, both, states, dk_in, dv_in, k_in, v_in, dk_out, dv_out, rest, rest_both, dk, dv, ends, sems
 ):
     width, flat = dk_out.shape
     heads = flat // E
     ahead = partial.shape[2] // E
+    bring = pltpu.make_async_copy(ends_in, ends, sems.at[0])
+    bring.start()
     waits = [[]] * ahead
     for h in range(ahead, heads):
         at = pl.ds((h - ahead) * E, E)
         pairs = [(k_in, rest_both.at[0]), (v_in, rest_both.at[1]), (dk_in, rest.at[0]), (dv_in, rest.at[1])]
         waits.append(fetch([(a, b.at[:, at]) for a, b in pairs], pl.ds(h * E, E), sems, h * 4))
+    bring.wait()
     bounds = slab_bounds(ends, lax.axis_index("seq"), width)
     rows = rows_of((width, E))
     copies = []
@@ -542,12 +561,13 @@
     partials = some_heads(0, heads - late, late_in, [])
     parts, partials = lax.optimization_barrier((parts, partials))
 
+    body, small = small_first(lambda *refs: chain_kernel(*refs, width=width), (prompt_ends, cand_prompt))
     chained = call(
-        lambda *refs: chain_kernel(*refs, width=width),
-        in_specs=[SMEM, SMEM, VMEM],
+        body,
+        in_specs=[ANY, ANY, VMEM],
         out_specs=VMEM,
         out_shape=like((count, per_slab + 1, rows, E), bf16),
-        scratch_shapes=[pltpu.VMEM((prompt_ends.shape[0] + 1, rows, E), f32)],
+        scratch_shapes=[pltpu.VMEM((prompt_ends.shape[0] + 1, rows, E), f32)] + small,
         name="chain",
     )(prompt_ends, cand_prompt, parts)
     states = exchange(chained)
@@ -615,9 +635,10 @@
     )(prompt_ends, *hbm(dq_part, late_grad), states)
     all_grads, prompt_dq, slope_far = lax.optimization_barrier((all_grads, prompt_dq, slope_far))
 
+    body, small = small_first(lambda *refs: listwise_kernel(*refs, width=width), (prompt_ends, cand_prompt))
     right, coef, loss = call(
-        lambda *refs: listwise_kernel(*refs, width=width),
-        in_specs=[SMEM, SMEM] + [VMEM] * 3,
+        body,
+        in_specs=[ANY, ANY] + [VMEM] * 3,
         out_specs=[VMEM] * 3,
         out_shape=[
             like((count, PIECES, rows, E), bf16),
@@ -628,7 +649,8 @@
             pltpu.VMEM((cands, E), f32),
             pltpu.VMEM((cands, E), f32),
             pltpu.VMEM((prompt_ends.shape[0], rows, E), f32),
-        ],
+        ]
+        + small,
         name="listwise",
     )(
         prompt_ends,
@@ -663,7 +685,7 @@
 
     prompt_dk, prompt_dv = call(
         right_kernel,
-        in_specs=[SMEM] + [VMEM] * 3 + [ANY] * 4,
+        in_specs=[ANY] + [VMEM] * 3 + [ANY] * 4,
         out_specs=[ANY] * 2,
         out_shape=[pltpu.HBM((width, flat), bf16)] * 2,
         scratch_shapes=[
@@ -671,6 +693,7 @@
             pltpu.VMEM((2, width, flat - ahead), bf16),
             pltpu.VMEM((width, flat), bf16),
             pltpu.VMEM((width, flat), bf16),
+            pltpu.SMEM(prompt_ends.shape, jnp.int32),
             pltpu.SemaphoreType.DMA((8 * heads,)),
         ],
         name="right",

time: 85.2 us -> 84.4 us (level)
  transfers between devices with their start and end apart: 7 -> 7, of which waited for: 5 -> 5; matrix products, arithmetic and copies ran while one was open for 0% -> 0% of each run, Pallas kernels for 39% -> 40%
where the time goes in v9:
time: 84.4 us; the launch traced here: 83.6 us
  Pallas kernels  45.5 us (54%)
  starting transfers between devices  19.9 us (24%)
  waiting for transfers between devices  17.4 us (21%)
    all_to_all x4, starting transfers between devices, exchange(): return lax.all_to_all(a, 'seq', 0, 0, tiled=True)  18.2 us
    all_to_all x4, waiting for transfers between devices, exchange(): return lax.all_to_all(a, 'seq', 0, 0, tiled=True)  16.7 us
    pallas_call x2, Pallas kernels, some_heads(): call(prompt_kernel, grid=(how_many,), in_specs=[SMEM] + [columns] * 4 + [...  14 us
    pallas_call x1, Pallas kernels, per_device(): call(lambda *refs: cand_kernel(*refs, scaling=scaling), grid=(heads,), in...  5.93 us
    pallas_call x1, Pallas kernels, per_device(): call(query_kernel, grid=(heads,), in_specs=[SMEM, whole, whole, parts_blo...  4.22 us
    pallas_call x1, Pallas kernels, per_device(): call(inside_kernel, grid=(heads,), in_specs=[SMEM] + [cand_block] * 3, ou...  3.85 us
    pallas_call x1, Pallas kernels, per_device(): call(right_kernel, in_specs=[ANY] + [VMEM] * 3 + [ANY] * 4, out_specs=[AN...  3.39 us
    pallas_call x1, Pallas kernels, per_device(): call(sums_kernel, in_specs=[ANY] * 3, out_specs=VMEM, out_shape=like((cou...  3.3 us
  transfers between devices with their start and end apart: 7, of which 5 were waited for; matrix products, arithmetic and copies ran while one was open for 0% of the time, Pallas kernels for 40%

profile of v9, /device:TPU:0, one launch (start us, length us, event | category | flops | bytes accessed | tf_op | source)
XLA Modules:
  0.0 83.6 jit_solution(13565138217725773257)
XLA Ops:
  0.6 0.0 copy-start.1
  0.6 3.3 %sums.1 = bf16[8,3,64,128]{3,2,1,0:T(8,128)(2,1)} custom-call(s32[8]{0:T(128)} %ends_in.3, bf16[1024,512]{1,0:T(8,128)(2,1)} %k_in.2, bf16[1024,512]{1,0:T(8,128)(2,1)} %v_in.2), custom_call_target="tpu_custom_call" | custom-call | tf_op jit(solution)/shard_map/sums/pallas_call | solution.py:532
  4.0 7.3 %all-to-all-start = ((bf16[8,3,64,128]{3,2,1,0:T(8,128)(2,1)}), bf16[8,3,64,128]{3,2,1,0:T(8,128)(2,1)S(1)}, u32[]{:S(2)}, u32[]{:S(2)}) async-start(bf16[8,3,64,128]{3,2,1,0:T(8,128)(2,1)} %sums.1), calls=%async_computation | async-start | bytes 786432 | tf_op jit(solution)/shard_map/all_to_all | solution.py:490
  11.2 0.0 copy-done.1
  11.2 0.0 copy-start.3
  11.2 0.0 copy-start.2
  11.2 9.3 %prompt.2 = (f32[1024,512]{1,0:T(8,128)}, f32[1024,512]{1,0:T(8,128)}, f32[1024,512]{1,0:T(8,128)}, bf16[8,1,64,128]{3,2,1,0:T(8,128)(2,1)}) custom-call(s32[8]{0:T(128)S(1)} %copy-done.1, bf16[1024,512]{1,0:T(8,128)(2,1)} %q.2, bf16[1024,512]{1,0:T(8,128)(2,1)} %k_in.2, bf16[1024,512]{1,0:T(8,128)(2,1)} %v_in.2, bf16[1024,512]{1,0:T(8,128)(2,1)} %g.2), custom_call_target="tpu_custom_call" | custom-call | tf_op jit(solution)/shard_map/prompt/pallas_call | solution.py:550
  20.5 2.4 %all-to-all-done.refs_2_ = bf16[8,3,64,128]{3,2,1,0:T(8,128)(2,1)S(1)} async-done(((bf16[8,3,64,128]{3,2,1,0:T(8,128)(2,1)}), bf16[8,3,64,128]{3,2,1,0:T(8,128)(2,1)S(1)}, u32[]{:S(2)}, u32[]{:S(2)}) %all-to-all-start) | async-done | bytes 393248 | tf_op jit(solution)/shard_map/all_to_all | solution.py:490
  22.9 0.0 copy-done.3
  22.9 1.6 %chain.1 = bf16[8,3,64,128]{3,2,1,0:T(8,128)(2,1)} custom-call(s32[8]{0:T(128)S(1)} %copy-done.1, s32[16]{0:T(128)S(1)} %copy-done.3, bf16[8,3,64,128]{3,2,1,0:T(8,128)(2,1)S(1)} %all-to-all-done.refs_2_), custom_call_target="tpu_custom_call" | custom-call | tf_op jit(solution)/shard_map/chain/pallas_call | solution.py:565
  24.5 3.6 %all-to-all-start.1 = ((bf16[8,3,64,128]{3,2,1,0:T(8,128)(2,1)}), bf16[8,3,64,128]{3,2,1,0:T(8,128)(2,1)S(1)}, u32[]{:S(2)}, u32[]{:S(2)}) async-start(bf16[8,3,64,128]{3,2,1,0:T(8,128)(2,1)} %chain.1), calls=%async_computation.1 | async-start | bytes 786432 | tf_op jit(solution)/shard_map/all_to_all | solution.py:490
  28.2 0.0 copy-done.2
  28.2 3.9 %inside.1.refs_2_ = f32[512,512]{1,0:T(8,128)S(1)} custom-call(s32[1,2]{1,0:T(1,128)S(1)} %copy-done.2, bf16[512,512]{1,0:T(8,128)(2,1)} %refs_2_, bf16[512,512]{1,0:T(8,128)(2,1)} %refs_3_, bf16[512,512]{1,0:T(8,128)(2,1)} %refs_4_), custom_call_target="tpu_custom_call" | custom-call | tf_op jit(solution)/shard_map/inside/pallas_call | solution.py:576
  32.0 0.0 copy-start
  32.0 0.0 copy-start.4
  32.1 4.7 %prompt.3 = (f32[1024,512]{1,0:T(8,128)}, f32[1024,512]{1,0:T(8,128)}, f32[1024,512]{1,0:T(8,128)}, bf16[8,1,64,128]{3,2,1,0:T(8,128)(2,1)}) custom-call(s32[8]{0:T(128)S(1)} %copy-done.1, bf16[1024,512]{1,0:T(8,128)(2,1)} %q.2, bf16[1024,512]{1,0:T(8,128)(2,1)} %k_in.2, ...), custom_call_target="tpu_custom_call", output_to_operand_aliasing={{0}: (5, {}), {1}: (6, {}), {2}: (7, {}), {3}: (8, {})} | custom-call | tf_op jit(solution)/shard_map/prompt/pallas_call | solution.py:550
  36.8 3.0 %all-to-all-done.1.refs_4_.states.refs_6_ = bf16[8,3,64,128]{3,2,1,0:T(8,128)(2,1)S(1)} async-done(((bf16[8,3,64,128]{3,2,1,0:T(8,128)(2,1)}), bf16[8,3,64,128]{3,2,1,0:T(8,128)(2,1)S(1)}, u32[]{:S(2)}, u32[]{:S(2)}) %all-to-all-start.1) | async-done | bytes 393248 | tf_op jit(solution)/shard_map/all_to_all | solution.py:490
  39.8 0.0 copy-done
  39.8 0.0 copy-done.4
  39.8 1.5 %scores.1 = (f32[512,512]{1,0:T(8,128)S(1)}, f32[8,128]{1,0:T(8,128)S(1)}) custom-call(s32[1,2]{1,0:T(1,128)S(1)} %copy-done.2, bf16[512,512]{1,0:T(8,128)(2,1)S(1)} %copy-done, f32[512,512]{1,0:T(8,128)S(1)} %inside.1.refs_2_, f32[1,512]{1,0:T(1,128)S(1)} %bitcast.6, bf16[8,3,64,128]{3,2,1,0:T(8,128)(2,1)S(1)} %all-to-all-done.1.refs_4_.states.refs_6_), custom_call_target="tpu_custom_call" | custom-call | tf_op jit(solution)/shard_map/scores/pallas_call | solution.py:589
  41.3 0.0 collective-permute-start.2
  41.3 1.6 %collective-permute-start.1 = (f32[8,128]{1,0:T(8,128)S(1)}, f32[8,128]{1,0:T(8,128)S(1)}, u32[]{:S(2)}, u32[]{:S(2)}) collective-permute-start(f32[8,128]{1,0:T(8,128)S(1)} %get-tuple-element.92.refs_1_), channel_id=1, source_target_pairs={{0,2},{1,3},{2,0},{3,1},{4,6},{5,7},{6,4},{7,5},{8,10},{9,11},{10,... | collective-permute-start | bytes 12296 | tf_op jit(solution)/shard_map/ppermute | solution.py:598
  42.8 0.2 collective-permute-start
  43.0 2.2 %grads.1.refs_0_ = bf16[8,208,128]{2,1,0:T(8,128)(2,1)} custom-call(s32[1,2]{1,0:T(1,128)S(1)} %copy-done.2, bf16[512,512]{1,0:T(8,128)(2,1)S(1)} %copy-done, f32[512,512]{1,0:T(8,128)S(1)} %get-tuple-element.95.refs_2_.near, bf16[8,1,64,128]{3,2,1,0:T(8,128)(2,1)} %get-tuple-element.91.refs_3_), custom_call_target="tpu_custom_call" | custom-call | tf_op jit(solution)/shard_map/grads/pallas_call | solution.py:600
  45.2 0.0 collective-permute-done.2.refs_4_
  45.2 0.0 collective-permute-done.1.refs_3_
  45.2 0.6 collective-permute-done.refs_2_
  45.9 0.7 append.1
  46.6 3.6 %all-to-all-start.2 = ((bf16[8,208,128]{2,1,0:T(8,128)(2,1)}), bf16[8,208,128]{2,1,0:T(8,128)(2,1)S(1)}, u32[]{:S(2)}, u32[]{:S(2)}) async-start(bf16[8,208,128]{2,1,0:T(8,128)(2,1)} %append.1), calls=%async_computation.2 | async-start | bytes 851968 | tf_op jit(solution)/shard_map/all_to_all | solution.py:490
  50.2 1.0 %save.1.refs_5_ = f32[512,512]{1,0:T(8,128)} custom-call(f32[512,512]{1,0:T(8,128)S(1)} %get-tuple-element.95.refs_2_.near), custom_call_target="tpu_custom_call" | custom-call | tf_op jit(solution)/shard_map/save/pallas_call | solution.py:620
  51.2 0.0 copy-start.5
  51.2 4.2 %query.1 = bf16[1024,512]{1,0:T(8,128)(2,1)} custom-call(s32[8]{0:T(128)S(1)} %copy-done.1, f32[1024,512]{1,0:T(8,128)} %get-tuple-element.93.part, bf16[1024,512]{1,0:T(8,128)(2,1)} %g.2, bf16[8,3,64,128]{3,2,1,0:T(8,128)(2,1)S(1)} %all-to-all-done.1.refs_4_.states.refs_6_), custom_call_target="tpu_custom_call" | custom-call | tf_op jit(solution)/shard_map/query/pallas_call | solution.py:628
  55.5 7.5 %all-to-all-done.2.refs_4_ = bf16[8,208,128]{2,1,0:T(8,128)(2,1)S(1)} async-done(((bf16[8,208,128]{2,1,0:T(8,128)(2,1)}), bf16[8,208,128]{2,1,0:T(8,128)(2,1)S(1)}, u32[]{:S(2)}, u32[]{:S(2)}) %all-to-all-start.2) | async-done | bytes 426016 | tf_op jit(solution)/shard_map/all_to_all | solution.py:490
  62.9 0.0 copy-done.5
  63.0 1.7 %listwise.1 = (bf16[8,3,64,128]{3,2,1,0:T(8,128)(2,1)}, f32[8,128]{1,0:T(8,128)S(1)}, f32[1,128]{1,0:T(1,128)}) custom-call(s32[8]{0:T(128)S(1)} %copy-done.1, s32[16]{0:T(128)S(1)} %copy-done.3, s32[1,16]{1,0:T(1,128)S(1)} %bitcast.5, s32[1,16]{1,0:T(1,128)S(1)} %bitcast.7, bf16[8,208,128]{2,1,0:T(8,128)(2,1)S(1)} %all-to-all-done.2.refs_4_), custom_call_target="tpu_custom_call" | custom-call | tf_op jit(solution)/shard_map/listwise/pallas_call | solution.py:639
  64.7 3.6 %all-to-all-start.3 = ((bf16[8,3,64,128]{3,2,1,0:T(8,128)(2,1)}), bf16[8,3,64,128]{3,2,1,0:T(8,128)(2,1)S(1)}, u32[]{:S(2)}, u32[]{:S(2)}) async-start(bf16[8,3,64,128]{3,2,1,0:T(8,128)(2,1)} %get-tuple-element.98), calls=%async_computation.3 | async-start | bytes 786432 | tf_op jit(solution)/shard_map/all_to_all | solution.py:490
  68.3 5.9 %cand.1 = (bf16[512,512]{1,0:T(8,128)(2,1)}, bf16[512,512]{1,0:T(8,128)(2,1)}, bf16[512,512]{1,0:T(8,128)(2,1)}) custom-call(s32[1,2]{1,0:T(1,128)S(1)} %copy-done.2, f32[8,128]{1,0:T(8,128)S(1)} %get-tuple-element.99.refs_1_, bf16[512,512]{1,0:T(8,128)(2,1)} %refs_2_, bf16[512,512]{1,0:T(8,128)(2,1)} %refs_3_, bf16[512,512]{1,0:T(8,128)(2,1)} %refs_4_, ...), custom_call_target="tpu_custom_call" | custom-call | tf_op jit(solution)/shard_map/cand/pallas_call | solution.py:664
  74.3 2.0 %stage.1 = (f32[2,1024,256]{2,1,0:T(8,128)S(1)}, bf16[2,1024,256]{2,1,0:T(8,128)(2,1)S(1)}) custom-call(f32[1024,512]{1,0:T(8,128)} %get-tuple-element.104.dk_part.dk_in, f32[1024,512]{1,0:T(8,128)} %get-tuple-element.105.dv_part.dv_in, bf16[1024,512]{1,0:T(8,128)(2,1)} %k_in.2, bf16[1024,512]{1,0:T(8,128)(2,1)} %v_in.2), custom_call_target="tpu_custom_call" | custom-call | tf_op jit(solution)/shard_map/stage/pallas_call | solution.py:676
  76.3 3.9 %all-to-all-done.3.states = bf16[8,3,64,128]{3,2,1,0:T(8,128)(2,1)S(1)} async-done(((bf16[8,3,64,128]{3,2,1,0:T(8,128)(2,1)}), bf16[8,3,64,128]{3,2,1,0:T(8,128)(2,1)S(1)}, u32[]{:S(2)}, u32[]{:S(2)}) %all-to-all-start.3) | async-done | bytes 393248 | tf_op jit(solution)/shard_map/all_to_all | solution.py:490
  80.2 3.4 %right.1 = (bf16[1024,512]{1,0:T(8,128)(2,1)}, bf16[1024,512]{1,0:T(8,128)(2,1)}) custom-call(s32[8]{0:T(128)S(1)} %copy-done.1, f32[2,1024,256]{2,1,0:T(8,128)S(1)} %get-tuple-element.110.partial, bf16[2,1024,256]{2,1,0:T(8,128)(2,1)S(1)} %get-tuple-element.111.both, bf16[8,3,64,128]{3,2,1,0:T(8,128)(2,1)S(1)} %all-to-all-done.3.states, ...), custom_call_target="tpu_custom_call" | custom-call | tf_op jit(solution)/shard_map/right/pallas_call | solution.py:686
Async XLA Ops:
  0.6 10.6 %copy-start.1 = (s32[8]{0:T(128)S(1)}, s32[8]{0:T(128)}, u32[]{:S(2)}) copy-start(s32[8]{0:T(128)} %ends_in.3) | copy-start | bytes 100
  4.0 19.0 %all-to-all-start = ((bf16[8,3,64,128]{3,2,1,0:T(8,128)(2,1)}), bf16[8,3,64,128]{3,2,1,0:T(8,128)(2,1)S(1)}, u32[]{:S(2)}, u32[]{:S(2)}) async-start(bf16[8,3,64,128]{3,2,1,0:T(8,128)(2,1)} %sums.1), calls=%async_computation | async-start | bytes 786432 | tf_op jit(solution)/shard_map/all_to_all | solution.py:490
  11.2 11.7 %copy-start.3 = (s32[16]{0:T(128)S(1)}, s32[16]{0:T(128)}, u32[]{:S(2)}) copy-start(s32[16]{0:T(128)} %refs_1_.5) | copy-start | bytes 196
  11.2 16.9 %copy-start.2 = (s32[1,2]{1,0:T(1,128)S(1)}, s32[1,2]{1,0:T(1,128)}, u32[]{:S(2)}) copy-start(s32[1,2]{1,0:T(1,128)} %refs_0_.9) | copy-start | bytes 28
  24.5 15.2 %all-to-all-start.1 = ((bf16[8,3,64,128]{3,2,1,0:T(8,128)(2,1)}), bf16[8,3,64,128]{3,2,1,0:T(8,128)(2,1)S(1)}, u32[]{:S(2)}, u32[]{:S(2)}) async-start(bf16[8,3,64,128]{3,2,1,0:T(8,128)(2,1)} %chain.1), calls=%async_computation.1 | async-start | bytes 786432 | tf_op jit(solution)/shard_map/all_to_all | solution.py:490
  32.0 7.7 %copy-start = (bf16[512,512]{1,0:T(8,128)(2,1)S(1)}, bf16[512,512]{1,0:T(8,128)(2,1)}, u32[]{:S(2)}) copy-start(bf16[512,512]{1,0:T(8,128)(2,1)} %refs_2_) | copy-start | bytes 1572868
  32.0 7.7 %copy-start.4 = (f32[512]{0:T(512)S(1)}, f32[512]{0:T(512)}, u32[]{:S(2)}) copy-start(f32[512]{0:T(512)} %param.19) | copy-start | bytes 6148
  41.3 4.0 %collective-permute-start.2 = (f32[8,128]{1,0:T(8,128)S(1)}, f32[8,128]{1,0:T(8,128)S(1)}, u32[]{:S(2)}, u32[]{:S(2)}) collective-permute-start(f32[8,128]{1,0:T(8,128)S(1)} %get-tuple-element.92.refs_1_), channel_id=1, source_target_pairs={{0,3},{1,0},{2,1},{3,2},{4,7},{5,4},{6,5},{7,6},{8,11},{9,8},{10,9... | collective-permute-start | bytes 12296 | tf_op jit(solution)/shard_map/ppermute | solution.py:598
  41.3 4.0 %collective-permute-start.1 = (f32[8,128]{1,0:T(8,128)S(1)}, f32[8,128]{1,0:T(8,128)S(1)}, u32[]{:S(2)}, u32[]{:S(2)}) collective-permute-start(f32[8,128]{1,0:T(8,128)S(1)} %get-tuple-element.92.refs_1_), channel_id=1, source_target_pairs={{0,2},{1,3},{2,0},{3,1},{4,6},{5,7},{6,4},{7,5},{8,10},{9,11},{10,... | collective-permute-start | bytes 12296 | tf_op jit(solution)/shard_map/ppermute | solution.py:598
  42.8 3.0 %collective-permute-start = (f32[8,128]{1,0:T(8,128)S(1)}, f32[8,128]{1,0:T(8,128)S(1)}, u32[]{:S(2)}, u32[]{:S(2)}) collective-permute-start(f32[8,128]{1,0:T(8,128)S(1)} %get-tuple-element.92.refs_1_), channel_id=1, source_target_pairs={{0,1},{1,2},{2,3},{3,0},{4,5},{5,6},{6,7},{7,4},{8,9},{9,10},{10,1... | collective-permute-start | bytes 12296 | tf_op jit(solution)/shard_map/ppermute | solution.py:598
  46.6 16.4 %all-to-all-start.2 = ((bf16[8,208,128]{2,1,0:T(8,128)(2,1)}), bf16[8,208,128]{2,1,0:T(8,128)(2,1)S(1)}, u32[]{:S(2)}, u32[]{:S(2)}) async-start(bf16[8,208,128]{2,1,0:T(8,128)(2,1)} %append.1), calls=%async_computation.2 | async-start | bytes 851968 | tf_op jit(solution)/shard_map/all_to_all | solution.py:490
  51.2 11.7 %copy-start.5 = (s32[16]{0:T(128)S(1)}, s32[16]{0:T(128)}, u32[]{:S(2)}) copy-start(s32[16]{0:T(128)} %param.23) | copy-start | bytes 196
  64.7 15.5 %all-to-all-start.3 = ((bf16[8,3,64,128]{3,2,1,0:T(8,128)(2,1)}), bf16[8,3,64,128]{3,2,1,0:T(8,128)(2,1)S(1)}, u32[]{:S(2)}, u32[]{:S(2)}) async-start(bf16[8,3,64,128]{3,2,1,0:T(8,128)(2,1)} %get-tuple-element.98), calls=%async_computation.3 | async-start | bytes 786432 | tf_op jit(solution)/shard_map/all_to_all | solution.py:490

commit v10 on v9

--- a/solution.py
+++ b/solution.py
@@ -108,7 +108,7 @@
     return jnp.concatenate([ref[h * share + o, place] for o in range(share)], axis=0)
 
 
-def sums_kernel(ends_in, k_in, v_in, out, ends, k, v, sems):
+def sums_kernel(ends_in, k_in, v_in, out, ends, k, v, made, sems):
     width, flat = k.shape
     heads = flat // E
     share = out.shape[0] // heads
@@ -131,6 +131,7 @@
     segments, of_first = slot_use(ends, me, width)
     rows = rows_of((width, E))
     zero = jnp.zeros((width, E), f32)
+    results = []
     for h in range(heads):
         for c in copies[h]:
             c.wait()
@@ -143,13 +144,18 @@
             pieces.append(jnp.where(inside, values, zero).astype(bf16))
             low = b
         sums = dot(k[:, at], jnp.concatenate(pieces, axis=1), 0, 0)
-        mine = out.at[pl.ds(h * share, share)]
+        some = pl.ds(h * share, share)
+        mine = made.at[some]
         cuts = [sums[:, m * E : (m + 1) * E] for m in range(PIECES)]
         source = jnp.where(of_first, cuts[0], cuts[1])
         spare = source - source.astype(bf16).astype(f32)
         store_parts(mine, 0, cuts[0])
         store_parts(mine, 1, jnp.where(segments == 1, spare, cuts[1]))
         store_parts(mine, 2, jnp.where(segments == PIECES, cuts[2], spare))
+        results.append(pltpu.make_async_copy(mine, out.at[some], sems.at[h, 2]))
+        results[-1].start()
+    for c in results:
+        c.wait()
 
 
 def chain_kernel(ends, cand_prompt, parts, out, held, *, width):
@@ -241,15 +247,17 @@
         c.wait()
 
 
-def grads_kernel(lengths, q, slope, head, out, sem, *, scaling):
+def grads_kernel(lengths, q, slope, head, out, made, passed, sems, *, scaling):
     width, flat = q.shape
     heads = flat // E
     count = out.shape[0]
     share = count // heads
     size = flat // count
     per_slab = lengths.shape[1]
-    bring = pltpu.make_async_copy(head.at[:, 0], out.at[:, pl.ds(per_slab * size, size)], sem)
+    bring = pltpu.make_async_copy(head.at[:, 0], passed, sems.at[heads])
     bring.start()
+    pass_on = pltpu.make_async_copy(passed, out.at[:, pl.ds(per_slab * size, size)], sems.at[heads + 1])
+    results = [pass_on]
     bounds = cand_bounds(lengths)
     rows = rows_of((width, E))
     for h in range(heads):
@@ -268,8 +276,17 @@
         for j in range(per_slab):
             for o in range(share):
                 start = j * E + o * size
-                out[h * share + o, j * size : (j + 1) * size] = grads[start : start + size]
-    bring.wait()
+                made[h * share + o, j * size : (j + 1) * size] = grads[start : start + size]
+        if h == 0:
+            bring.wait()
+            pass_on.start()
+        some = pl.ds(h * share, share)
+        results.append(
+            pltpu.make_async_copy(made.at[some], out.at[some, pl.ds(0, per_slab * size)], sems.at[h])
+        )
+        results[-1].start()
+    for c in results:
+        c.wait()
 
 
 def append_kernel(payload, *refs, per_slab):
@@ -532,11 +549,11 @@
     pieces = call(
         sums_kernel,
         in_specs=[ANY] * 3,
-        out_specs=VMEM,
-        out_shape=like((count, PIECES, rows, E), bf16),
+        out_specs=ANY,
+        out_shape=pltpu.HBM((count, PIECES, rows, E), bf16),
         scratch_shapes=[pltpu.SMEM(prompt_ends.shape, jnp.int32)]
         + [pltpu.VMEM((width, flat), bf16)] * 2
-        + [pltpu.SemaphoreType.DMA((heads + 1, 2))],
+        + [pltpu.VMEM((count, PIECES, rows, E), bf16), pltpu.SemaphoreType.DMA((heads + 1, 3))],
         name="sums",
     )(*hbm(prompt_ends, prompt_k, prompt_v))
     parts = exchange(pieces)
@@ -600,9 +617,13 @@
     grads = call(
         lambda *refs: grads_kernel(*refs, scaling=scaling),
         in_specs=[SMEM, VMEM, VMEM, ANY],
-        out_specs=VMEM,
+        out_specs=ANY,
         out_shape=pltpu.HBM(payload_shape, bf16),
-        scratch_shapes=[pltpu.SemaphoreType.DMA],
+        scratch_shapes=[
+            pltpu.VMEM((count, per_slab * rows, E), bf16),
+            pltpu.VMEM((count, rows, E), bf16),
+            pltpu.SemaphoreType.DMA((heads + 2,)),
+        ],
         name="grads",
     )(cand_lengths, near_q, *near(slope), *hbm(head_part))
     grads = call(

time: 84.4 us -> 85.4 us (1.012)
  no operation moved by 1% of the time
where the time goes in v10:
time: 85.4 us; the launch traced here: 84.3 us
  Pallas kernels  46 us (54%)
  starting transfers between devices  20 us (23%)
  waiting for transfers between devices  17.4 us (20%)
  between operations  0.94 us (1%)
    all_to_all x4, starting transfers between devices, exchange(): return lax.all_to_all(a, 'seq', 0, 0, tiled=True)  18.2 us
    all_to_all x4, waiting for transfers between devices, exchange(): return lax.all_to_all(a, 'seq', 0, 0, tiled=True)  17.2 us
    pallas_call x2, Pallas kernels, some_heads(): call(prompt_kernel, grid=(how_many,), in_specs=[SMEM] + [columns] * 4 + [...  14 us
    pallas_call x1, Pallas kernels, per_device(): call(lambda *refs: cand_kernel(*refs, scaling=scaling), grid=(heads,), in...  5.92 us
    pallas_call x1, Pallas kernels, per_device(): call(query_kernel, grid=(heads,), in_specs=[SMEM, whole, whole, parts_blo...  4.22 us
    pallas_call x1, Pallas kernels, per_device(): call(inside_kernel, grid=(heads,), in_specs=[SMEM] + [cand_block] * 3, ou...  3.85 us
    pallas_call x1, Pallas kernels, per_device(): call(right_kernel, in_specs=[ANY] + [VMEM] * 3 + [ANY] * 4, out_specs=[AN...  3.55 us
    pallas_call x1, Pallas kernels, per_device(): call(sums_kernel, in_specs=[ANY] * 3, out_specs=ANY, out_shape=pltpu.HBM(...  3.22 us
  transfers between devices with their start and end apart: 7, of which 5 were waited for; matrix products, arithmetic and copies ran while one was open for 0% of the time, Pallas kernels for 40%

profile of v10, /device:TPU:0, one launch (start us, length us, event | category | flops | bytes accessed | tf_op | source)
XLA Modules:
  0.0 84.3 jit_solution(11679795031171544419)
XLA Ops:
  0.6 0.0 copy-start.1
  0.6 3.2 %sums.1 = bf16[8,3,64,128]{3,2,1,0:T(8,128)(2,1)} custom-call(s32[8]{0:T(128)} %ends_in.3, bf16[1024,512]{1,0:T(8,128)(2,1)} %k_in.2, bf16[1024,512]{1,0:T(8,128)(2,1)} %v_in.2), custom_call_target="tpu_custom_call" | custom-call | tf_op jit(solution)/shard_map/sums/pallas_call | solution.py:549
  3.9 7.3 %all-to-all-start = ((bf16[8,3,64,128]{3,2,1,0:T(8,128)(2,1)}), bf16[8,3,64,128]{3,2,1,0:T(8,128)(2,1)S(1)}, u32[]{:S(2)}, u32[]{:S(2)}) async-start(bf16[8,3,64,128]{3,2,1,0:T(8,128)(2,1)} %sums.1), calls=%async_computation | async-start | bytes 786432 | tf_op jit(solution)/shard_map/all_to_all | solution.py:507
  11.2 0.0 copy-done.1
  11.2 0.0 copy-start.3
  11.2 0.0 copy-start.2
  11.2 9.3 %prompt.2 = (f32[1024,512]{1,0:T(8,128)}, f32[1024,512]{1,0:T(8,128)}, f32[1024,512]{1,0:T(8,128)}, bf16[8,1,64,128]{3,2,1,0:T(8,128)(2,1)}) custom-call(s32[8]{0:T(128)S(1)} %copy-done.1, bf16[1024,512]{1,0:T(8,128)(2,1)} %q.2, bf16[1024,512]{1,0:T(8,128)(2,1)} %k_in.2, bf16[1024,512]{1,0:T(8,128)(2,1)} %v_in.2, bf16[1024,512]{1,0:T(8,128)(2,1)} %g.2), custom_call_target="tpu_custom_call" | custom-call | tf_op jit(solution)/shard_map/prompt/pallas_call | solution.py:567
  20.5 2.4 %all-to-all-done.refs_2_ = bf16[8,3,64,128]{3,2,1,0:T(8,128)(2,1)S(1)} async-done(((bf16[8,3,64,128]{3,2,1,0:T(8,128)(2,1)}), bf16[8,3,64,128]{3,2,1,0:T(8,128)(2,1)S(1)}, u32[]{:S(2)}, u32[]{:S(2)}) %all-to-all-start) | async-done | bytes 393248 | tf_op jit(solution)/shard_map/all_to_all | solution.py:507
  22.8 0.0 copy-done.3
  22.8 1.6 %chain.1 = bf16[8,3,64,128]{3,2,1,0:T(8,128)(2,1)} custom-call(s32[8]{0:T(128)S(1)} %copy-done.1, s32[16]{0:T(128)S(1)} %copy-done.3, bf16[8,3,64,128]{3,2,1,0:T(8,128)(2,1)S(1)} %all-to-all-done.refs_2_), custom_call_target="tpu_custom_call" | custom-call | tf_op jit(solution)/shard_map/chain/pallas_call | solution.py:582
  24.5 3.6 %all-to-all-start.1 = ((bf16[8,3,64,128]{3,2,1,0:T(8,128)(2,1)}), bf16[8,3,64,128]{3,2,1,0:T(8,128)(2,1)S(1)}, u32[]{:S(2)}, u32[]{:S(2)}) async-start(bf16[8,3,64,128]{3,2,1,0:T(8,128)(2,1)} %chain.1), calls=%async_computation.1 | async-start | bytes 786432 | tf_op jit(solution)/shard_map/all_to_all | solution.py:507
  28.1 0.0 copy-done.2
  28.1 3.9 %inside.1.refs_2_ = f32[512,512]{1,0:T(8,128)S(1)} custom-call(s32[1,2]{1,0:T(1,128)S(1)} %copy-done.2, bf16[512,512]{1,0:T(8,128)(2,1)} %refs_2_, bf16[512,512]{1,0:T(8,128)(2,1)} %refs_3_, bf16[512,512]{1,0:T(8,128)(2,1)} %refs_4_), custom_call_target="tpu_custom_call" | custom-call | tf_op jit(solution)/shard_map/inside/pallas_call | solution.py:593
  32.0 0.0 copy-start
  32.0 0.0 copy-start.4
  32.0 4.7 %prompt.3 = (f32[1024,512]{1,0:T(8,128)}, f32[1024,512]{1,0:T(8,128)}, f32[1024,512]{1,0:T(8,128)}, bf16[8,1,64,128]{3,2,1,0:T(8,128)(2,1)}) custom-call(s32[8]{0:T(128)S(1)} %copy-done.1, bf16[1024,512]{1,0:T(8,128)(2,1)} %q.2, bf16[1024,512]{1,0:T(8,128)(2,1)} %k_in.2, ...), custom_call_target="tpu_custom_call", output_to_operand_aliasing={{0}: (5, {}), {1}: (6, {}), {2}: (7, {}), {3}: (8, {})} | custom-call | tf_op jit(solution)/shard_map/prompt/pallas_call | solution.py:567
  36.7 2.9 %all-to-all-done.1.refs_4_.states.refs_6_ = bf16[8,3,64,128]{3,2,1,0:T(8,128)(2,1)S(1)} async-done(((bf16[8,3,64,128]{3,2,1,0:T(8,128)(2,1)}), bf16[8,3,64,128]{3,2,1,0:T(8,128)(2,1)S(1)}, u32[]{:S(2)}, u32[]{:S(2)}) %all-to-all-start.1) | async-done | bytes 393248 | tf_op jit(solution)/shard_map/all_to_all | solution.py:507
  39.7 0.0 copy-done
  39.7 0.0 copy-done.4
  39.7 1.5 %scores.1 = (f32[512,512]{1,0:T(8,128)S(1)}, f32[8,128]{1,0:T(8,128)S(1)}) custom-call(s32[1,2]{1,0:T(1,128)S(1)} %copy-done.2, bf16[512,512]{1,0:T(8,128)(2,1)S(1)} %copy-done, f32[512,512]{1,0:T(8,128)S(1)} %inside.1.refs_2_, f32[1,512]{1,0:T(1,128)S(1)} %bitcast.6, bf16[8,3,64,128]{3,2,1,0:T(8,128)(2,1)S(1)} %all-to-all-done.1.refs_4_.states.refs_6_), custom_call_target="tpu_custom_call" | custom-call | tf_op jit(solution)/shard_map/scores/pallas_call | solution.py:606
  41.2 0.0 collective-permute-start.2
  41.2 1.6 %collective-permute-start.1 = (f32[8,128]{1,0:T(8,128)S(1)}, f32[8,128]{1,0:T(8,128)S(1)}, u32[]{:S(2)}, u32[]{:S(2)}) collective-permute-start(f32[8,128]{1,0:T(8,128)S(1)} %get-tuple-element.92.refs_1_), channel_id=1, source_target_pairs={{0,2},{1,3},{2,0},{3,1},{4,6},{5,7},{6,4},{7,5},{8,10},{9,11},{10,... | collective-permute-start | bytes 12296 | tf_op jit(solution)/shard_map/ppermute | solution.py:615
  42.8 0.2 collective-permute-start
  43.0 2.6 %grads.1.refs_0_ = bf16[8,208,128]{2,1,0:T(8,128)(2,1)} custom-call(s32[1,2]{1,0:T(1,128)S(1)} %copy-done.2, bf16[512,512]{1,0:T(8,128)(2,1)S(1)} %copy-done, f32[512,512]{1,0:T(8,128)S(1)} %get-tuple-element.95.refs_2_.near, bf16[8,1,64,128]{3,2,1,0:T(8,128)(2,1)} %get-tuple-element.91.refs_3_), custom_call_target="tpu_custom_call" | custom-call | tf_op jit(solution)/shard_map/grads/pallas_call | solution.py:617
  45.6 0.0 collective-permute-done.2.refs_4_
  45.6 0.0 collective-permute-done.1.refs_3_
  45.6 0.2 collective-permute-done.refs_2_
  45.8 0.7 append.1
  46.5 3.6 %all-to-all-start.2 = ((bf16[8,208,128]{2,1,0:T(8,128)(2,1)}), bf16[8,208,128]{2,1,0:T(8,128)(2,1)S(1)}, u32[]{:S(2)}, u32[]{:S(2)}) async-start(bf16[8,208,128]{2,1,0:T(8,128)(2,1)} %append.1), calls=%async_computation.2 | async-start | bytes 851968 | tf_op jit(solution)/shard_map/all_to_all | solution.py:507
  50.2 1.0 %save.1.refs_5_ = f32[512,512]{1,0:T(8,128)} custom-call(f32[512,512]{1,0:T(8,128)S(1)} %get-tuple-element.95.refs_2_.near), custom_call_target="tpu_custom_call" | custom-call | tf_op jit(solution)/shard_map/save/pallas_call | solution.py:641
  51.2 0.0 copy-start.5
  51.2 4.2 %query.1 = bf16[1024,512]{1,0:T(8,128)(2,1)} custom-call(s32[8]{0:T(128)S(1)} %copy-done.1, f32[1024,512]{1,0:T(8,128)} %get-tuple-element.93.part, bf16[1024,512]{1,0:T(8,128)(2,1)} %g.2, bf16[8,3,64,128]{3,2,1,0:T(8,128)(2,1)S(1)} %all-to-all-done.1.refs_4_.states.refs_6_), custom_call_target="tpu_custom_call" | custom-call | tf_op jit(solution)/shard_map/query/pallas_call | solution.py:649
  55.4 7.9 %all-to-all-done.2.refs_4_ = bf16[8,208,128]{2,1,0:T(8,128)(2,1)S(1)} async-done(((bf16[8,208,128]{2,1,0:T(8,128)(2,1)}), bf16[8,208,128]{2,1,0:T(8,128)(2,1)S(1)}, u32[]{:S(2)}, u32[]{:S(2)}) %all-to-all-start.2) | async-done | bytes 426016 | tf_op jit(solution)/shard_map/all_to_all | solution.py:507
  63.3 0.0 copy-done.5
  63.3 1.7 %listwise.1 = (bf16[8,3,64,128]{3,2,1,0:T(8,128)(2,1)}, f32[8,128]{1,0:T(8,128)S(1)}, f32[1,128]{1,0:T(1,128)}) custom-call(s32[8]{0:T(128)S(1)} %copy-done.1, s32[16]{0:T(128)S(1)} %copy-done.3, s32[1,16]{1,0:T(1,128)S(1)} %bitcast.5, s32[1,16]{1,0:T(1,128)S(1)} %bitcast.7, bf16[8,208,128]{2,1,0:T(8,128)(2,1)S(1)} %all-to-all-done.2.refs_4_), custom_call_target="tpu_custom_call" | custom-call | tf_op jit(solution)/shard_map/listwise/pallas_call | solution.py:660
  65.1 3.6 %all-to-all-start.3 = ((bf16[8,3,64,128]{3,2,1,0:T(8,128)(2,1)}), bf16[8,3,64,128]{3,2,1,0:T(8,128)(2,1)S(1)}, u32[]{:S(2)}, u32[]{:S(2)}) async-start(bf16[8,3,64,128]{3,2,1,0:T(8,128)(2,1)} %get-tuple-element.98), calls=%async_computation.3 | async-start | bytes 786432 | tf_op jit(solution)/shard_map/all_to_all | solution.py:507
  68.7 5.9 %cand.1 = (bf16[512,512]{1,0:T(8,128)(2,1)}, bf16[512,512]{1,0:T(8,128)(2,1)}, bf16[512,512]{1,0:T(8,128)(2,1)}) custom-call(s32[1,2]{1,0:T(1,128)S(1)} %copy-done.2, f32[8,128]{1,0:T(8,128)S(1)} %get-tuple-element.99.refs_1_, bf16[512,512]{1,0:T(8,128)(2,1)} %refs_2_, bf16[512,512]{1,0:T(8,128)(2,1)} %refs_3_, bf16[512,512]{1,0:T(8,128)(2,1)} %refs_4_, ...), custom_call_target="tpu_custom_call" | custom-call | tf_op jit(solution)/shard_map/cand/pallas_call | solution.py:685
  74.6 2.0 %stage.1 = (f32[2,1024,256]{2,1,0:T(8,128)S(1)}, bf16[2,1024,256]{2,1,0:T(8,128)(2,1)S(1)}) custom-call(f32[1024,512]{1,0:T(8,128)} %get-tuple-element.104.dk_part.dk_in, f32[1024,512]{1,0:T(8,128)} %get-tuple-element.105.dv_part.dv_in, bf16[1024,512]{1,0:T(8,128)(2,1)} %k_in.2, bf16[1024,512]{1,0:T(8,128)(2,1)} %v_in.2), custom_call_target="tpu_custom_call" | custom-call | tf_op jit(solution)/shard_map/stage/pallas_call | solution.py:697
  76.7 4.0 %all-to-all-done.3.states = bf16[8,3,64,128]{3,2,1,0:T(8,128)(2,1)S(1)} async-done(((bf16[8,3,64,128]{3,2,1,0:T(8,128)(2,1)}), bf16[8,3,64,128]{3,2,1,0:T(8,128)(2,1)S(1)}, u32[]{:S(2)}, u32[]{:S(2)}) %all-to-all-start.3) | async-done | bytes 393248 | tf_op jit(solution)/shard_map/all_to_all | solution.py:507
  80.6 3.6 %right.1 = (bf16[1024,512]{1,0:T(8,128)(2,1)}, bf16[1024,512]{1,0:T(8,128)(2,1)}) custom-call(s32[8]{0:T(128)S(1)} %copy-done.1, f32[2,1024,256]{2,1,0:T(8,128)S(1)} %get-tuple-element.110.partial, bf16[2,1024,256]{2,1,0:T(8,128)(2,1)S(1)} %get-tuple-element.111.both, bf16[8,3,64,128]{3,2,1,0:T(8,128)(2,1)S(1)} %all-to-all-done.3.states, ...), custom_call_target="tpu_custom_call" | custom-call | tf_op jit(solution)/shard_map/right/pallas_call | solution.py:707
Async XLA Ops:
  0.6 10.5 %copy-start.1 = (s32[8]{0:T(128)S(1)}, s32[8]{0:T(128)}, u32[]{:S(2)}) copy-start(s32[8]{0:T(128)} %ends_in.3) | copy-start | bytes 100
  3.9 19.0 %all-to-all-start = ((bf16[8,3,64,128]{3,2,1,0:T(8,128)(2,1)}), bf16[8,3,64,128]{3,2,1,0:T(8,128)(2,1)S(1)}, u32[]{:S(2)}, u32[]{:S(2)}) async-start(bf16[8,3,64,128]{3,2,1,0:T(8,128)(2,1)} %sums.1), calls=%async_computation | async-start | bytes 786432 | tf_op jit(solution)/shard_map/all_to_all | solution.py:507
  11.2 11.7 %copy-start.3 = (s32[16]{0:T(128)S(1)}, s32[16]{0:T(128)}, u32[]{:S(2)}) copy-start(s32[16]{0:T(128)} %refs_1_.5) | copy-start | bytes 196
  11.2 16.9 %copy-start.2 = (s32[1,2]{1,0:T(1,128)S(1)}, s32[1,2]{1,0:T(1,128)}, u32[]{:S(2)}) copy-start(s32[1,2]{1,0:T(1,128)} %refs_0_.9) | copy-start | bytes 28
  24.5 15.2 %all-to-all-start.1 = ((bf16[8,3,64,128]{3,2,1,0:T(8,128)(2,1)}), bf16[8,3,64,128]{3,2,1,0:T(8,128)(2,1)S(1)}, u32[]{:S(2)}, u32[]{:S(2)}) async-start(bf16[8,3,64,128]{3,2,1,0:T(8,128)(2,1)} %chain.1), calls=%async_computation.1 | async-start | bytes 786432 | tf_op jit(solution)/shard_map/all_to_all | solution.py:507
  32.0 7.7 %copy-start = (bf16[512,512]{1,0:T(8,128)(2,1)S(1)}, bf16[512,512]{1,0:T(8,128)(2,1)}, u32[]{:S(2)}) copy-start(bf16[512,512]{1,0:T(8,128)(2,1)} %refs_2_) | copy-start | bytes 1572868
  32.0 7.7 %copy-start.4 = (f32[512]{0:T(512)S(1)}, f32[512]{0:T(512)}, u32[]{:S(2)}) copy-start(f32[512]{0:T(512)} %param.19) | copy-start | bytes 6148
  41.2 4.4 %collective-permute-start.2 = (f32[8,128]{1,0:T(8,128)S(1)}, f32[8,128]{1,0:T(8,128)S(1)}, u32[]{:S(2)}, u32[]{:S(2)}) collective-permute-start(f32[8,128]{1,0:T(8,128)S(1)} %get-tuple-element.92.refs_1_), channel_id=1, source_target_pairs={{0,3},{1,0},{2,1},{3,2},{4,7},{5,4},{6,5},{7,6},{8,11},{9,8},{10,9... | collective-permute-start | bytes 12296 | tf_op jit(solution)/shard_map/ppermute | solution.py:615
  41.2 4.4 %collective-permute-start.1 = (f32[8,128]{1,0:T(8,128)S(1)}, f32[8,128]{1,0:T(8,128)S(1)}, u32[]{:S(2)}, u32[]{:S(2)}) collective-permute-start(f32[8,128]{1,0:T(8,128)S(1)} %get-tuple-element.92.refs_1_), channel_id=1, source_target_pairs={{0,2},{1,3},{2,0},{3,1},{4,6},{5,7},{6,4},{7,5},{8,10},{9,11},{10,... | collective-permute-start | bytes 12296 | tf_op jit(solution)/shard_map/ppermute | solution.py:615
  42.8 3.0 %collective-permute-start = (f32[8,128]{1,0:T(8,128)S(1)}, f32[8,128]{1,0:T(8,128)S(1)}, u32[]{:S(2)}, u32[]{:S(2)}) collective-permute-start(f32[8,128]{1,0:T(8,128)S(1)} %get-tuple-element.92.refs_1_), channel_id=1, source_target_pairs={{0,1},{1,2},{2,3},{3,0},{4,5},{5,6},{6,7},{7,4},{8,9},{9,10},{10,1... | collective-permute-start | bytes 12296 | tf_op jit(solution)/shard_map/ppermute | solution.py:615
  46.5 16.8 %all-to-all-start.2 = ((bf16[8,208,128]{2,1,0:T(8,128)(2,1)}), bf16[8,208,128]{2,1,0:T(8,128)(2,1)S(1)}, u32[]{:S(2)}, u32[]{:S(2)}) async-start(bf16[8,208,128]{2,1,0:T(8,128)(2,1)} %append.1), calls=%async_computation.2 | async-start | bytes 851968 | tf_op jit(solution)/shard_map/all_to_all | solution.py:507
  51.2 12.1 %copy-start.5 = (s32[16]{0:T(128)S(1)}, s32[16]{0:T(128)}, u32[]{:S(2)}) copy-start(s32[16]{0:T(128)} %param.23) | copy-start | bytes 196
  65.1 15.5 %all-to-all-start.3 = ((bf16[8,3,64,128]{3,2,1,0:T(8,128)(2,1)}), bf16[8,3,64,128]{3,2,1,0:T(8,128)(2,1)S(1)}, u32[]{:S(2)}, u32[]{:S(2)}) async-start(bf16[8,3,64,128]{3,2,1,0:T(8,128)(2,1)} %get-tuple-element.98), calls=%async_computation.3 | async-start | bytes 786432 | tf_op jit(solution)/shard_map/all_to_all | solution.py:507

commit v11 on v9

--- a/solution.py
+++ b/solution.py
@@ -467,19 +467,16 @@
         for c in waits[h]:
             c.wait()
 
-        def finish(pieces):
+        def finish(pieces, to, part, operand, axis):
             mats = [load_matrix(states, m, h, states.shape[0] // heads) for m in range(pieces)]
-            cut = lambda a: [a[:, m * E : (m + 1) * E] for m in range(pieces)]
-            some = bounds[: pieces - 1]
-            by_v = dot(kv[1, :, at], jnp.concatenate(mats, axis=0), 1, 1)
-            dk[:, mine] = (near[0, :, at] + pick_rows(rows, some, cut(by_v))).astype(bf16)
-            by_k = dot(kv[0, :, at], jnp.concatenate(mats, axis=1), 1, 0)
-            dv[:, mine] = (near[1, :, at] + pick_rows(rows, some, cut(by_k))).astype(bf16)
-
-        pl.when(bounds[-1] < width)(lambda: finish(PIECES))
-        pl.when(bounds[-1] >= width)(lambda: finish(PIECES - 1))
+            product = dot(kv[operand, :, at], jnp.concatenate(mats, axis=1 - axis), 1, axis)
+            options = [product[:, m * E : (m + 1) * E] for m in range(pieces)]
+            to[:, mine] = (near[part, :, at] + pick_rows(rows, bounds[: pieces - 1], options)).astype(bf16)
+
         columns = pl.ds(h * E, E)
-        for i, (a, b) in enumerate(((dk, dk_out), (dv, dv_out))):
+        for i, (a, b, operand, axis) in enumerate(((dk, dk_out, 1, 1), (dv, dv_out, 0, 0))):
+            pl.when(bounds[-1] < width)(lambda: finish(PIECES, a, i, operand, axis))
+            pl.when(bounds[-1] >= width)(lambda: finish(PIECES - 1, a, i, operand, axis))
             copies.append(pltpu.make_async_copy(a.at[:, columns], b.at[:, columns], sems.at[(heads + h) * 4 + i]))
             copies[-1].start()
     for c in copies:

time: 84.4 us -> 85.9 us (1.018)
  Pallas kernels: 45.5 us -> 46.9 us
    pallas_call x1, Pallas kernels: 3.39 us -> 4.79 us  [per_device(): call(right_kernel, in_specs=[ANY] + [VMEM] * 3 + [ANY] * 4, out_specs=[AN...]
  transfers between devices with their start and end apart: 7 -> 7, of which waited for: 5 -> 5; matrix products, arithmetic and copies ran while one was open for 0% -> 0% of each run, Pallas kernels for 40% -> 39%
where the time goes in v11:
time: 85.9 us; the launch traced here: 85.2 us
  Pallas kernels  46.9 us (55%)
  starting transfers between devices  20 us (23%)
  waiting for transfers between devices  17.3 us (20%)
  between operations  0.94 us (1%)
    all_to_all x4, starting transfers between devices, exchange(): return lax.all_to_all(a, 'seq', 0, 0, tiled=True)  18.2 us
    all_to_all x4, waiting for transfers between devices, exchange(): return lax.all_to_all(a, 'seq', 0, 0, tiled=True)  16.7 us
    pallas_call x2, Pallas kernels, some_heads(): call(prompt_kernel, grid=(how_many,), in_specs=[SMEM] + [columns] * 4 + [...  14 us
    pallas_call x1, Pallas kernels, per_device(): call(lambda *refs: cand_kernel(*refs, scaling=scaling), grid=(heads,), in...  5.93 us
    pallas_call x1, Pallas kernels, per_device(): call(right_kernel, in_specs=[ANY] + [VMEM] * 3 + [ANY] * 4, out_specs=[AN...  4.79 us
    pallas_call x1, Pallas kernels, per_device(): call(query_kernel, grid=(heads,), in_specs=[SMEM, whole, whole, parts_blo...  4.22 us
    pallas_call x1, Pallas kernels, per_device(): call(inside_kernel, grid=(heads,), in_specs=[SMEM] + [cand_block] * 3, ou...  3.85 us
    pallas_call x1, Pallas kernels, per_device(): call(sums_kernel, in_specs=[ANY] * 3, out_specs=VMEM, out_shape=like((cou...  3.3 us
  transfers between devices with their start and end apart: 7, of which 5 were waited for; matrix products, arithmetic and copies ran while one was open for 0% of the time, Pallas kernels for 39%

profile of v11, /device:TPU:0, one launch (start us, length us, event | category | flops | bytes accessed | tf_op | source)
XLA Modules:
  0.0 85.2 jit_solution(72806714207368726)
XLA Ops:
  0.6 0.0 copy-start.1
  0.6 3.3 %sums.1 = bf16[8,3,64,128]{3,2,1,0:T(8,128)(2,1)} custom-call(s32[8]{0:T(128)} %ends_in.3, bf16[1024,512]{1,0:T(8,128)(2,1)} %k_in.2, bf16[1024,512]{1,0:T(8,128)(2,1)} %v_in.2), custom_call_target="tpu_custom_call" | custom-call | tf_op jit(solution)/shard_map/sums/pallas_call | solution.py:529
  4.0 7.3 %all-to-all-start = ((bf16[8,3,64,128]{3,2,1,0:T(8,128)(2,1)}), bf16[8,3,64,128]{3,2,1,0:T(8,128)(2,1)S(1)}, u32[]{:S(2)}, u32[]{:S(2)}) async-start(bf16[8,3,64,128]{3,2,1,0:T(8,128)(2,1)} %sums.1), calls=%async_computation | async-start | bytes 786432 | tf_op jit(solution)/shard_map/all_to_all | solution.py:487
  11.2 0.0 copy-done.1
  11.2 0.0 copy-start.3
  11.2 0.0 copy-start.2
  11.2 9.3 %prompt.2 = (f32[1024,512]{1,0:T(8,128)}, f32[1024,512]{1,0:T(8,128)}, f32[1024,512]{1,0:T(8,128)}, bf16[8,1,64,128]{3,2,1,0:T(8,128)(2,1)}) custom-call(s32[8]{0:T(128)S(1)} %copy-done.1, bf16[1024,512]{1,0:T(8,128)(2,1)} %q.2, bf16[1024,512]{1,0:T(8,128)(2,1)} %k_in.2, bf16[1024,512]{1,0:T(8,128)(2,1)} %v_in.2, bf16[1024,512]{1,0:T(8,128)(2,1)} %g.2), custom_call_target="tpu_custom_call" | custom-call | tf_op jit(solution)/shard_map/prompt/pallas_call | solution.py:547
  20.5 2.4 %all-to-all-done.refs_2_ = bf16[8,3,64,128]{3,2,1,0:T(8,128)(2,1)S(1)} async-done(((bf16[8,3,64,128]{3,2,1,0:T(8,128)(2,1)}), bf16[8,3,64,128]{3,2,1,0:T(8,128)(2,1)S(1)}, u32[]{:S(2)}, u32[]{:S(2)}) %all-to-all-start) | async-done | bytes 393248 | tf_op jit(solution)/shard_map/all_to_all | solution.py:487
  22.9 0.0 copy-done.3
  22.9 1.6 %chain.1 = bf16[8,3,64,128]{3,2,1,0:T(8,128)(2,1)} custom-call(s32[8]{0:T(128)S(1)} %copy-done.1, s32[16]{0:T(128)S(1)} %copy-done.3, bf16[8,3,64,128]{3,2,1,0:T(8,128)(2,1)S(1)} %all-to-all-done.refs_2_), custom_call_target="tpu_custom_call" | custom-call | tf_op jit(solution)/shard_map/chain/pallas_call | solution.py:562
  24.5 3.6 %all-to-all-start.1 = ((bf16[8,3,64,128]{3,2,1,0:T(8,128)(2,1)}), bf16[8,3,64,128]{3,2,1,0:T(8,128)(2,1)S(1)}, u32[]{:S(2)}, u32[]{:S(2)}) async-start(bf16[8,3,64,128]{3,2,1,0:T(8,128)(2,1)} %chain.1), calls=%async_computation.1 | async-start | bytes 786432 | tf_op jit(solution)/shard_map/all_to_all | solution.py:487
  28.2 0.0 copy-done.2
  28.2 3.9 %inside.1.refs_2_ = f32[512,512]{1,0:T(8,128)S(1)} custom-call(s32[1,2]{1,0:T(1,128)S(1)} %copy-done.2, bf16[512,512]{1,0:T(8,128)(2,1)} %refs_2_, bf16[512,512]{1,0:T(8,128)(2,1)} %refs_3_, bf16[512,512]{1,0:T(8,128)(2,1)} %refs_4_), custom_call_target="tpu_custom_call" | custom-call | tf_op jit(solution)/shard_map/inside/pallas_call | solution.py:573
  32.0 0.0 copy-start
  32.0 0.0 copy-start.4
  32.0 4.7 %prompt.3 = (f32[1024,512]{1,0:T(8,128)}, f32[1024,512]{1,0:T(8,128)}, f32[1024,512]{1,0:T(8,128)}, bf16[8,1,64,128]{3,2,1,0:T(8,128)(2,1)}) custom-call(s32[8]{0:T(128)S(1)} %copy-done.1, bf16[1024,512]{1,0:T(8,128)(2,1)} %q.2, bf16[1024,512]{1,0:T(8,128)(2,1)} %k_in.2, ...), custom_call_target="tpu_custom_call", output_to_operand_aliasing={{0}: (5, {}), {1}: (6, {}), {2}: (7, {}), {3}: (8, {})} | custom-call | tf_op jit(solution)/shard_map/prompt/pallas_call | solution.py:547
  36.8 2.9 %all-to-all-done.1.refs_4_.states.refs_6_ = bf16[8,3,64,128]{3,2,1,0:T(8,128)(2,1)S(1)} async-done(((bf16[8,3,64,128]{3,2,1,0:T(8,128)(2,1)}), bf16[8,3,64,128]{3,2,1,0:T(8,128)(2,1)S(1)}, u32[]{:S(2)}, u32[]{:S(2)}) %all-to-all-start.1) | async-done | bytes 393248 | tf_op jit(solution)/shard_map/all_to_all | solution.py:487
  39.7 0.0 copy-done
  39.7 0.0 copy-done.4
  39.7 1.5 %scores.1 = (f32[512,512]{1,0:T(8,128)S(1)}, f32[8,128]{1,0:T(8,128)S(1)}) custom-call(s32[1,2]{1,0:T(1,128)S(1)} %copy-done.2, bf16[512,512]{1,0:T(8,128)(2,1)S(1)} %copy-done, f32[512,512]{1,0:T(8,128)S(1)} %inside.1.refs_2_, f32[1,512]{1,0:T(1,128)S(1)} %bitcast.6, bf16[8,3,64,128]{3,2,1,0:T(8,128)(2,1)S(1)} %all-to-all-done.1.refs_4_.states.refs_6_), custom_call_target="tpu_custom_call" | custom-call | tf_op jit(solution)/shard_map/scores/pallas_call | solution.py:586
  41.2 0.0 collective-permute-start.2
  41.2 1.6 %collective-permute-start.1 = (f32[8,128]{1,0:T(8,128)S(1)}, f32[8,128]{1,0:T(8,128)S(1)}, u32[]{:S(2)}, u32[]{:S(2)}) collective-permute-start(f32[8,128]{1,0:T(8,128)S(1)} %get-tuple-element.92.refs_1_), channel_id=1, source_target_pairs={{0,2},{1,3},{2,0},{3,1},{4,6},{5,7},{6,4},{7,5},{8,10},{9,11},{10,... | collective-permute-start | bytes 12296 | tf_op jit(solution)/shard_map/ppermute | solution.py:595
  42.9 0.2 collective-permute-start
  43.0 2.2 %grads.1.refs_0_ = bf16[8,208,128]{2,1,0:T(8,128)(2,1)} custom-call(s32[1,2]{1,0:T(1,128)S(1)} %copy-done.2, bf16[512,512]{1,0:T(8,128)(2,1)S(1)} %copy-done, f32[512,512]{1,0:T(8,128)S(1)} %get-tuple-element.95.refs_2_.near, bf16[8,1,64,128]{3,2,1,0:T(8,128)(2,1)} %get-tuple-element.91.refs_3_), custom_call_target="tpu_custom_call" | custom-call | tf_op jit(solution)/shard_map/grads/pallas_call | solution.py:597
  45.2 0.0 collective-permute-done.2.refs_4_
  45.3 0.0 collective-permute-done.1.refs_3_
  45.3 0.6 collective-permute-done.refs_2_
  45.9 0.7 append.1
  46.6 3.6 %all-to-all-start.2 = ((bf16[8,208,128]{2,1,0:T(8,128)(2,1)}), bf16[8,208,128]{2,1,0:T(8,128)(2,1)S(1)}, u32[]{:S(2)}, u32[]{:S(2)}) async-start(bf16[8,208,128]{2,1,0:T(8,128)(2,1)} %append.1), calls=%async_computation.2 | async-start | bytes 851968 | tf_op jit(solution)/shard_map/all_to_all | solution.py:487
  50.2 1.0 %save.1.refs_5_ = f32[512,512]{1,0:T(8,128)} custom-call(f32[512,512]{1,0:T(8,128)S(1)} %get-tuple-element.95.refs_2_.near), custom_call_target="tpu_custom_call" | custom-call | tf_op jit(solution)/shard_map/save/pallas_call | solution.py:617
  51.2 0.0 copy-start.5
  51.3 4.2 %query.1 = bf16[1024,512]{1,0:T(8,128)(2,1)} custom-call(s32[8]{0:T(128)S(1)} %copy-done.1, f32[1024,512]{1,0:T(8,128)} %get-tuple-element.93.part, bf16[1024,512]{1,0:T(8,128)(2,1)} %g.2, bf16[8,3,64,128]{3,2,1,0:T(8,128)(2,1)S(1)} %all-to-all-done.1.refs_4_.states.refs_6_), custom_call_target="tpu_custom_call" | custom-call | tf_op jit(solution)/shard_map/query/pallas_call | solution.py:625
  55.5 7.5 %all-to-all-done.2.refs_4_ = bf16[8,208,128]{2,1,0:T(8,128)(2,1)S(1)} async-done(((bf16[8,208,128]{2,1,0:T(8,128)(2,1)}), bf16[8,208,128]{2,1,0:T(8,128)(2,1)S(1)}, u32[]{:S(2)}, u32[]{:S(2)}) %all-to-all-start.2) | async-done | bytes 426016 | tf_op jit(solution)/shard_map/all_to_all | solution.py:487
  63.0 0.0 copy-done.5
  63.0 1.7 %listwise.1 = (bf16[8,3,64,128]{3,2,1,0:T(8,128)(2,1)}, f32[8,128]{1,0:T(8,128)S(1)}, f32[1,128]{1,0:T(1,128)}) custom-call(s32[8]{0:T(128)S(1)} %copy-done.1, s32[16]{0:T(128)S(1)} %copy-done.3, s32[1,16]{1,0:T(1,128)S(1)} %bitcast.5, s32[1,16]{1,0:T(1,128)S(1)} %bitcast.7, bf16[8,208,128]{2,1,0:T(8,128)(2,1)S(1)} %all-to-all-done.2.refs_4_), custom_call_target="tpu_custom_call" | custom-call | tf_op jit(solution)/shard_map/listwise/pallas_call | solution.py:636
  64.7 3.6 %all-to-all-start.3 = ((bf16[8,3,64,128]{3,2,1,0:T(8,128)(2,1)}), bf16[8,3,64,128]{3,2,1,0:T(8,128)(2,1)S(1)}, u32[]{:S(2)}, u32[]{:S(2)}) async-start(bf16[8,3,64,128]{3,2,1,0:T(8,128)(2,1)} %get-tuple-element.98), calls=%async_computation.3 | async-start | bytes 786432 | tf_op jit(solution)/shard_map/all_to_all | solution.py:487
  68.4 5.9 %cand.1 = (bf16[512,512]{1,0:T(8,128)(2,1)}, bf16[512,512]{1,0:T(8,128)(2,1)}, bf16[512,512]{1,0:T(8,128)(2,1)}) custom-call(s32[1,2]{1,0:T(1,128)S(1)} %copy-done.2, f32[8,128]{1,0:T(8,128)S(1)} %get-tuple-element.99.refs_1_, bf16[512,512]{1,0:T(8,128)(2,1)} %refs_2_, bf16[512,512]{1,0:T(8,128)(2,1)} %refs_3_, bf16[512,512]{1,0:T(8,128)(2,1)} %refs_4_, ...), custom_call_target="tpu_custom_call" | custom-call | tf_op jit(solution)/shard_map/cand/pallas_call | solution.py:661
  74.3 2.0 %stage.1 = (f32[2,1024,256]{2,1,0:T(8,128)S(1)}, bf16[2,1024,256]{2,1,0:T(8,128)(2,1)S(1)}) custom-call(f32[1024,512]{1,0:T(8,128)} %get-tuple-element.104.dk_part.dk_in, f32[1024,512]{1,0:T(8,128)} %get-tuple-element.105.dv_part.dv_in, bf16[1024,512]{1,0:T(8,128)(2,1)} %k_in.2, bf16[1024,512]{1,0:T(8,128)(2,1)} %v_in.2), custom_call_target="tpu_custom_call" | custom-call | tf_op jit(solution)/shard_map/stage/pallas_call | solution.py:673
  76.3 3.9 %all-to-all-done.3.states = bf16[8,3,64,128]{3,2,1,0:T(8,128)(2,1)S(1)} async-done(((bf16[8,3,64,128]{3,2,1,0:T(8,128)(2,1)}), bf16[8,3,64,128]{3,2,1,0:T(8,128)(2,1)S(1)}, u32[]{:S(2)}, u32[]{:S(2)}) %all-to-all-start.3) | async-done | bytes 393248 | tf_op jit(solution)/shard_map/all_to_all | solution.py:487
  80.2 4.8 %right.1 = (bf16[1024,512]{1,0:T(8,128)(2,1)}, bf16[1024,512]{1,0:T(8,128)(2,1)}) custom-call(s32[8]{0:T(128)S(1)} %copy-done.1, f32[2,1024,256]{2,1,0:T(8,128)S(1)} %get-tuple-element.110.partial, bf16[2,1024,256]{2,1,0:T(8,128)(2,1)S(1)} %get-tuple-element.111.both, bf16[8,3,64,128]{3,2,1,0:T(8,128)(2,1)S(1)} %all-to-all-done.3.states, ...), custom_call_target="tpu_custom_call" | custom-call | tf_op jit(solution)/shard_map/right/pallas_call | solution.py:683
Async XLA Ops:
  0.6 10.6 %copy-start.1 = (s32[8]{0:T(128)S(1)}, s32[8]{0:T(128)}, u32[]{:S(2)}) copy-start(s32[8]{0:T(128)} %ends_in.3) | copy-start | bytes 100
  4.0 18.9 %all-to-all-start = ((bf16[8,3,64,128]{3,2,1,0:T(8,128)(2,1)}), bf16[8,3,64,128]{3,2,1,0:T(8,128)(2,1)S(1)}, u32[]{:S(2)}, u32[]{:S(2)}) async-start(bf16[8,3,64,128]{3,2,1,0:T(8,128)(2,1)} %sums.1), calls=%async_computation | async-start | bytes 786432 | tf_op jit(solution)/shard_map/all_to_all | solution.py:487
  11.2 11.7 %copy-start.3 = (s32[16]{0:T(128)S(1)}, s32[16]{0:T(128)}, u32[]{:S(2)}) copy-start(s32[16]{0:T(128)} %refs_1_.5) | copy-start | bytes 196
  11.2 16.9 %copy-start.2 = (s32[1,2]{1,0:T(1,128)S(1)}, s32[1,2]{1,0:T(1,128)}, u32[]{:S(2)}) copy-start(s32[1,2]{1,0:T(1,128)} %refs_0_.9) | copy-start | bytes 28
  24.5 15.2 %all-to-all-start.1 = ((bf16[8,3,64,128]{3,2,1,0:T(8,128)(2,1)}), bf16[8,3,64,128]{3,2,1,0:T(8,128)(2,1)S(1)}, u32[]{:S(2)}, u32[]{:S(2)}) async-start(bf16[8,3,64,128]{3,2,1,0:T(8,128)(2,1)} %chain.1), calls=%async_computation.1 | async-start | bytes 786432 | tf_op jit(solution)/shard_map/all_to_all | solution.py:487
  32.0 7.7 %copy-start = (bf16[512,512]{1,0:T(8,128)(2,1)S(1)}, bf16[512,512]{1,0:T(8,128)(2,1)}, u32[]{:S(2)}) copy-start(bf16[512,512]{1,0:T(8,128)(2,1)} %refs_2_) | copy-start | bytes 1572868
  32.0 7.7 %copy-start.4 = (f32[512]{0:T(512)S(1)}, f32[512]{0:T(512)}, u32[]{:S(2)}) copy-start(f32[512]{0:T(512)} %param.19) | copy-start | bytes 6148
  41.2 4.0 %collective-permute-start.2 = (f32[8,128]{1,0:T(8,128)S(1)}, f32[8,128]{1,0:T(8,128)S(1)}, u32[]{:S(2)}, u32[]{:S(2)}) collective-permute-start(f32[8,128]{1,0:T(8,128)S(1)} %get-tuple-element.92.refs_1_), channel_id=1, source_target_pairs={{0,3},{1,0},{2,1},{3,2},{4,7},{5,4},{6,5},{7,6},{8,11},{9,8},{10,9... | collective-permute-start | bytes 12296 | tf_op jit(solution)/shard_map/ppermute | solution.py:595
  41.2 4.0 %collective-permute-start.1 = (f32[8,128]{1,0:T(8,128)S(1)}, f32[8,128]{1,0:T(8,128)S(1)}, u32[]{:S(2)}, u32[]{:S(2)}) collective-permute-start(f32[8,128]{1,0:T(8,128)S(1)} %get-tuple-element.92.refs_1_), channel_id=1, source_target_pairs={{0,2},{1,3},{2,0},{3,1},{4,6},{5,7},{6,4},{7,5},{8,10},{9,11},{10,... | collective-permute-start | bytes 12296 | tf_op jit(solution)/shard_map/ppermute | solution.py:595
  42.9 3.0 %collective-permute-start = (f32[8,128]{1,0:T(8,128)S(1)}, f32[8,128]{1,0:T(8,128)S(1)}, u32[]{:S(2)}, u32[]{:S(2)}) collective-permute-start(f32[8,128]{1,0:T(8,128)S(1)} %get-tuple-element.92.refs_1_), channel_id=1, source_target_pairs={{0,1},{1,2},{2,3},{3,0},{4,5},{5,6},{6,7},{7,4},{8,9},{9,10},{10,1... | collective-permute-start | bytes 12296 | tf_op jit(solution)/shard_map/ppermute | solution.py:595
  46.6 16.4 %all-to-all-start.2 = ((bf16[8,208,128]{2,1,0:T(8,128)(2,1)}), bf16[8,208,128]{2,1,0:T(8,128)(2,1)S(1)}, u32[]{:S(2)}, u32[]{:S(2)}) async-start(bf16[8,208,128]{2,1,0:T(8,128)(2,1)} %append.1), calls=%async_computation.2 | async-start | bytes 851968 | tf_op jit(solution)/shard_map/all_to_all | solution.py:487
  51.2 11.7 %copy-start.5 = (s32[16]{0:T(128)S(1)}, s32[16]{0:T(128)}, u32[]{:S(2)}) copy-start(s32[16]{0:T(128)} %param.23) | copy-start | bytes 196
  64.7 15.5 %all-to-all-start.3 = ((bf16[8,3,64,128]{3,2,1,0:T(8,128)(2,1)}), bf16[8,3,64,128]{3,2,1,0:T(8,128)(2,1)S(1)}, u32[]{:S(2)}, u32[]{:S(2)}) async-start(bf16[8,3,64,128]{3,2,1,0:T(8,128)(2,1)} %get-tuple-element.98), calls=%async_computation.3 | async-start | bytes 786432 | tf_op jit(solution)/shard_map/all_to_all | solution.py:487
